TPU v7x, 128 devices: a whole 4x4x4 slice. The times are simulated.
128 devices in a mesh: row: 4 (over y_hi, core), col: 4 (over z), dp: 8 (over y_lo, x).
Axes of the slice: x: 4, y: 4 (y_hi: 2, y_lo: 2; y = y_hi * 2 + y_lo), z: 4, core: 2. Of those that a mesh axis runs over, the one named last changes fastest.
Arguments:
- observed: bfloat16 [4096, 2048], P(('row', 'dp'), 'col'), may hold values from -6 to 6
- next_observed: bfloat16 [4096, 2048], P(('row', 'dp'), 'col'), may hold values from -6 to 6
- actions: bfloat16 [4096, 128], P(('row', 'dp')), may hold values from -1 to 1
- next_mean: bfloat16 [4096, 128], P(('row', 'dp')), may hold values from -1.1953125 to 1.1953125
- policy_noise: float32 [4096, 128], P(('row', 'dp')), may hold values from -1.5 to 1.5
- rewards: bfloat16 [4096], P(('row', 'dp')), may hold values from -5 to 5
- discounts: bfloat16 [4096], P(('row', 'dp')), may hold values from 0.5 to 0.98828125
- actor_flags: int32 [4096], P(('row', 'dp')), may hold values 0 or 1
- critic_in: float32 [2, 2048, 2048], P(None, 'col', 'row'), may hold values from -0.125 to 0.125
- critic_act: float32 [2, 128, 2048], P(None, None, 'col'), may hold values from -0.5 to 0.5
- critic_head: float32 [2, 2048], P(None, 'row'), may hold values from -0.125 to 0.125
- target_in: float32 [2, 2048, 2048], P(None, 'col', 'row'), may hold values from -0.125 to 0.125
- target_act: float32 [2, 128, 2048], P(None, None, 'col'), may hold values from -0.5 to 0.5
- target_head: float32 [2, 2048], P(None, 'row'), may hold values from -0.125 to 0.125
Outputs:
- new_in: float32 [2, 2048, 2048], P(None, 'col', 'row')
- new_act: float32 [2, 128, 2048], P(None, None, 'col')
- new_head: float32 [2, 2048], P(None, 'row')
- new_target_in: float32 [2, 2048, 2048], P(None, 'col', 'row')
- new_target_act: float32 [2, 128, 2048], P(None, None, 'col')
- new_target_head: float32 [2, 2048], P(None, 'row')
- temporal_errors: float32 [2, 4096], P(None, ('row', 'dp'))
- action_slope: float32 [4096, 128], P(('row', 'dp'))
All inputs are finite; a program needn't handle non-finite values. No bound on the sum of `actor_flags` on one device may be relied on, other than what follows from the above.
Results may differ from a plain program's by a relative error of at most 0.008.
Values may be sent and summed in bfloat16 or wider, within the bound.
No kernel may reach another device: no remote copies, remote signals or barrier semaphores. Data moves between devices by JAX's collectives and lax.ppermute only.
A program may use at most 128 MiB of HBM per device.

v0:
```python
import math

import jax
import jax.numpy as jnp
from jax import lax
from jax.sharding import PartitionSpec as P

noise_clip = 0.5
matrix_rate = 0.004
head_rate = 0.0001
blend_rate = 0.005


def in_one_piece(arrays, axis, dim, along):
    widths = [math.prod(a.shape[along:]) for a in arrays]
    both = jnp.concatenate(
        [a.reshape(*a.shape[:along], w) for a, w in zip(arrays, widths)], axis=along
    )
    whole = lax.all_gather(both, axis, axis=dim, tiled=True)
    blocks = jnp.split(whole, [sum(widths[:k]) for k in range(1, len(widths))], axis=along)
    return tuple(
        (b.reshape(*whole.shape[:along], *a.shape[along:]) for a, b in zip(arrays, blocks))
    )


def in_one_piece_2(arrays, axis, dim, along):
    ends, at = ([], 0)
    for a in arrays[:-1]:
        at += a.shape[along]
        ends.append(at)
    both = jnp.concatenate(arrays, axis=along)
    return tuple(
        jnp.split(lax.psum_scatter(both, axis, scatter_dimension=dim, tiled=True), ends, axis=along)
    )


def sent_to_all(x, axis):
    copies = jnp.broadcast_to(x, (lax.axis_size(axis), *x.shape))
    return lax.all_to_all(copies, axis, split_axis=0, concat_axis=0, tiled=True)


def taken_together(x, axis):
    return sent_to_all(x, axis).sum(axis=0)


def packed_total(arrays, axis):
    ends = [0]
    for a in arrays:
        ends.append(ends[-1] + a.size)
    running = taken_together(jnp.concatenate([a.ravel() for a in arrays]), axis)
    return tuple((running[b:e].reshape(a.shape) for a, b, e in zip(arrays, ends, ends[1:])))


def in_one_piece_3(arrays, axis, dim, along):
    both = jnp.concatenate(arrays, axis=along)
    whole, at, gathered = (lax.all_gather(both, axis, axis=dim, tiled=True), 0, [])
    for a in arrays:
        gathered.append(lax.slice_in_dim(whole, at, at + a.shape[along], axis=along))
        at += a.shape[along]
    return tuple(gathered)


def rows_first(arrays, axis, dims):
    turned = [jnp.moveaxis(a, dim, 0) for a, dim in zip(arrays, dims)]
    widths = [t[0].size for t in turned]
    both = jnp.concatenate([t.reshape(-1, w) for t, w in zip(turned, widths)], axis=1)
    whole = lax.all_gather(both, axis, axis=0, tiled=True)
    blocks = jnp.split(whole, [sum(widths[:k]) for k in range(1, len(widths))], axis=1)
    return tuple(
        (
            jnp.moveaxis(b.reshape(-1, *t.shape[1:]), 0, dim)
            for b, t, dim in zip(blocks, turned, dims)
        )
    )


def silu_slope(preact):
    sigma = jax.nn.sigmoid(preact)
    return sigma * (1.0 + preact * (1.0 - sigma))


def embed(states, moves, weight_act):
    summed = states.astype(jnp.float32) + jnp.dot(
        moves, weight_act.astype(jnp.bfloat16), preferred_element_type=jnp.float32
    )
    return summed.astype(jnp.bfloat16)


def contract_rows(left, right):
    return lax.dot_general(
        left, right, (((0,), (0,)), ((), ())), preferred_element_type=jnp.float32
    )


def on_device(
    observed,
    next_observed,
    actions,
    next_mean,
    policy_noise,
    rewards,
    discounts,
    actor_flags,
    critic_in,
    critic_act,
    critic_head,
    target_in,
    target_act,
    target_head,
):
    noisy = jnp.clip(
        next_mean.astype(jnp.float32) + jnp.clip(policy_noise, -noise_clip, noise_clip), -1.0, 1.0
    ).astype(jnp.bfloat16)
    states, next_states, moves, next_moves, group_rewards, group_discounts = in_one_piece(
        (observed, next_observed, actions, noisy, rewards, discounts), "row", 0, 1
    )
    inner = [critic_in[which].astype(jnp.bfloat16) for which in range(2)]
    online = [embed(states, moves, critic_act[which]) for which in range(2)]
    shadow = [embed(next_states, next_moves, target_act[which]) for which in range(2)]
    partials = [
        jnp.dot(online[which], inner[which], preferred_element_type=jnp.float32)
        for which in range(2)
    ]
    partials += [
        jnp.dot(
            shadow[which], target_in[which].astype(jnp.bfloat16), preferred_element_type=jnp.float32
        )
        for which in range(2)
    ]
    total_rows = states.shape[0]
    preacts = tuple(
        (
            part.astype(jnp.float32)
            for part in in_one_piece_2(
                (
                    partials[0].astype(jnp.bfloat16),
                    partials[1].astype(jnp.bfloat16),
                    partials[2].astype(jnp.bfloat16),
                    partials[3].astype(jnp.bfloat16),
                ),
                "col",
                0,
                1,
            )
        )
    )
    row_count = total_rows // lax.axis_size("col")
    first_row = lax.axis_index("col") * row_count
    share_rewards = lax.dynamic_slice_in_dim(group_rewards, first_row, row_count).astype(
        jnp.float32
    )
    share_discounts = lax.dynamic_slice_in_dim(group_discounts, first_row, row_count).astype(
        jnp.float32
    )
    heads = [critic_head[0], critic_head[1], target_head[0], target_head[1]]
    hiddens = [jax.nn.silu(preacts[which]) for which in range(4)]
    value_terms = [
        jnp.dot(hiddens[which], heads[which], precision=lax.Precision.HIGHEST) for which in range(4)
    ]
    values = packed_total((value_terms[0], value_terms[1], value_terms[2], value_terms[3]), "row")
    goal = share_rewards + share_discounts * jnp.minimum(values[2], values[3])
    errors = [values[0] - goal, values[1] - goal]
    slopes = [
        (heads[which] * silu_slope(preacts[which])).astype(jnp.bfloat16) for which in range(2)
    ]
    head_grads = [
        jnp.dot(2.0 * errors[which], hiddens[which], precision=lax.Precision.HIGHEST)
        for which in range(2)
    ]
    slopes = list(in_one_piece_3((slopes[0], slopes[1]), "col", 0, 1))
    errors = list(rows_first((errors[0], errors[1]), "col", (0, 0)))
    head_grads = list(packed_total((head_grads[0], head_grads[1]), "col"))
    deltas = [
        (2.0 * errors[which][:, None] * slopes[which].astype(jnp.float32)).astype(jnp.bfloat16)
        for which in range(2)
    ]
    back_terms = [
        lax.dot_general(
            slopes[which],
            inner[which],
            (((1,), (1,)), ((), ())),
            preferred_element_type=jnp.float32,
        )
        for which in range(2)
    ]
    grad_ins = [contract_rows(online[which], deltas[which]) for which in range(2)]
    own_rows = observed.shape[0]
    own_first = lax.axis_index("row") * own_rows
    own_errors = [
        lax.dynamic_slice_in_dim(errors[which], own_first, own_rows) for which in range(2)
    ]
    backs = lax.psum((back_terms[0], back_terms[1]), "row")
    grad_embedded = [
        (2.0 * errors[which][:, None] * backs[which]).astype(jnp.bfloat16) for which in range(2)
    ]
    grad_acts = [contract_rows(moves, grad_embedded[which]) for which in range(2)]
    mine = lax.dynamic_slice_in_dim(backs[0], own_first, own_rows).astype(jnp.bfloat16)
    push_term = lax.dot_general(
        mine,
        critic_act[0].astype(jnp.bfloat16),
        (((1,), (1,)), ((), ())),
        preferred_element_type=jnp.float32,
    )
    action_slope = taken_together(push_term, "col") * actor_flags.astype(jnp.float32)[:, None]
    temporal_errors = jnp.stack(own_errors)
    olds = [
        critic_in[0],
        critic_in[1],
        critic_act[0],
        critic_act[1],
        critic_head[0],
        critic_head[1],
    ]
    rates = [matrix_rate, matrix_rate, matrix_rate, matrix_rate, head_rate, head_rate]
    summed = (
        lax.psum(grad_ins[0].astype(jnp.bfloat16), "dp").astype(jnp.float32),
        lax.psum(grad_ins[1].astype(jnp.bfloat16), "dp").astype(jnp.float32),
        lax.psum(grad_acts[0].astype(jnp.bfloat16), "dp").astype(jnp.float32),
        lax.psum(grad_acts[1].astype(jnp.bfloat16), "dp").astype(jnp.float32),
        lax.psum(head_grads[0].astype(jnp.bfloat16), "dp").astype(jnp.float32),
        lax.psum(head_grads[1].astype(jnp.bfloat16), "dp").astype(jnp.float32),
    )
    fresh = [olds[which] - rates[which] * summed[which] for which in range(6)]
    new_in = jnp.stack([fresh[0], fresh[1]])
    new_act = jnp.stack([fresh[2], fresh[3]])
    new_head = jnp.stack([fresh[4], fresh[5]])
    new_target_in = blend_rate * new_in + (1.0 - blend_rate) * target_in
    new_target_act = blend_rate * new_act + (1.0 - blend_rate) * target_act
    new_target_head = blend_rate * new_head + (1.0 - blend_rate) * target_head
    return (
        new_in,
        new_act,
        new_head,
        new_target_in,
        new_target_act,
        new_target_head,
        temporal_errors,
        action_slope,
    )


def solution(mesh):
    return jax.shard_map(
        on_device,
        mesh=mesh,
        in_specs=(
            P(("row", "dp"), "col"),
            P(("row", "dp"), "col"),
            P(("row", "dp"), None),
            P(("row", "dp"), None),
            P(("row", "dp"), None),
            P(("row", "dp")),
            P(("row", "dp")),
            P(("row", "dp")),
            P(None, "col", "row"),
            P(None, None, "col"),
            P(None, "row"),
            P(None, "col", "row"),
            P(None, None, "col"),
            P(None, "row"),
        ),
        out_specs=(
            P(None, "col", "row"),
            P(None, None, "col"),
            P(None, "row"),
            P(None, "col", "row"),
            P(None, None, "col"),
            P(None, "row"),
            P(None, ("row", "dp")),
            P(("row", "dp"), None),
        ),
        check_vma=False,
    )
```

profile of v0, /device:TPU:0, one launch (start us, length us, event | category | flops | bytes accessed | tf_op | source)
XLA Modules:
  0.0 270.5 jit_solution(15028285660459501925)
XLA Ops:
  7.2 0.0 all-gather.3.cloned.1.call-start
  7.2 0.8 copy.40
  8.0 0.8 copy.41
  8.8 0.9 clamp_convert_fusion
  9.6 1.8 concatenate.18
  11.4 0.0 all-gather.3.cloned.1.call-update
  11.5 0.0 reduce-scatter.4.cloned.1.call-start
  11.5 1.1 convert.14
  12.7 2.8 %convert.15 = bf16[2,512,512]{2,1,0:T(8,128)(2,1)} convert(f32[2,512,512]{2,1,0:T(8,128)} %param.25) | non-fusion elementwise | flops 524288 | bytes 3145728 | tf_op jit(solution)/shard_map/convert.6
  15.5 21.6 %all-gather.3.cloned.1.call-done = bf16[512,1282]{1,0:T(8,128)(2,1)} async-done(((bf16[128,1282]{1,0:T(8,128)(2,1)}), bf16[512,1282]{1,0:T(8,128)(2,1)}) %all-gather.3.cloned.1.call-update) | async-done | bytes 1312784 | tf_op jit(solution)/shard_map/all_gather | solution.py:19
  37.1 1.4 fusion
  38.5 1.3 convolution_convert_fusion.5
  39.8 1.4 fusion.1
  41.2 0.8 copy-done.3
  42.0 1.3 convolution_convert_fusion.4
  43.3 2.7 %convolution_convert_fusion.2 = bf16[512,512]{0,1:T(8,128)(2,1)} fusion(bf16[2,512,512]{2,1,0:T(8,128)(2,1)} %convert.15, bf16[512,1282]{1,0:T(8,128)(2,1)} %all-gather.3.cloned.1.call-done, bf16[2,128,512]{2,1,0:T(8,128)(2,1)S(1)} %convert.14), kind=kOutput, calls=%fused_computation.13 | convolution fusion | flops 336592896 | bytes 1835008 | tf_op jit(solution)/shard_map/dot_general | solution.py:125
  46.0 2.7 %convolution_convert_fusion.3 = bf16[512,512]{0,1:T(8,128)(2,1)} fusion(bf16[2,512,512]{2,1,0:T(8,128)(2,1)} %convert.15, bf16[512,1282]{1,0:T(8,128)(2,1)} %all-gather.3.cloned.1.call-done, bf16[2,128,512]{2,1,0:T(8,128)(2,1)S(1)} %convert.14), kind=kOutput, calls=%fused_computation.14 | convolution fusion | flops 336592896 | bytes 1835008 | tf_op jit(solution)/shard_map/dot_general | solution.py:125
  48.7 3.0 %pad_maximum_fusion = bf16[512,2048]{0,1:T(8,128)(2,1)} fusion(bf16[512,512]{0,1:T(8,128)(2,1)} %convolution_convert_fusion.2, bf16[512,512]{0,1:T(8,128)(2,1)} %convolution_convert_fusion.3, bf16[512,512]{0,1:T(8,128)(2,1)} %convolution_convert_fusion.4, bf16[512,512]{0,1:T(8,128)(2,1)} %convolution_convert_fusion.5), kind=kLoop, calls=%fused_computation | loop fusion | flops 8388608 | bytes 4194304 | tf_op jit(solution)/shard_map/concatenate | solution.py:31
  51.7 3.9 %copy.48 = bf16[512,2048]{1,0:T(8,128)(2,1)} copy(bf16[512,2048]{0,1:T(8,128)(2,1)} %pad_maximum_fusion) | data formatting | bytes 4194304
  55.6 0.0 reduce-scatter.4.cloned.1.call-update
  55.6 0.0 all-gather.5.cloned.1.call-start
  55.7 0.6 copy-done.10
  56.3 28.8 %reduce-scatter.4.cloned.1.call-done = bf16[128,2048]{1,0:T(8,128)(2,1)} async-done(((bf16[512,2048]{1,0:T(8,128)(2,1)}), bf16[128,2048]{1,0:T(8,128)(2,1)}) %reduce-scatter.4.cloned.1.call-update) | async-done | bytes 524304 | tf_op jit(solution)/shard_map/reduce_scatter | solution.py:33
  85.1 1.2 fusion.30
  86.3 0.7 pad_maximum_fusion.3
  87.0 0.0 all-gather.5.cloned.1.call-update
  87.1 1.3 convolution_bitcast_fusion.3
  88.4 1.3 convolution_bitcast_fusion.1
  89.7 0.4 convolution_bitcast_fusion.2
  90.1 0.4 convolution_bitcast_fusion
  90.5 0.6 broadcast_in_dim.10
  91.1 4.3 %all-to-all-start = ((f32[4,1,512]{2,1,0:T(1,128)}), f32[4,1,512]{2,1,0:T(1,128)S(1)}, u32[]{:S(2)}, u32[]{:S(2)}) async-start(f32[4,1,512]{2,1,0:T(1,128)} %broadcast_in_dim.10), calls=%async_computation | async-start | bytes 16384 | tf_op jit(solution)/shard_map/all_to_all | solution.py:39
  95.4 1.1 fusion.82
  96.5 0.1 convert_reduce_fusion
  96.6 4.1 %all-to-all-done = f32[4,1,512]{2,1,0:T(1,128)S(1)} async-done(((f32[4,1,512]{2,1,0:T(1,128)}), f32[4,1,512]{2,1,0:T(1,128)S(1)}, u32[]{:S(2)}, u32[]{:S(2)}) %all-to-all-start) | async-done | bytes 8224 | tf_op jit(solution)/shard_map/all_to_all | solution.py:39
  100.7 10.5 %all-gather.5.cloned.1.call-done = bf16[512,1024]{1,0:T(8,128)(2,1)} async-done(((bf16[128,1024]{1,0:T(8,128)(2,1)}), bf16[512,1024]{1,0:T(8,128)(2,1)}) %all-gather.5.cloned.1.call-update) | async-done | bytes 1048592 | tf_op jit(solution)/shard_map/all_gather | solution.py:56
  111.2 2.6 fusion.13
  113.8 1.4 fusion.10
  115.3 0.0 all-reduce.6.cloned.1.call-update
  115.3 1.2 fusion.49
  116.5 1.2 fusion.50
  117.7 0.6 broadcast_in_dim.11
  118.3 3.5 %all-to-all-start.1 = ((f32[4,1,1024]{2,1,0:T(1,128)}), f32[4,1,1024]{2,1,0:T(1,128)S(1)}, u32[]{:S(2)}, u32[]{:S(2)}) async-start(f32[4,1,1024]{2,1,0:T(1,128)} %broadcast_in_dim.11), calls=%async_computation.1 | async-start | bytes 32768 | tf_op jit(solution)/shard_map/all_to_all | solution.py:39
  121.9 10.2 %all_gather.10 = f32[512,2]{0,1:T(2,128)S(1)} all-gather(f32[128,2]{0,1:T(2,128)S(1)} %pad_maximum_fusion.7), channel_id=1, replica_groups=mesh['row'=4,'col'=4,'dp'=8] {'col'}, dimensions={0}, use_global_device_ids=true | all-gather | bytes 5120 | tf_op jit(solution)/shard_map/all_gather | solution.py:67
  132.1 0.6 pad_maximum_fusion.8
  132.7 2.6 convolution_convert_fusion
  135.3 1.3 convolution_convert_fusion.1
  136.6 38.3 %all-reduce.6.cloned.1.call-done = (f32[512,512]{1,0:T(8,128)}, f32[512,512]{1,0:T(8,128)}) async-done(((f32[512,512]{1,0:T(8,128)}, f32[512,512]{1,0:T(8,128)}), (f32[512,512]{1,0:T(8,128)}, f32[512,512]{1,0:T(8,128)})) %all-reduce.6.cloned.1.call-update) | async-done | bytes 2097168 | tf_op jit(solution)/shard_map/psum | solution.py:192
  175.0 2.3 convolution_convert_fusion.6
  177.3 2.3 convolution_convert_fusion.7
  179.5 0.0 all-reduce.8.cloned.1.call-update
  179.6 18.8 %all-reduce.1 = (bf16[512]{0:T(512)(128)(2,1)S(1)}, bf16[512]{0:T(512)(128)(2,1)S(1)}) all-reduce(bf16[512]{0:T(512)(128)(2,1)S(1)} %get-tuple-element.39, bf16[512]{0:T(512)(128)(2,1)S(1)} %get-tuple-element.38), channel_id=1, replica_groups=mesh['row'=4,'col'=4,'dp'=8] {'dp'}, use_global_device_ids=true, to_apply=%region_10.11 | all-reduce | flops 1024 | bytes 4096 | tf_op jit(solution)/shard_map/psum | solution.py:221
  198.4 1.1 fusion.40
  199.6 0.7 broadcast_in_dim.12
  200.3 4.4 %all-to-all-start.2 = ((f32[4,128,128]{2,1,0:T(8,128)}), f32[4,128,128]{2,1,0:T(8,128)S(1)}, u32[]{:S(2)}, u32[]{:S(2)}) async-start(f32[4,128,128]{2,1,0:T(8,128)} %broadcast_in_dim.12), calls=%async_computation.2 | async-start | bytes 524288 | tf_op jit(solution)/shard_map/all_to_all | solution.py:39
  204.7 0.6 multiply_add_fusion.2
  205.3 6.1 %all-to-all-done.2 = f32[4,128,128]{2,1,0:T(8,128)S(1)} async-done(((f32[4,128,128]{2,1,0:T(8,128)}), f32[4,128,128]{2,1,0:T(8,128)S(1)}, u32[]{:S(2)}, u32[]{:S(2)}) %all-to-all-start.2) | async-done | bytes 262176 | tf_op jit(solution)/shard_map/all_to_all | solution.py:39
  211.4 0.7 broadcast_multiply_fusion
  212.1 45.5 %all-reduce.8.cloned.1.call-done = (bf16[512,512]{1,0:T(8,128)(2,1)}, bf16[512,512]{1,0:T(8,128)(2,1)}, bf16[128,512]{1,0:T(8,128)(2,1)}, bf16[128,512]{1,0:T(8,128)(2,1)}) async-done(((bf16[512,512]{1,0:T(8,128)(2,1)}, bf16[512,512]{1,0:T(8,128)(2,1)}, bf16[128,512]{1,0:T(8,128)(2,1)}, bf16[128,512]{1,0:T(8,128)(2,1)}), (bf16[512,512]{1,0:T(8,128)(2,1)}, bf16[512,512]{1,0:T(8,128)(2,1)}, ...) | async-done | bytes 1310736 | tf_op jit(solution)/shard_map/psum | solution.py:217
  257.6 1.1 fusion.39
  258.7 1.1 multiply_add_fusion.1
  259.8 0.4 fusion.5
  260.2 1.2 copy-done.1
  261.4 2.5 multiply_add_fusion
  (42 shorter events, 0.2 us)
Async XLA Ops:
  7.2 29.9 %all-gather.3.cloned.1.call-start = ((), (), s32[]{:S(2)}) async-start(), calls=%async_computation.4 | async-start | bytes 1802240 | tf_op jit(solution)/shard_map/all_gather | solution.py:19
  11.4 25.6 %copy-start.2 = (f32[2,128,512]{2,1,0:T(8,128)S(1)}, f32[2,128,512]{2,1,0:T(8,128)}, u32[]{:S(2)}) copy-start(f32[2,128,512]{2,1,0:T(8,128)} %param.23) | copy-start | bytes 1572868
  11.5 73.6 %reduce-scatter.4.cloned.1.call-start = ((), (), s32[]{:S(2)}) async-start(), calls=%async_computation.6 | async-start | bytes 2621440 | tf_op jit(solution)/shard_map/reduce_scatter | solution.py:33
  12.6 25.8 %copy-start = (f32[2,512,512]{2,1,0:T(8,128)S(1)}, f32[2,512,512]{2,1,0:T(8,128)}, u32[]{:S(2)}) copy-start(f32[2,512,512]{2,1,0:T(8,128)} %param.22) | copy-start | bytes 6291460
  41.2 0.8 copy-start.3
  55.6 0.7 copy-start.10
  55.6 31.4 %copy-start.12 = (s32[128]{0:T(128)S(1)}, s32[128]{0:T(128)}, u32[]{:S(2)}) copy-start(s32[128]{0:T(128)} %param.21) | copy-start | bytes 1540
  55.6 32.8 %copy-start.11 = (f32[2,512]{1,0:T(2,128)S(1)}, f32[2,512]{1,0:T(2,128)}, u32[]{:S(2)}) copy-start(f32[2,512]{1,0:T(2,128)} %param.27) | copy-start | bytes 12292
  55.6 55.6 %all-gather.5.cloned.1.call-start = ((), (), s32[]{:S(2)}) async-start(), calls=%async_computation.5 | async-start | bytes 1310720 | tf_op jit(solution)/shard_map/all_gather | solution.py:56
  87.0 2.6 copy-start.9
  91.1 9.6 %all-to-all-start = ((f32[4,1,512]{2,1,0:T(1,128)}), f32[4,1,512]{2,1,0:T(1,128)S(1)}, u32[]{:S(2)}, u32[]{:S(2)}) async-start(f32[4,1,512]{2,1,0:T(1,128)} %broadcast_in_dim.10), calls=%async_computation | async-start | bytes 16384 | tf_op jit(solution)/shard_map/all_to_all | solution.py:39
  95.4 79.6 %all-reduce.6.cloned.1.call-start = ((), (), s32[]{:S(2)}) async-start(), calls=%async_computation.7 | async-start | bytes 4194304 | tf_op jit(solution)/shard_map/psum | solution.py:192
  111.2 2.6 copy-start.5
  118.3 14.3 %all-to-all-start.1 = ((f32[4,1,1024]{2,1,0:T(1,128)}), f32[4,1,1024]{2,1,0:T(1,128)S(1)}, u32[]{:S(2)}, u32[]{:S(2)}) async-start(f32[4,1,1024]{2,1,0:T(1,128)} %broadcast_in_dim.11), calls=%async_computation.1 | async-start | bytes 32768 | tf_op jit(solution)/shard_map/all_to_all | solution.py:39
  121.8 135.7 %all-reduce.8.cloned.1.call-start = ((), (), s32[]{:S(2)}) async-start(), calls=%async_computation.8 | async-start | bytes 2621440 | tf_op jit(solution)/shard_map/psum | solution.py:217
  132.7 2.6 copy-start.6
  179.5 79.2 %copy-start.4 = (f32[2,128,512]{2,1,0:T(8,128)S(1)}, f32[2,128,512]{2,1,0:T(8,128)}, u32[]{:S(2)}) copy-start(f32[2,128,512]{2,1,0:T(8,128)} %param.26) | copy-start | bytes 1572868
  200.3 11.1 %all-to-all-start.2 = ((f32[4,128,128]{2,1,0:T(8,128)}), f32[4,128,128]{2,1,0:T(8,128)S(1)}, u32[]{:S(2)}, u32[]{:S(2)}) async-start(f32[4,128,128]{2,1,0:T(8,128)} %broadcast_in_dim.12), calls=%async_computation.2 | async-start | bytes 524288 | tf_op jit(solution)/shard_map/all_to_all | solution.py:39
  257.6 2.3 copy-start.7
  257.6 2.3 copy-start.8
  259.8 1.6 copy-start.1
Sparse Core Ops, SparseCore 0:
  11.6 25.4 all-gather.2
  55.8 29.2 reduce-scatter.3
  87.4 23.7 all-gather.4
  115.4 59.5 all-reduce.5
  179.7 77.8 all-reduce.7
where the time goes:
time: 271 us; the launch traced here: 270 us
  waiting for transfers between devices  155 us (57%)
  matrix products  30.3 us (11%)
  blocking collectives  29 us (11%)
  other arithmetic  17 us (6%)
  between operations  14 us (5%)
  local copies, waits for them, and re-layouts  13 us (5%)
  starting transfers between devices  12.3 us (5%)
    psum x1, waiting for transfers between devices, on_device(): lax.psum(grad_ins[1].astype(jnp.bfloat16), 'dp').astype(jnp.float32)  45.5 us
    psum x1, waiting for transfers between devices, on_device(): backs = lax.psum((back_terms[0], back_terms[1]), 'row')  38.3 us
    reduce_scatter x1, waiting for transfers between devices, in_one_piece_2(): lax.psum_scatter(both, axis, scatter_dimension=dim, tiled=True)  28.8 us
    all_gather x1, waiting for transfers between devices, in_one_piece(): whole = lax.all_gather(both, axis, axis=dim, tiled=True)  21.6 us
    psum x1, blocking collectives, on_device(): lax.psum(head_grads[1].astype(jnp.bfloat16), 'dp').astype(jnp.float32)  18.8 us
    all_to_all x3, starting transfers between devices, sent_to_all(): return lax.all_to_all(copies, axis, split_axis=0, concat_axis=0, tiled=True)  12.2 us
    all_gather x1, waiting for transfers between devices, in_one_piece_3(): lax.all_gather(both, axis, axis=dim, tiled=True)  10.5 us
    all_gather x1, blocking collectives, rows_first(): whole = lax.all_gather(both, axis, axis=0, tiled=True)  10.2 us
  transfers between devices with their start and end apart: 8, of which 7 were waited for; matrix products, arithmetic and copies ran while one was open for 7% of the time, Pallas kernels for 0%

commit v1 on v0

v1 whole, which is shorter than its diff:
```python
import jax
import jax.numpy as jnp
from jax import lax
from jax.experimental import pallas as pl
from jax.experimental.pallas import tpu as pltpu
from jax.sharding import PartitionSpec as P

noise_clip = 0.5
matrix_rate = 0.004
head_rate = 0.0001
blend_rate = 0.005

bf16 = jnp.bfloat16
f32 = jnp.float32

VMEM = pl.BlockSpec(memory_space=pltpu.VMEM)
SMEM = pl.BlockSpec(memory_space=pltpu.SMEM)


def call(body, outs, ins, scratch=(), scalars=None, mib=16, flops=0, name=None):
    specs = [VMEM] * len(ins)
    if scalars is not None:
        ins = [scalars, *ins]
        specs = [SMEM, *specs]
    moved = sum(a.size * a.dtype.itemsize for a in ins)
    moved += sum(o.size * o.dtype.itemsize for o in outs)
    return pl.pallas_call(
        body,
        out_shape=tuple(outs),
        in_specs=specs,
        out_specs=tuple(VMEM for _ in outs),
        scratch_shapes=list(scratch),
        compiler_params=pltpu.CompilerParams(vmem_limit_bytes=mib * 2**20),
        cost_estimate=pl.CostEstimate(flops=flops, bytes_accessed=moved, transcendentals=0),
        name=name,
    )(*ins)


def shape(*dims, dtype=bf16):
    return jax.ShapeDtypeStruct(dims, dtype)


def dot(a, b):
    return jnp.dot(a, b, preferred_element_type=f32)


def swap(x, axis, bit):
    n = lax.axis_size(axis)
    return lax.ppermute(x, axis, [(i, i ^ bit) for i in range(n)])


def pack_body(obs, nxt, act, mean, noise, out):
    out[:, 0:512] = obs[...]
    out[:, 512:1024] = nxt[...]
    out[:, 1024:1152] = act[...]
    clipped = jnp.clip(noise[...], -noise_clip, noise_clip)
    out[:, 1152:1280] = jnp.clip(mean[...].astype(f32) + clipped, -1.0, 1.0).astype(bf16)


def weights_body(cin, tin, cact, tact, w, a, p):
    for k in range(2):
        w[k] = cin[k].astype(bf16)
        w[2 + k] = tin[k].astype(bf16)
        a[k] = cact[k].astype(bf16)
        a[2 + k] = tact[k].astype(bf16)
    p[...] = dot(a[0], w[0]).T.astype(bf16)


def forward_body(at, x0, x1, a, w, mine, out1, out2, out3, emb, acts, xs, part):
    core, col = at[0], at[1]
    xs[pl.ds(pl.multiple_of(core * 128, 128), 128), :] = x0[...]
    xs[pl.ds(pl.multiple_of((1 - core) * 128, 128), 128), :] = x1[...]
    for q in range(4):
        s = 0 if q < 2 else 512
        m = 1024 if q < 2 else 1152
        e = (xs[:, s : s + 512].astype(f32) + dot(xs[:, m : m + 128], a[q])).astype(bf16)
        if q < 2:
            emb[q] = e
        part[:, 512 * q : 512 * q + 512] = dot(e, w[q])
    acts[...] = xs[:, 1024:1152]

    def rows(k):
        return pl.ds(pl.multiple_of((col ^ k) * 64, 64), 64)

    mine[...] = part[rows(0), :]
    out1[...] = part[rows(1), :].astype(bf16)
    out2[...] = part[rows(2), :].astype(bf16)
    out3[...] = part[rows(3), :].astype(bf16)


def turn_body(emb1, emb2, acts1, acts2, left):
    for k in range(2):
        left[k, 0:512, 0:256] = emb1[k].T
        left[k, 0:512, 256:512] = emb2[k].T
        left[k, 512:640, 0:256] = acts1[...].T
        left[k, 512:640, 256:512] = acts2[...].T


def hidden_body(at, m1, r11, r12, r13, m2, r21, r22, r23, heads, rew, slope, hidden, packet, vals):
    y_hi = at[2]
    vals[...] = jnp.zeros_like(vals)
    for half, (m, r1, r2, r3) in enumerate(((m1, r11, r12, r13), (m2, r21, r22, r23))):
        rows = slice(64 * half, 64 * half + 64)
        for q in range(4):
            cols = slice(512 * q, 512 * q + 512)
            pre = (m[:, cols] + r1[:, cols].astype(f32)) + (
                r2[:, cols].astype(f32) + r3[:, cols].astype(f32)
            )
            sig = jax.nn.sigmoid(pre)
            hid = pre * sig
            v = heads[q : q + 1, :]
            vals[rows, q : q + 1] = jnp.sum(hid * v, axis=1, keepdims=True)
            if q < 2:
                hidden[rows, cols] = hid
                slope[rows, cols] = (v * (sig * (1.0 + pre * (1.0 - sig)))).astype(bf16)
    turned = vals[...].T[0:8, :]
    swapped = jnp.concatenate([turned[:, 64:128], turned[:, 0:64]], axis=1)
    turned = jnp.where(y_hi == 1, swapped, turned)
    line = lax.broadcasted_iota(jnp.int32, (8, 128), 0)
    turned = jnp.where(line < 4, turned, rew[...])
    for i in range(16):
        packet[i] = turned


def grads_body(
    at, s0, s1, s2, s3, got, left, hidden, p,
    o0, o1, o2, o3, o4, o5, o6, o7, keep, give, terr,
    delta, slope0, grad, errs,
):
    core, col, y_hi, dp = at[0], at[1], at[2], at[3]
    for c in range(4):
        v = (got[c] + got[4 + c]) + (got[8 + c] + got[12 + c])
        lanes = slice(64 * (c % 2), 64 * (c % 2) + 64)
        both = jnp.concatenate([got[c // 2 * 4][:, lanes], got[(2 + c // 2) * 4][:, lanes]], axis=1)
        goal = both[4:5] + both[5:6] * jnp.minimum(v[2:3], v[3:4])
        e = v[0:2] - goal
        e = jnp.where(y_hi == 1, jnp.concatenate([e[:, 64:128], e[:, 0:64]], axis=1), e)
        errs[c, 0:2, :] = e
    lo = jnp.concatenate([errs[0, 0:2, 0:64], errs[1, 0:2, 0:64]], axis=1)
    hi = jnp.concatenate([errs[2, 0:2, 0:64], errs[3, 0:2, 0:64]], axis=1)
    terr[...] = jnp.where(core == 1, hi, lo)
    for k, s in enumerate((s0, s1, s2, s3)):
        c = col ^ k
        block = jnp.concatenate([errs[c], jnp.zeros((120, 128), f32)], axis=0)
        e = 2.0 * block.T
        for half in range(2):
            rows = slice(64 * half, 64 * half + 64)
            to = pl.ds(pl.multiple_of(256 * half + 64 * c, 64), 64)
            slope0[to, :] = s[rows, 0:512]
            for q in range(2):
                cols = slice(512 * q, 512 * q + 512)
                delta[q, to, :] = (e[rows, q : q + 1] * s[rows, cols].astype(f32)).astype(bf16)
        if k == 0:
            heads = [
                jnp.sum(e[:, q : q + 1] * hidden[:, 512 * q : 512 * q + 512], axis=0, keepdims=True)
                for q in range(2)
            ]
    for q in range(2):
        grad[q] = dot(left[q], delta[q])
    tail = jnp.concatenate([*heads, jnp.zeros((14, 512), f32)], axis=0).astype(bf16)
    for k, o in enumerate((o0, o1, o2, o3, o4, o5, o6, o7)):
        d = dp ^ k
        wide = pl.ds(pl.multiple_of(64 * d, 64), 64)
        thin = pl.ds(pl.multiple_of(512 + 16 * d, 16), 16)
        o[0:64, :] = grad[0, wide, :].astype(bf16)
        o[64:128, :] = grad[1, wide, :].astype(bf16)
        o[128:144, :] = grad[0, thin, :].astype(bf16)
        o[144:160, :] = grad[1, thin, :].astype(bf16)
        o[160:176, :] = tail
    push = dot(slope0[...], p[...])
    first, second = push[0:128], push[128:256]
    keep[0] = jnp.where(core == 1, second, first)
    give[0] = jnp.where(core == 1, first, second)
    first, second = push[256:384], push[384:512]
    keep[1] = jnp.where(core == 1, second, first)
    give[1] = jnp.where(core == 1, first, second)


def total_body(c0, c1, c2, c3, c4, c5, c6, c7, w, chunk, act, head):
    def at(rows):
        x = [c[rows, :].astype(f32) for c in (c0, c1, c2, c3, c4, c5, c6, c7)]
        return ((x[0] + x[1]) + (x[2] + x[3])) + ((x[4] + x[5]) + (x[6] + x[7]))

    chunk[...] = at(slice(0, 128)).astype(bf16)
    head[...] = at(slice(160, 168))
    for q in range(2):
        m = at(slice(128 + 16 * q, 144 + 16 * q)).astype(bf16)
        act[16 * q : 16 * q + 16, :] = lax.dot_general(
            m, w[q], (((1,), (1,)), ((), ())), preferred_element_type=f32
        )


def update_body(at, g0, g1, g2, g3, g4, g5, g6, g7, cin, tin, fresh, blended):
    dp = at[3]
    for k, g in enumerate((g0, g1, g2, g3, g4, g5, g6, g7)):
        rows = pl.ds(pl.multiple_of(64 * (dp ^ k), 64), 64)
        for q in range(2):
            new = cin[q, rows, :] - matrix_rate * g[64 * q : 64 * q + 64, :].astype(f32)
            fresh[q, rows, :] = new
            blended[q, rows, :] = blend_rate * new + (1.0 - blend_rate) * tin[q, rows, :]


def on_device(
    observed,
    next_observed,
    actions,
    next_mean,
    policy_noise,
    rewards,
    discounts,
    actor_flags,
    critic_in,
    critic_act,
    critic_head,
    target_in,
    target_act,
    target_head,
):
    row, col, dp = lax.axis_index("row"), lax.axis_index("col"), lax.axis_index("dp")
    at = jnp.stack([row % 2, col, row // 2, dp]).astype(jnp.int32)

    (own,) = call(
        pack_body, [shape(128, 1280)],
        [observed, next_observed, actions, next_mean, policy_noise], name="pack",
    )
    sib = swap(own, "row", 1)
    far = swap(own, "row", 2)
    w16, a16, p16 = call(
        weights_body,
        [shape(4, 512, 512), shape(4, 128, 512), shape(512, 128)],
        [critic_in, target_in, critic_act, target_act],
        mib=24, flops=2 * 128 * 512 * 512, name="weights",
    )

    def forward(x0, x1, name):
        return call(
            forward_body,
            [
                shape(64, 2048, dtype=f32), shape(64, 2048), shape(64, 2048), shape(64, 2048),
                shape(2, 256, 512), shape(256, 128),
            ],
            [x0, x1, a16, w16],
            scratch=[pltpu.VMEM((256, 1280), bf16), pltpu.VMEM((256, 2048), f32)],
            scalars=at, mib=24, flops=8 * 256 * 640 * 512, name=name,
        )

    mine1, *out1, emb1, acts1 = forward(own, sib, "forward_near")
    in1 = [swap(x, "col", k + 1) for k, x in enumerate(out1)]
    farsib = swap(far, "row", 1)
    mine2, *out2, emb2, acts2 = forward(far, farsib, "forward_far")
    in2 = [swap(x, "col", k + 1) for k, x in enumerate(out2)]
    (left,) = call(
        turn_body, [shape(2, 640, 512)], [emb1, emb2, acts1, acts2], name="turn"
    )
    heads = jnp.concatenate(
        [critic_head, target_head, jnp.zeros((4, 512), f32)], axis=0
    )
    blank = jnp.zeros((1, 128), f32)
    rew = jnp.concatenate(
        [blank, blank, blank, blank, rewards.astype(f32)[None], discounts.astype(f32)[None], blank, blank]
    )
    slope, hidden, packet = call(
        hidden_body,
        [shape(128, 1024), shape(128, 1024, dtype=f32), shape(16, 8, 128, dtype=f32)],
        [mine1, *in1, mine2, *in2, heads, rew],
        scratch=[pltpu.VMEM((128, 128), f32)],
        scalars=at, name="hidden", flops=128 * 2048 * 30,
    )
    slopes = [slope] + [swap(slope, "col", k) for k in (1, 2, 3)]
    got = lax.all_to_all(packet, ("row", "col"), 0, 0, tiled=True)
    *chunks, keep, give, temporal_errors = call(
        grads_body,
        [shape(176, 512)] * 8
        + [shape(2, 128, 128, dtype=f32), shape(2, 128, 128, dtype=f32), shape(2, 128, dtype=f32)],
        [*slopes, got, left, hidden, p16],
        scratch=[
            pltpu.VMEM((2, 512, 512), bf16), pltpu.VMEM((512, 512), bf16),
            pltpu.VMEM((2, 640, 512), f32), pltpu.VMEM((4, 8, 128), f32),
        ],
        scalars=at, mib=24, name="grads", flops=4 * 640 * 512 * 512,
    )
    summed = [chunks[0]] + [swap(chunks[k], "dp", k) for k in range(1, 8)]
    push = keep + swap(give, "row", 1)
    push = push[0] + swap(push[1], "row", 2)
    push = push + swap(push, "col", 1)
    push = push + swap(push, "col", 2)
    action_slope = actor_flags.astype(f32)[:, None] * push

    chunk, act, head = call(
        total_body,
        [shape(128, 512), shape(32, 512, dtype=f32), shape(8, 512, dtype=f32)],
        [*summed, w16], name="total", flops=4 * 16 * 512 * 512,
    )
    parts = [chunk] + [swap(chunk, "dp", k) for k in range(1, 8)]
    act = act + swap(act, "row", 1)
    act = act + swap(act, "row", 2)
    head = head + swap(head, "col", 1)
    head = head + swap(head, "col", 2)
    acts = lax.all_to_all(
        jnp.broadcast_to(act.astype(bf16), (8, 32, 512)), "dp", 0, 0, tiled=True
    )
    grad_act = acts.reshape(8, 2, 16, 512).swapaxes(0, 1).reshape(2, 128, 512).astype(f32)

    new_in, new_target_in = call(
        update_body,
        [shape(2, 512, 512, dtype=f32)] * 2,
        [*parts, critic_in, target_in],
        scalars=at, mib=24, name="update",
    )
    new_act = critic_act - matrix_rate * grad_act
    new_target_act = blend_rate * new_act + (1.0 - blend_rate) * target_act
    new_head = critic_head - head_rate * head[0:2]
    new_target_head = blend_rate * new_head + (1.0 - blend_rate) * target_head
    return (
        new_in,
        new_act,
        new_head,
        new_target_in,
        new_target_act,
        new_target_head,
        temporal_errors,
        action_slope,
    )


def solution(mesh):
    return jax.shard_map(
        on_device,
        mesh=mesh,
        in_specs=(
            P(("row", "dp"), "col"),
            P(("row", "dp"), "col"),
            P(("row", "dp"), None),
            P(("row", "dp"), None),
            P(("row", "dp"), None),
            P(("row", "dp")),
            P(("row", "dp")),
            P(("row", "dp")),
            P(None, "col", "row"),
            P(None, None, "col"),
            P(None, "row"),
            P(None, "col", "row"),
            P(None, None, "col"),
            P(None, "row"),
        ),
        out_specs=(
            P(None, "col", "row"),
            P(None, None, "col"),
            P(None, "row"),
            P(None, "col", "row"),
            P(None, None, "col"),
            P(None, "row"),
            P(None, ("row", "dp")),
            P(("row", "dp"), None),
        ),
        check_vma=False,
    )
```

time: 271 us -> 145 us (0.54)
  waiting for transfers between devices: 155 us -> 42.6 us
  starting transfers between devices: 12.3 us -> 63.2 us
  matrix products: 30.3 us -> 0 us
  blocking collectives: 29 us -> 0 us
  other arithmetic: 17 us -> 2.83 us
  Pallas kernels: 0 us -> 13.6 us
  between operations: 14 us -> 0.96 us
  local copies, waits for them, and re-layouts: 13 us -> 20.9 us
    psum x2 -> x0, waiting for transfers between devices: 83.8 us -> none  [the longest x1 45.5 us: on_device(): lax.psum(grad_ins[1].astype(jnp.bfloat16), 'dp').astype(jnp.float32)]
    ppermute x0 -> x34, starting transfers between devices: none -> 55.3 us  [swap(): return lax.ppermute(x, axis, [(i, i ^ bit) for i in range(n)])]
    ppermute x0 -> x34, waiting for transfers between devices: none -> 38 us  [swap(): return lax.ppermute(x, axis, [(i, i ^ bit) for i in range(n)])]
    all_gather x2 -> x0, waiting for transfers between devices: 32.1 us -> none  [the longest x1 21.6 us: in_one_piece(): whole = lax.all_gather(both, axis, axis=dim, tiled=True)]
    dot_general x19 -> x0, matrix products: 30.3 us -> none  [the longest x4 8.52 us: contract_rows(): lax.dot_general(left, right, (((0,), (0,)), ((), ())), preferred_element_...]
    reduce_scatter x1 -> x0, waiting for transfers between devices: 28.8 us -> none  [in_one_piece_2(): lax.psum_scatter(both, axis, scatter_dimension=dim, tiled=True)]
    psum x1 -> x0, blocking collectives: 18.8 us -> none  [on_device(): lax.psum(head_grads[1].astype(jnp.bfloat16), 'dp').astype(jnp.float32)]
    pallas_call x0 -> x9, Pallas kernels: none -> 13.6 us  [call(): pl.pallas_call(body, out_shape=tuple(outs), in_specs=specs, out_specs=tup...]
  transfers between devices with their start and end apart: 8 -> 36, of which waited for: 7 -> 13; matrix products, arithmetic and copies ran while one was open for 7% -> 2% of each run, Pallas kernels for 0% -> 6%
where the time goes in v1:
time: 145 us; the launch traced here: 144 us
  starting transfers between devices  63.2 us (44%)
  waiting for transfers between devices  42.6 us (29%)
  local copies, waits for them, and re-layouts  20.9 us (14%)
  Pallas kernels  13.6 us (9%)
  other arithmetic  2.83 us (2%)
    ppermute x34, starting transfers between devices, swap(): return lax.ppermute(x, axis, [(i, i ^ bit) for i in range(n)])  55.3 us
    ppermute x34, waiting for transfers between devices, swap(): return lax.ppermute(x, axis, [(i, i ^ bit) for i in range(n)])  38 us
    unnamed x56, local copies, waits for them, and re-layouts  20 us
    pallas_call x9, Pallas kernels, call(): pl.pallas_call(body, out_shape=tuple(outs), in_specs=specs, out_specs=tup...  13.6 us
    all_to_all x1, starting transfers between devices, on_device(): got = lax.all_to_all(packet, ('row', 'col'), 0, 0, tiled=True)  4.58 us
    all_to_all x1, waiting for transfers between devices, on_device(): got = lax.all_to_all(packet, ('row', 'col'), 0, 0, tiled=True)  4.31 us
    all_to_all x1, starting transfers between devices, on_device(): lax.all_to_all(jnp.broadcast_to(act.astype(bf16), (8, 32, 512)), 'dp', 0,...  3.41 us
  transfers between devices with their start and end apart: 36, of which 13 were waited for; matrix products, arithmetic and copies ran while one was open for 2% of the time, Pallas kernels for 6%

profile of v1, /device:TPU:0, one launch (start us, length us, event | category | flops | bytes accessed | tf_op | source)
XLA Modules:
  0.0 144.2 jit_solution(5049715017292166248)
XLA Ops:
  0.6 0.9 copy-done.16
  1.5 0.9 copy-done.17
  2.4 0.8 copy-done.20
  3.3 0.8 copy-done.21
  4.0 0.8 copy-done.22
  4.8 3.4 %collective-permute-start.4 = (bf16[128,1280]{1,0:T(8,128)(2,1)S(1)}, bf16[128,1280]{1,0:T(8,128)(2,1)S(1)}, u32[]{:S(2)}, u32[]{:S(2)}) collective-permute-start(bf16[128,1280]{1,0:T(8,128)(2,1)S(1)} %pack.1.x0), channel_id=1, source_target_pairs={{0,64},{32,96},{64,0},{96,32},{1,65},{33,97},{65,1},{97,33},{2,66}... | collective-permute-start | bytes 983048 | tf_op jit(solution)/shard_map/ppermute | solution.py:49
  8.3 7.6 %collective-permute-done.4.x0 = bf16[128,1280]{1,0:T(8,128)(2,1)S(1)} collective-permute-done((bf16[128,1280]{1,0:T(8,128)(2,1)S(1)}, bf16[128,1280]{1,0:T(8,128)(2,1)S(1)}, u32[]{:S(2)}, u32[]{:S(2)}) %collective-permute-start.4) | collective-permute-done | bytes 327712 | tf_op jit(solution)/shard_map/ppermute | solution.py:49
  16.1 1.6 %copy-done = f32[2,512,512]{2,1,0:T(8,128)S(1)} copy-done((f32[2,512,512]{2,1,0:T(8,128)S(1)}, f32[2,512,512]{2,1,0:T(8,128)}, u32[]{:S(2)}) %copy-start) | copy-done | bytes 2097176
  17.7 1.6 %copy-done.2 = f32[2,512,512]{2,1,0:T(8,128)S(1)} copy-done((f32[2,512,512]{2,1,0:T(8,128)S(1)}, f32[2,512,512]{2,1,0:T(8,128)}, u32[]{:S(2)}) %copy-start.2) | copy-done | bytes 2097176
  19.3 1.0 copy-done.4
  20.3 1.0 copy-done.6
  21.3 0.5 weights.1
  21.9 2.0 %forward_near.1 = (f32[64,2048]{1,0:T(8,128)S(1)}, bf16[64,2048]{1,0:T(8,128)(2,1)S(1)}, bf16[64,2048]{1,0:T(8,128)(2,1)S(1)}, bf16[64,2048]{1,0:T(8,128)(2,1)S(...) custom-call(s32[4]{0:T(128)S(1)} %pad_add_fusion.at, bf16[128,1280]{1,0:T(8,128)(2,1)S(1)} %pack.1.x0, ...), custom_call_target="tpu_custom_call" | custom-call | flops 671088640 | bytes 5177360 | tf_op jit(solution)/shard_map/forward_near/pallas_call | solution.py:27
  23.9 0.8 copy-done.8
  24.6 2.0 %collective-permute-start.1 = (bf16[64,2048]{1,0:T(8,128)(2,1)S(1)}, bf16[64,2048]{1,0:T(8,128)(2,1)S(1)}, u32[]{:S(2)}, u32[]{:S(2)}) collective-permute-start(bf16[64,2048]{1,0:T(8,128)(2,1)S(1)} %get-tuple-element.45), channel_id=1, source_target_pairs={{0,8},{8,0},{16,24},{24,16},{1,9},{9,1},{17,25},{25,17},{2,10},{10... | collective-permute-start | bytes 786440 | tf_op jit(solution)/shard_map/ppermute | solution.py:49
  26.6 3.7 %collective-permute-start.2 = (bf16[64,2048]{1,0:T(8,128)(2,1)S(1)}, bf16[64,2048]{1,0:T(8,128)(2,1)S(1)}, u32[]{:S(2)}, u32[]{:S(2)}) collective-permute-start(bf16[64,2048]{1,0:T(8,128)(2,1)S(1)} %get-tuple-element.46), channel_id=1, source_target_pairs={{0,16},{8,24},{16,0},{24,8},{1,17},{9,25},{17,1},{25,9},{2,18},{10... | collective-permute-start | bytes 786440 | tf_op jit(solution)/shard_map/ppermute | solution.py:49
  30.3 1.9 %forward_far.1 = (f32[64,2048]{1,0:T(8,128)S(1)}, bf16[64,2048]{1,0:T(8,128)(2,1)S(1)}, bf16[64,2048]{1,0:T(8,128)(2,1)S(1)}, bf16[64,2048]{1,0:T(8,128)(2,1)S(1...) custom-call(s32[4]{0:T(128)S(1)} %pad_add_fusion.at, bf16[128,1280]{1,0:T(8,128)(2,1)S(1)} %collective-permute-done.4.x0, ...), custom_call_target="tpu_custom_call" | custom-call | flops 671088640 | bytes 5177360 | tf_op jit(solution)/shard_map/forward_far/pallas_call | solution.py:27
  32.3 0.8 copy-done.10
  33.1 4.7 %collective-permute-start.7 = (bf16[64,2048]{1,0:T(8,128)(2,1)S(1)}, bf16[64,2048]{1,0:T(8,128)(2,1)S(1)}, u32[]{:S(2)}, u32[]{:S(2)}) collective-permute-start(bf16[64,2048]{1,0:T(8,128)(2,1)S(1)} %get-tuple-element.50), channel_id=1, source_target_pairs={{0,16},{8,24},{16,0},{24,8},{1,17},{9,25},{17,1},{25,9},{2,18},{10... | collective-permute-start | bytes 786440 | tf_op jit(solution)/shard_map/ppermute | solution.py:49
  38.0 5.0 %collective-permute-done.2.r12 = bf16[64,2048]{1,0:T(8,128)(2,1)S(1)} collective-permute-done((bf16[64,2048]{1,0:T(8,128)(2,1)S(1)}, bf16[64,2048]{1,0:T(8,128)(2,1)S(1)}, u32[]{:S(2)}, u32[]{:S(2)}) %collective-permute-start.2) | collective-permute-done | bytes 262176 | tf_op jit(solution)/shard_map/ppermute | solution.py:49
  42.9 3.4 %collective-permute-done.3.r13 = bf16[64,2048]{1,0:T(8,128)(2,1)S(1)} collective-permute-done((bf16[64,2048]{1,0:T(8,128)(2,1)S(1)}, bf16[64,2048]{1,0:T(8,128)(2,1)S(1)}, u32[]{:S(2)}, u32[]{:S(2)}) %collective-permute-start.3) | collective-permute-done | bytes 262176 | tf_op jit(solution)/shard_map/ppermute | solution.py:49
  46.3 7.6 %collective-permute-done.7.r22 = bf16[64,2048]{1,0:T(8,128)(2,1)S(1)} collective-permute-done((bf16[64,2048]{1,0:T(8,128)(2,1)S(1)}, bf16[64,2048]{1,0:T(8,128)(2,1)S(1)}, u32[]{:S(2)}, u32[]{:S(2)}) %collective-permute-start.7) | collective-permute-done | bytes 262176 | tf_op jit(solution)/shard_map/ppermute | solution.py:49
  53.9 2.6 %collective-permute-done.8.r23 = bf16[64,2048]{1,0:T(8,128)(2,1)S(1)} collective-permute-done((bf16[64,2048]{1,0:T(8,128)(2,1)S(1)}, bf16[64,2048]{1,0:T(8,128)(2,1)S(1)}, u32[]{:S(2)}, u32[]{:S(2)}) %collective-permute-start.8) | collective-permute-done | bytes 262176 | tf_op jit(solution)/shard_map/ppermute | solution.py:49
  56.5 1.8 %hidden.1 = (bf16[128,1024]{1,0:T(8,128)(2,1)}, f32[128,1024]{1,0:T(8,128)S(1)}, f32[16,8,128]{2,1,0:T(8,128)}) custom-call(s32[4]{0:T(128)S(1)} %pad_add_fusion.at, f32[64,2048]{1,0:T(8,128)S(1)} %get-tuple-element.44.m1, bf16[64,2048]{1,0:T(8,128)(2,1)S(1)} %collective-permute-done.1.r11, bf16[64,2048]{1,0:T(8,128)(2,1)S(1)} %collective-permute-done.2.r12, ...), custom_call_target="tpu_custom_call" | custom-call | flops 7864320 | bytes 3493904 | tf_op jit(solution)/shard_map/hidden/pallas_call | solution.py:27
  58.3 0.8 copy-done.12
  59.1 1.7 %collective-permute-start.10 = (bf16[128,1024]{1,0:T(8,128)(2,1)}, bf16[128,1024]{1,0:T(8,128)(2,1)}, u32[]{:S(2)}, u32[]{:S(2)}) collective-permute-start(bf16[128,1024]{1,0:T(8,128)(2,1)} %get-tuple-element.52.s0), channel_id=1, source_target_pairs={{0,16},{8,24},{16,0},{24,8},{1,17},{9,25},{17,1},{25,9},{2,18},{10... | collective-permute-start | bytes 786440 | tf_op jit(solution)/shard_map/ppermute | solution.py:49
  60.9 3.0 %collective-permute-start.11 = (bf16[128,1024]{1,0:T(8,128)(2,1)}, bf16[128,1024]{1,0:T(8,128)(2,1)}, u32[]{:S(2)}, u32[]{:S(2)}) collective-permute-start(bf16[128,1024]{1,0:T(8,128)(2,1)} %get-tuple-element.52.s0), channel_id=1, source_target_pairs={{0,24},{8,16},{16,8},{24,0},{1,25},{9,17},{17,9},{25,1},{2,26},{10... | collective-permute-start | bytes 786440 | tf_op jit(solution)/shard_map/ppermute | solution.py:49
  63.8 4.6 %all-to-all-start = ((f32[16,8,128]{2,1,0:T(8,128)}), f32[16,8,128]{2,1,0:T(8,128)S(1)}, u32[]{:S(2)}, u32[]{:S(2)}) async-start(f32[16,8,128]{2,1,0:T(8,128)} %get-tuple-element.53), calls=%async_computation | async-start | bytes 131072 | tf_op jit(solution)/shard_map/all_to_all | solution.py:270
  68.4 1.0 copy-done.9
  69.5 1.0 copy-done.11
  70.5 0.8 copy-done.19
  71.8 4.3 %all-to-all-done.got = f32[16,8,128]{2,1,0:T(8,128)S(1)} async-done(((f32[16,8,128]{2,1,0:T(8,128)}), f32[16,8,128]{2,1,0:T(8,128)S(1)}, u32[]{:S(2)}, u32[]{:S(2)}) %all-to-all-start) | async-done | bytes 65568 | tf_op jit(solution)/shard_map/all_to_all | solution.py:270
  76.1 1.0 copy-done.13
  77.1 0.9 copy-done.15
  78.0 3.4 %grads.1 = (bf16[176,512]{1,0:T(8,128)(2,1)S(1)}, bf16[176,512]{1,0:T(8,128)(2,1)S(1)}, bf16[176,512]{1,0:T(8,128)(2,1)S(1)}, bf16[176,512]{1,0:T(8,128)(2,1)S(1...) custom-call(s32[4]{0:T(128)S(1)} %pad_add_fusion.at, ...), custom_call_target="tpu_custom_call" | custom-call | flops 671088640 | bytes 4785168 | tf_op jit(solution)/shard_map/grads/pallas_call | solution.py:27
  81.4 1.5 %collective-permute-start.12 = (bf16[176,512]{1,0:T(8,128)(2,1)S(1)}, bf16[176,512]{1,0:T(8,128)(2,1)S(1)}, u32[]{:S(2)}, u32[]{:S(2)}) collective-permute-start(bf16[176,512]{1,0:T(8,128)(2,1)S(1)} %get-tuple-element.61), channel_id=1, source_target_pairs={{0,1},{1,0},{2,3},{3,2},{4,5},{5,4},{6,7},{7,6},{8,9},{9,8},{10,11... | collective-permute-start | bytes 540680 | tf_op jit(solution)/shard_map/ppermute | solution.py:49
  82.9 2.7 %collective-permute-start.13 = (bf16[176,512]{1,0:T(8,128)(2,1)S(1)}, bf16[176,512]{1,0:T(8,128)(2,1)S(1)}, u32[]{:S(2)}, u32[]{:S(2)}) collective-permute-start(bf16[176,512]{1,0:T(8,128)(2,1)S(1)} %get-tuple-element.62), channel_id=1, source_target_pairs={{0,2},{1,3},{2,0},{3,1},{4,6},{5,7},{6,4},{7,5},{8,10},{9,11},{10,... | collective-permute-start | bytes 540680 | tf_op jit(solution)/shard_map/ppermute | solution.py:49
  86.1 1.2 collective-permute-start.15
  87.3 0.5 collective-permute-start.16
  87.9 0.9 collective-permute-done.12.c1
  88.8 3.7 %collective-permute-start.17 = (bf16[176,512]{1,0:T(8,128)(2,1)S(1)}, bf16[176,512]{1,0:T(8,128)(2,1)S(1)}, u32[]{:S(2)}, u32[]{:S(2)}) collective-permute-start(bf16[176,512]{1,0:T(8,128)(2,1)S(1)} %get-tuple-element.66), channel_id=1, source_target_pairs={{0,6},{1,7},{2,4},{3,5},{4,2},{5,3},{6,0},{7,1},{8,14},{9,15},{10,... | collective-permute-start | bytes 540680 | tf_op jit(solution)/shard_map/ppermute | solution.py:49
  92.5 2.4 %collective-permute-done.13.c2 = bf16[176,512]{1,0:T(8,128)(2,1)S(1)} collective-permute-done((bf16[176,512]{1,0:T(8,128)(2,1)S(1)}, bf16[176,512]{1,0:T(8,128)(2,1)S(1)}, u32[]{:S(2)}, u32[]{:S(2)}) %collective-permute-start.13) | collective-permute-done | bytes 180256 | tf_op jit(solution)/shard_map/ppermute | solution.py:49
  94.9 1.1 collective-permute-start.18
  96.0 1.5 %collective-permute-done.14.c3 = bf16[176,512]{1,0:T(8,128)(2,1)S(1)} collective-permute-done((bf16[176,512]{1,0:T(8,128)(2,1)S(1)}, bf16[176,512]{1,0:T(8,128)(2,1)S(1)}, u32[]{:S(2)}, u32[]{:S(2)}) %collective-permute-start.14) | collective-permute-done | bytes 180256 | tf_op jit(solution)/shard_map/ppermute | solution.py:49
  97.6 2.8 %collective-permute-start.31 = (f32[128,128]{1,0:T(8,128)S(1)}, f32[128,128]{1,0:T(8,128)S(1)}, u32[]{:S(2)}, u32[]{:S(2)}) collective-permute-start(f32[128,128]{1,0:T(8,128)S(1)} %slice_bitcast_fusion), channel_id=1, source_target_pairs={{0,64},{32,96},{64,0},{96,32},{1,65},{33,97},{65,1},{97,33},{2,66}... | collective-permute-start | bytes 196616 | tf_op jit(solution)/shard_map/ppermute | solution.py:49
  100.4 2.3 %collective-permute-done.17.c6 = bf16[176,512]{1,0:T(8,128)(2,1)S(1)} collective-permute-done((bf16[176,512]{1,0:T(8,128)(2,1)S(1)}, bf16[176,512]{1,0:T(8,128)(2,1)S(1)}, u32[]{:S(2)}, u32[]{:S(2)}) %collective-permute-start.17) | collective-permute-done | bytes 180256 | tf_op jit(solution)/shard_map/ppermute | solution.py:49
  102.7 3.1 %collective-permute-done.18.c7 = bf16[176,512]{1,0:T(8,128)(2,1)S(1)} collective-permute-done((bf16[176,512]{1,0:T(8,128)(2,1)S(1)}, bf16[176,512]{1,0:T(8,128)(2,1)S(1)}, u32[]{:S(2)}, u32[]{:S(2)}) %collective-permute-start.18) | collective-permute-done | bytes 180256 | tf_op jit(solution)/shard_map/ppermute | solution.py:49
  105.8 0.6 total.1
  106.6 3.7 %collective-permute-start.20 = (bf16[128,512]{1,0:T(8,128)(2,1)S(1)}, bf16[128,512]{1,0:T(8,128)(2,1)S(1)}, u32[]{:S(2)}, u32[]{:S(2)}) collective-permute-start(bf16[128,512]{1,0:T(8,128)(2,1)S(1)} %get-tuple-element.68.g0), channel_id=1, source_target_pairs={{0,2},{1,3},{2,0},{3,1},{4,6},{5,7},{6,4},{7,5},{8,10},{9,11},{10,... | collective-permute-start | bytes 393224 | tf_op jit(solution)/shard_map/ppermute | solution.py:49
  110.4 0.9 collective-permute-start.21
  111.4 4.0 %collective-permute-start.29 = (f32[8,512]{1,0:T(8,128)S(1)}, f32[8,512]{1,0:T(8,128)S(1)}, u32[]{:S(2)}, u32[]{:S(2)}) collective-permute-start(f32[8,512]{1,0:T(8,128)S(1)} %add.38), channel_id=1, source_target_pairs={{0,16},{8,24},{16,0},{24,8},{1,17},{9,25},{17,1},{25,9},{2,18},{10... | collective-permute-start | bytes 49160 | tf_op jit(solution)/shard_map/ppermute | solution.py:49
  115.5 1.6 %collective-permute-done.29 = f32[8,512]{1,0:T(8,128)S(1)} collective-permute-done((f32[8,512]{1,0:T(8,128)S(1)}, f32[8,512]{1,0:T(8,128)S(1)}, u32[]{:S(2)}, u32[]{:S(2)}) %collective-permute-start.29) | collective-permute-done | bytes 16416 | tf_op jit(solution)/shard_map/ppermute | solution.py:49
  117.0 2.9 %collective-permute-start.27 = (f32[32,512]{1,0:T(8,128)S(1)}, f32[32,512]{1,0:T(8,128)S(1)}, u32[]{:S(2)}, u32[]{:S(2)}) collective-permute-start(f32[32,512]{1,0:T(8,128)S(1)} %add.36), channel_id=1, source_target_pairs={{0,64},{32,96},{64,0},{96,32},{1,65},{33,97},{65,1},{97,33},{2,66}... | collective-permute-start | bytes 196616 | tf_op jit(solution)/shard_map/ppermute | solution.py:49
  119.9 0.6 multiply_add_fusion.1
  121.2 4.3 %collective-permute-start.24 = (bf16[128,512]{1,0:T(8,128)(2,1)S(1)}, bf16[128,512]{1,0:T(8,128)(2,1)S(1)}, u32[]{:S(2)}, u32[]{:S(2)}) collective-permute-start(bf16[128,512]{1,0:T(8,128)(2,1)S(1)} %get-tuple-element.68.g0), channel_id=1, source_target_pairs={{0,6},{1,7},{2,4},{3,5},{4,2},{5,3},{6,0},{7,1},{8,14},{9,15},{10,... | collective-permute-start | bytes 393224 | tf_op jit(solution)/shard_map/ppermute | solution.py:49
  125.5 2.2 %collective-permute-start.25 = (bf16[128,512]{1,0:T(8,128)(2,1)S(1)}, bf16[128,512]{1,0:T(8,128)(2,1)S(1)}, u32[]{:S(2)}, u32[]{:S(2)}) collective-permute-start(bf16[128,512]{1,0:T(8,128)(2,1)S(1)} %get-tuple-element.68.g0), channel_id=1, source_target_pairs={{0,7},{1,6},{2,5},{3,4},{4,3},{5,2},{6,1},{7,0},{8,15},{9,14},{10,... | collective-permute-start | bytes 393224 | tf_op jit(solution)/shard_map/ppermute | solution.py:49
  127.7 3.6 %collective-permute-start.33 = (f32[128,128]{1,0:T(8,128)S(1)}, f32[128,128]{1,0:T(8,128)S(1)}, u32[]{:S(2)}, u32[]{:S(2)}) collective-permute-start(f32[128,128]{1,0:T(8,128)S(1)} %add.44), channel_id=1, source_target_pairs={{0,16},{8,24},{16,0},{24,8},{1,17},{9,25},{17,1},{25,9},{2,18},{10... | collective-permute-start | bytes 196616 | tf_op jit(solution)/shard_map/ppermute | solution.py:49
  131.4 0.7 broadcast_in_dim.24
  132.1 3.4 %all-to-all-start.1 = ((bf16[8,32,512]{2,1,0:T(8,128)(2,1)}), bf16[8,32,512]{2,1,0:T(8,128)(2,1)S(1)}, u32[]{:S(2)}, u32[]{:S(2)}) async-start(bf16[8,32,512]{2,1,0:T(8,128)(2,1)} %broadcast_in_dim.24), calls=%async_computation.1 | async-start | bytes 524288 | tf_op jit(solution)/shard_map/all_to_all | solution.py:299
  135.6 1.6 %copy-done.1 = f32[2,512,512]{2,1,0:T(8,128)S(1)} copy-done((f32[2,512,512]{2,1,0:T(8,128)S(1)}, f32[2,512,512]{2,1,0:T(8,128)}, u32[]{:S(2)}) %copy-start.1) | copy-done | bytes 2097176
  137.2 1.6 %copy-done.3 = f32[2,512,512]{2,1,0:T(8,128)S(1)} copy-done((f32[2,512,512]{2,1,0:T(8,128)S(1)}, f32[2,512,512]{2,1,0:T(8,128)}, u32[]{:S(2)}) %copy-start.3) | copy-done | bytes 2097176
  138.7 3.0 %update.1 = (f32[2,512,512]{2,1,0:T(8,128)}, f32[2,512,512]{2,1,0:T(8,128)}) custom-call(s32[4]{0:T(128)S(1)} %pad_add_fusion.at, bf16[128,512]{1,0:T(8,128)(2,1)S(1)} %get-tuple-element.68.g0, bf16[128,512]{1,0:T(8,128)(2,1)S(1)} %collective-permute-done.19.g1, bf16[128,512]{1,0:T(8,128)(2,1)S(1)} %collective-permute-done.20.g2, ...), custom_call_target="tpu_custom_call" | custom-call | bytes 9437200 | tf_op jit(solution)/shard_map/update/pallas_call | solution.py:27
  141.8 0.7 add_multiply_fusion
  143.0 1.2 multiply_add_fusion
  (95 shorter events, 3.0 us)
Async XLA Ops:
  0.6 0.9 copy-start.16
  1.5 0.9 copy-start.17
  2.4 0.8 copy-start.20
  3.3 0.8 copy-start.21
  4.0 0.8 copy-start.22
  4.8 11.1 %collective-permute-start.4 = (bf16[128,1280]{1,0:T(8,128)(2,1)S(1)}, bf16[128,1280]{1,0:T(8,128)(2,1)S(1)}, u32[]{:S(2)}, u32[]{:S(2)}) collective-permute-start(bf16[128,1280]{1,0:T(8,128)(2,1)S(1)} %pack.1.x0), channel_id=1, source_target_pairs={{0,64},{32,96},{64,0},{96,32},{1,65},{33,97},{65,1},{97,33},{2,66}... | collective-permute-start | bytes 983048 | tf_op jit(solution)/shard_map/ppermute | solution.py:49
  8.2 13.7 %collective-permute-start = (bf16[128,1280]{1,0:T(8,128)(2,1)S(1)}, bf16[128,1280]{1,0:T(8,128)(2,1)S(1)}, u32[]{:S(2)}, u32[]{:S(2)}) collective-permute-start(bf16[128,1280]{1,0:T(8,128)(2,1)S(1)} %pack.1.x0), channel_id=1, source_target_pairs={{0,32},{32,0},{64,96},{96,64},{1,33},{33,1},{65,97},{97,65},{2,34}... | collective-permute-start | bytes 983048 | tf_op jit(solution)/shard_map/ppermute | solution.py:49
  15.9 14.4 %collective-permute-start.5 = (bf16[128,1280]{1,0:T(8,128)(2,1)S(1)}, bf16[128,1280]{1,0:T(8,128)(2,1)S(1)}, u32[]{:S(2)}, u32[]{:S(2)}) collective-permute-start(bf16[128,1280]{1,0:T(8,128)(2,1)S(1)} %collective-permute-done.4.x0), channel_id=1, source_target_pairs={{0,32},{32,0},{64,96},{96,64},{1,33},{33,1},{65,97},{97,65},{2,34}... | collective-permute-start | bytes 983048 | tf_op jit(solution)/shard_map/ppermute | solution.py:49
  16.1 1.6 %copy-start = (f32[2,512,512]{2,1,0:T(8,128)S(1)}, f32[2,512,512]{2,1,0:T(8,128)}, u32[]{:S(2)}) copy-start(f32[2,512,512]{2,1,0:T(8,128)} %cin.3) | copy-start | bytes 6291460
  17.7 1.6 %copy-start.2 = (f32[2,512,512]{2,1,0:T(8,128)S(1)}, f32[2,512,512]{2,1,0:T(8,128)}, u32[]{:S(2)}) copy-start(f32[2,512,512]{2,1,0:T(8,128)} %tin.3) | copy-start | bytes 6291460
  19.3 1.0 copy-start.4
  20.3 1.0 copy-start.6
  21.8 10.4 %copy-start.14 = (bf16[512,128]{1,0:T(8,128)(2,1)}, bf16[512,128]{1,0:T(8,128)(2,1)S(1)}, u32[]{:S(2)}) copy-start(bf16[512,128]{1,0:T(8,128)(2,1)S(1)} %get-tuple-element.59.p) | copy-start | bytes 393220
  21.8 4.8 %copy-start.25 = (bf16[128]{0:T(256)(128)(2,1)S(1)}, bf16[128]{0:T(256)(128)(2,1)}, u32[]{:S(2)}) copy-start(bf16[128]{0:T(256)(128)(2,1)} %param.20) | copy-start | bytes 772
  21.9 4.8 %copy-start.26 = (bf16[128]{0:T(256)(128)(2,1)S(1)}, bf16[128]{0:T(256)(128)(2,1)}, u32[]{:S(2)}) copy-start(bf16[128]{0:T(256)(128)(2,1)} %param.19) | copy-start | bytes 772
  23.8 0.8 copy-start.8
  24.6 13.3 %copy-start.23 = (f32[2,512]{1,0:T(2,128)S(1)}, f32[2,512]{1,0:T(2,128)}, u32[]{:S(2)}) copy-start(f32[2,512]{1,0:T(2,128)} %param.27) | copy-start | bytes 12292
  24.6 13.3 %copy-start.24 = (f32[2,512]{1,0:T(2,128)S(1)}, f32[2,512]{1,0:T(2,128)}, u32[]{:S(2)}) copy-start(f32[2,512]{1,0:T(2,128)} %param.24) | copy-start | bytes 12292
  24.6 13.1 %collective-permute-start.1 = (bf16[64,2048]{1,0:T(8,128)(2,1)S(1)}, bf16[64,2048]{1,0:T(8,128)(2,1)S(1)}, u32[]{:S(2)}, u32[]{:S(2)}) collective-permute-start(bf16[64,2048]{1,0:T(8,128)(2,1)S(1)} %get-tuple-element.45), channel_id=1, source_target_pairs={{0,8},{8,0},{16,24},{24,16},{1,9},{9,1},{17,25},{25,17},{2,10},{10... | collective-permute-start | bytes 786440 | tf_op jit(solution)/shard_map/ppermute | solution.py:49
  26.6 16.3 %collective-permute-start.2 = (bf16[64,2048]{1,0:T(8,128)(2,1)S(1)}, bf16[64,2048]{1,0:T(8,128)(2,1)S(1)}, u32[]{:S(2)}, u32[]{:S(2)}) collective-permute-start(bf16[64,2048]{1,0:T(8,128)(2,1)S(1)} %get-tuple-element.46), channel_id=1, source_target_pairs={{0,16},{8,24},{16,0},{24,8},{1,17},{9,25},{17,1},{25,9},{2,18},{10... | collective-permute-start | bytes 786440 | tf_op jit(solution)/shard_map/ppermute | solution.py:49
  30.3 16.0 %collective-permute-start.3 = (bf16[64,2048]{1,0:T(8,128)(2,1)S(1)}, bf16[64,2048]{1,0:T(8,128)(2,1)S(1)}, u32[]{:S(2)}, u32[]{:S(2)}) collective-permute-start(bf16[64,2048]{1,0:T(8,128)(2,1)S(1)} %get-tuple-element.47), channel_id=1, source_target_pairs={{0,24},{8,16},{16,8},{24,0},{1,25},{9,17},{17,9},{25,1},{2,26},{10... | collective-permute-start | bytes 786440 | tf_op jit(solution)/shard_map/ppermute | solution.py:49
  32.3 0.8 copy-start.10
  33.0 35.4 %copy-start.18 = (bf16[256,128]{1,0:T(8,128)(2,1)}, bf16[256,128]{1,0:T(8,128)(2,1)S(1)}, u32[]{:S(2)}) copy-start(bf16[256,128]{1,0:T(8,128)(2,1)S(1)} %get-tuple-element.57.acts2) | copy-start | bytes 196612
  33.1 13.2 %collective-permute-start.6 = (bf16[64,2048]{1,0:T(8,128)(2,1)S(1)}, bf16[64,2048]{1,0:T(8,128)(2,1)S(1)}, u32[]{:S(2)}, u32[]{:S(2)}) collective-permute-start(bf16[64,2048]{1,0:T(8,128)(2,1)S(1)} %get-tuple-element.49), channel_id=1, source_target_pairs={{0,8},{8,0},{16,24},{24,16},{1,9},{9,1},{17,25},{25,17},{2,10},{10... | collective-permute-start | bytes 786440 | tf_op jit(solution)/shard_map/ppermute | solution.py:49
  33.1 20.8 %collective-permute-start.7 = (bf16[64,2048]{1,0:T(8,128)(2,1)S(1)}, bf16[64,2048]{1,0:T(8,128)(2,1)S(1)}, u32[]{:S(2)}, u32[]{:S(2)}) collective-permute-start(bf16[64,2048]{1,0:T(8,128)(2,1)S(1)} %get-tuple-element.50), channel_id=1, source_target_pairs={{0,16},{8,24},{16,0},{24,8},{1,17},{9,25},{17,1},{25,9},{2,18},{10... | collective-permute-start | bytes 786440 | tf_op jit(solution)/shard_map/ppermute | solution.py:49
  37.8 18.7 %collective-permute-start.8 = (bf16[64,2048]{1,0:T(8,128)(2,1)S(1)}, bf16[64,2048]{1,0:T(8,128)(2,1)S(1)}, u32[]{:S(2)}, u32[]{:S(2)}) collective-permute-start(bf16[64,2048]{1,0:T(8,128)(2,1)S(1)} %get-tuple-element.51), channel_id=1, source_target_pairs={{0,24},{8,16},{16,8},{24,0},{1,25},{9,17},{17,9},{25,1},{2,26},{10... | collective-permute-start | bytes 786440 | tf_op jit(solution)/shard_map/ppermute | solution.py:49
  58.3 0.8 copy-start.12
  59.1 16.9 %collective-permute-start.9 = (bf16[128,1024]{1,0:T(8,128)(2,1)}, bf16[128,1024]{1,0:T(8,128)(2,1)}, u32[]{:S(2)}, u32[]{:S(2)}) collective-permute-start(bf16[128,1024]{1,0:T(8,128)(2,1)} %get-tuple-element.52.s0), channel_id=1, source_target_pairs={{0,8},{8,0},{16,24},{24,16},{1,9},{9,1},{17,25},{25,17},{2,10},{10... | collective-permute-start | bytes 786440 | tf_op jit(solution)/shard_map/ppermute | solution.py:49
  59.1 16.9 %collective-permute-start.10 = (bf16[128,1024]{1,0:T(8,128)(2,1)}, bf16[128,1024]{1,0:T(8,128)(2,1)}, u32[]{:S(2)}, u32[]{:S(2)}) collective-permute-start(bf16[128,1024]{1,0:T(8,128)(2,1)} %get-tuple-element.52.s0), channel_id=1, source_target_pairs={{0,16},{8,24},{16,0},{24,8},{1,17},{9,25},{17,1},{25,9},{2,18},{10... | collective-permute-start | bytes 786440 | tf_op jit(solution)/shard_map/ppermute | solution.py:49
  60.9 15.2 %collective-permute-start.11 = (bf16[128,1024]{1,0:T(8,128)(2,1)}, bf16[128,1024]{1,0:T(8,128)(2,1)}, u32[]{:S(2)}, u32[]{:S(2)}) collective-permute-start(bf16[128,1024]{1,0:T(8,128)(2,1)} %get-tuple-element.52.s0), channel_id=1, source_target_pairs={{0,24},{8,16},{16,8},{24,0},{1,25},{9,17},{17,9},{25,1},{2,26},{10... | collective-permute-start | bytes 786440 | tf_op jit(solution)/shard_map/ppermute | solution.py:49
  63.8 12.2 %all-to-all-start = ((f32[16,8,128]{2,1,0:T(8,128)}), f32[16,8,128]{2,1,0:T(8,128)S(1)}, u32[]{:S(2)}, u32[]{:S(2)}) async-start(f32[16,8,128]{2,1,0:T(8,128)} %get-tuple-element.53), calls=%async_computation | async-start | bytes 131072 | tf_op jit(solution)/shard_map/all_to_all | solution.py:270
  68.4 1.0 copy-start.9
  69.5 1.0 copy-start.11
  70.5 0.8 copy-start.19
  76.1 1.0 copy-start.13
  77.1 0.9 copy-start.15
  81.4 25.2 %copy-start.27 = (s32[128]{0:T(128)S(1)}, s32[128]{0:T(128)}, u32[]{:S(2)}) copy-start(s32[128]{0:T(128)} %param.21) | copy-start | bytes 1540
  81.4 7.4 %collective-permute-start.12 = (bf16[176,512]{1,0:T(8,128)(2,1)S(1)}, bf16[176,512]{1,0:T(8,128)(2,1)S(1)}, u32[]{:S(2)}, u32[]{:S(2)}) collective-permute-start(bf16[176,512]{1,0:T(8,128)(2,1)S(1)} %get-tuple-element.61), channel_id=1, source_target_pairs={{0,1},{1,0},{2,3},{3,2},{4,5},{5,4},{6,7},{7,6},{8,9},{9,8},{10,11... | collective-permute-start | bytes 540680 | tf_op jit(solution)/shard_map/ppermute | solution.py:49
  82.9 12.0 %collective-permute-start.13 = (bf16[176,512]{1,0:T(8,128)(2,1)S(1)}, bf16[176,512]{1,0:T(8,128)(2,1)S(1)}, u32[]{:S(2)}, u32[]{:S(2)}) collective-permute-start(bf16[176,512]{1,0:T(8,128)(2,1)S(1)} %get-tuple-element.62), channel_id=1, source_target_pairs={{0,2},{1,3},{2,0},{3,1},{4,6},{5,7},{6,4},{7,5},{8,10},{9,11},{10,... | collective-permute-start | bytes 540680 | tf_op jit(solution)/shard_map/ppermute | solution.py:49
  85.6 1.7 %collective-permute-start.30 = (f32[2,128,128]{2,1,0:T(8,128)S(1)}, f32[2,128,128]{2,1,0:T(8,128)S(1)}, u32[]{:S(2)}, u32[]{:S(2)}) collective-permute-start(f32[2,128,128]{2,1,0:T(8,128)S(1)} %get-tuple-element.75), channel_id=1, source_target_pairs={{0,32},{32,0},{64,96},{96,64},{1,33},{33,1},{65,97},{97,65},{2,34}... | collective-permute-start | bytes 393224 | tf_op jit(solution)/shard_map/ppermute | solution.py:49
  85.6 11.9 %collective-permute-start.14 = (bf16[176,512]{1,0:T(8,128)(2,1)S(1)}, bf16[176,512]{1,0:T(8,128)(2,1)S(1)}, u32[]{:S(2)}, u32[]{:S(2)}) collective-permute-start(bf16[176,512]{1,0:T(8,128)(2,1)S(1)} %get-tuple-element.63), channel_id=1, source_target_pairs={{0,3},{1,2},{2,1},{3,0},{4,7},{5,6},{6,5},{7,4},{8,11},{9,10},{10,... | collective-permute-start | bytes 540680 | tf_op jit(solution)/shard_map/ppermute | solution.py:49
  86.1 14.3 %collective-permute-start.15 = (bf16[176,512]{1,0:T(8,128)(2,1)S(1)}, bf16[176,512]{1,0:T(8,128)(2,1)S(1)}, u32[]{:S(2)}, u32[]{:S(2)}) collective-permute-start(bf16[176,512]{1,0:T(8,128)(2,1)S(1)} %get-tuple-element.64), channel_id=1, source_target_pairs={{0,4},{1,5},{2,6},{3,7},{4,0},{5,1},{6,2},{7,3},{8,12},{9,13},{10,... | collective-permute-start | bytes 540680 | tf_op jit(solution)/shard_map/ppermute | solution.py:49
  87.3 13.1 %collective-permute-start.16 = (bf16[176,512]{1,0:T(8,128)(2,1)S(1)}, bf16[176,512]{1,0:T(8,128)(2,1)S(1)}, u32[]{:S(2)}, u32[]{:S(2)}) collective-permute-start(bf16[176,512]{1,0:T(8,128)(2,1)S(1)} %get-tuple-element.65), channel_id=1, source_target_pairs={{0,5},{1,4},{2,7},{3,6},{4,1},{5,0},{6,3},{7,2},{8,13},{9,12},{10,... | collective-permute-start | bytes 540680 | tf_op jit(solution)/shard_map/ppermute | solution.py:49
  88.8 13.9 %collective-permute-start.17 = (bf16[176,512]{1,0:T(8,128)(2,1)S(1)}, bf16[176,512]{1,0:T(8,128)(2,1)S(1)}, u32[]{:S(2)}, u32[]{:S(2)}) collective-permute-start(bf16[176,512]{1,0:T(8,128)(2,1)S(1)} %get-tuple-element.66), channel_id=1, source_target_pairs={{0,6},{1,7},{2,4},{3,5},{4,2},{5,3},{6,0},{7,1},{8,14},{9,15},{10,... | collective-permute-start | bytes 540680 | tf_op jit(solution)/shard_map/ppermute | solution.py:49
  94.9 10.9 %collective-permute-start.18 = (bf16[176,512]{1,0:T(8,128)(2,1)S(1)}, bf16[176,512]{1,0:T(8,128)(2,1)S(1)}, u32[]{:S(2)}, u32[]{:S(2)}) collective-permute-start(bf16[176,512]{1,0:T(8,128)(2,1)S(1)} %get-tuple-element.67), channel_id=1, source_target_pairs={{0,7},{1,6},{2,5},{3,4},{4,3},{5,2},{6,1},{7,0},{8,15},{9,14},{10,... | collective-permute-start | bytes 540680 | tf_op jit(solution)/shard_map/ppermute | solution.py:49
  97.6 13.8 %collective-permute-start.31 = (f32[128,128]{1,0:T(8,128)S(1)}, f32[128,128]{1,0:T(8,128)S(1)}, u32[]{:S(2)}, u32[]{:S(2)}) collective-permute-start(f32[128,128]{1,0:T(8,128)S(1)} %slice_bitcast_fusion), channel_id=1, source_target_pairs={{0,64},{32,96},{64,0},{96,32},{1,65},{33,97},{65,1},{97,33},{2,66}... | collective-permute-start | bytes 196616 | tf_op jit(solution)/shard_map/ppermute | solution.py:49
  106.4 4.9 %collective-permute-start.28 = (f32[8,512]{1,0:T(8,128)S(1)}, f32[8,512]{1,0:T(8,128)S(1)}, u32[]{:S(2)}, u32[]{:S(2)}) collective-permute-start(f32[8,512]{1,0:T(8,128)S(1)} %get-tuple-element.71), channel_id=1, source_target_pairs={{0,8},{8,0},{16,24},{24,16},{1,9},{9,1},{17,25},{25,17},{2,10},{10... | collective-permute-start | bytes 49160 | tf_op jit(solution)/shard_map/ppermute | solution.py:49
  106.6 14.2 %collective-permute-start.19 = (bf16[128,512]{1,0:T(8,128)(2,1)S(1)}, bf16[128,512]{1,0:T(8,128)(2,1)S(1)}, u32[]{:S(2)}, u32[]{:S(2)}) collective-permute-start(bf16[128,512]{1,0:T(8,128)(2,1)S(1)} %get-tuple-element.68.g0), channel_id=1, source_target_pairs={{0,1},{1,0},{2,3},{3,2},{4,5},{5,4},{6,7},{7,6},{8,9},{9,8},{10,11... | collective-permute-start | bytes 393224 | tf_op jit(solution)/shard_map/ppermute | solution.py:49
  106.6 14.5 %collective-permute-start.20 = (bf16[128,512]{1,0:T(8,128)(2,1)S(1)}, bf16[128,512]{1,0:T(8,128)(2,1)S(1)}, u32[]{:S(2)}, u32[]{:S(2)}) collective-permute-start(bf16[128,512]{1,0:T(8,128)(2,1)S(1)} %get-tuple-element.68.g0), channel_id=1, source_target_pairs={{0,2},{1,3},{2,0},{3,1},{4,6},{5,7},{6,4},{7,5},{8,10},{9,11},{10,... | collective-permute-start | bytes 393224 | tf_op jit(solution)/shard_map/ppermute | solution.py:49
  110.4 15.1 %collective-permute-start.21 = (bf16[128,512]{1,0:T(8,128)(2,1)S(1)}, bf16[128,512]{1,0:T(8,128)(2,1)S(1)}, u32[]{:S(2)}, u32[]{:S(2)}) collective-permute-start(bf16[128,512]{1,0:T(8,128)(2,1)S(1)} %get-tuple-element.68.g0), channel_id=1, source_target_pairs={{0,3},{1,2},{2,1},{3,0},{4,7},{5,6},{6,5},{7,4},{8,11},{9,10},{10,... | collective-permute-start | bytes 393224 | tf_op jit(solution)/shard_map/ppermute | solution.py:49
  111.3 4.0 %collective-permute-start.26 = (f32[32,512]{1,0:T(8,128)S(1)}, f32[32,512]{1,0:T(8,128)S(1)}, u32[]{:S(2)}, u32[]{:S(2)}) collective-permute-start(f32[32,512]{1,0:T(8,128)S(1)} %get-tuple-element.70), channel_id=1, source_target_pairs={{0,32},{32,0},{64,96},{96,64},{1,33},{33,1},{65,97},{97,65},{2,34}... | collective-permute-start | bytes 196616 | tf_op jit(solution)/shard_map/ppermute | solution.py:49
  111.4 5.7 %collective-permute-start.29 = (f32[8,512]{1,0:T(8,128)S(1)}, f32[8,512]{1,0:T(8,128)S(1)}, u32[]{:S(2)}, u32[]{:S(2)}) collective-permute-start(f32[8,512]{1,0:T(8,128)S(1)} %add.38), channel_id=1, source_target_pairs={{0,16},{8,24},{16,0},{24,8},{1,17},{9,25},{17,1},{25,9},{2,18},{10... | collective-permute-start | bytes 49160 | tf_op jit(solution)/shard_map/ppermute | solution.py:49
  115.3 5.2 %collective-permute-start.32 = (f32[128,128]{1,0:T(8,128)S(1)}, f32[128,128]{1,0:T(8,128)S(1)}, u32[]{:S(2)}, u32[]{:S(2)}) collective-permute-start(f32[128,128]{1,0:T(8,128)S(1)} %fusion), channel_id=1, source_target_pairs={{0,8},{8,0},{16,24},{24,16},{1,9},{9,1},{17,25},{25,17},{2,10},{10... | collective-permute-start | bytes 196616 | tf_op jit(solution)/shard_map/ppermute | solution.py:49
  117.0 10.7 %collective-permute-start.27 = (f32[32,512]{1,0:T(8,128)S(1)}, f32[32,512]{1,0:T(8,128)S(1)}, u32[]{:S(2)}, u32[]{:S(2)}) collective-permute-start(f32[32,512]{1,0:T(8,128)S(1)} %add.36), channel_id=1, source_target_pairs={{0,64},{32,96},{64,0},{96,32},{1,65},{33,97},{65,1},{97,33},{2,66}... | collective-permute-start | bytes 196616 | tf_op jit(solution)/shard_map/ppermute | solution.py:49
  120.6 15.0 %collective-permute-start.22 = (bf16[128,512]{1,0:T(8,128)(2,1)S(1)}, bf16[128,512]{1,0:T(8,128)(2,1)S(1)}, u32[]{:S(2)}, u32[]{:S(2)}) collective-permute-start(bf16[128,512]{1,0:T(8,128)(2,1)S(1)} %get-tuple-element.68.g0), channel_id=1, source_target_pairs={{0,4},{1,5},{2,6},{3,7},{4,0},{5,1},{6,2},{7,3},{8,12},{9,13},{10,... | collective-permute-start | bytes 393224 | tf_op jit(solution)/shard_map/ppermute | solution.py:49
  120.9 14.7 %collective-permute-start.23 = (bf16[128,512]{1,0:T(8,128)(2,1)S(1)}, bf16[128,512]{1,0:T(8,128)(2,1)S(1)}, u32[]{:S(2)}, u32[]{:S(2)}) collective-permute-start(bf16[128,512]{1,0:T(8,128)(2,1)S(1)} %get-tuple-element.68.g0), channel_id=1, source_target_pairs={{0,5},{1,4},{2,7},{3,6},{4,1},{5,0},{6,3},{7,2},{8,13},{9,12},{10,... | collective-permute-start | bytes 393224 | tf_op jit(solution)/shard_map/ppermute | solution.py:49
  121.2 14.4 %collective-permute-start.24 = (bf16[128,512]{1,0:T(8,128)(2,1)S(1)}, bf16[128,512]{1,0:T(8,128)(2,1)S(1)}, u32[]{:S(2)}, u32[]{:S(2)}) collective-permute-start(bf16[128,512]{1,0:T(8,128)(2,1)S(1)} %get-tuple-element.68.g0), channel_id=1, source_target_pairs={{0,6},{1,7},{2,4},{3,5},{4,2},{5,3},{6,0},{7,1},{8,14},{9,15},{10,... | collective-permute-start | bytes 393224 | tf_op jit(solution)/shard_map/ppermute | solution.py:49
  125.5 10.0 %collective-permute-start.25 = (bf16[128,512]{1,0:T(8,128)(2,1)S(1)}, bf16[128,512]{1,0:T(8,128)(2,1)S(1)}, u32[]{:S(2)}, u32[]{:S(2)}) collective-permute-start(bf16[128,512]{1,0:T(8,128)(2,1)S(1)} %get-tuple-element.68.g0), channel_id=1, source_target_pairs={{0,7},{1,6},{2,5},{3,4},{4,3},{5,2},{6,1},{7,0},{8,15},{9,14},{10,... | collective-permute-start | bytes 393224 | tf_op jit(solution)/shard_map/ppermute | solution.py:49
  127.7 14.1 %collective-permute-start.33 = (f32[128,128]{1,0:T(8,128)S(1)}, f32[128,128]{1,0:T(8,128)S(1)}, u32[]{:S(2)}, u32[]{:S(2)}) collective-permute-start(f32[128,128]{1,0:T(8,128)S(1)} %add.44), channel_id=1, source_target_pairs={{0,16},{8,24},{16,0},{24,8},{1,17},{9,25},{17,1},{25,9},{2,18},{10... | collective-permute-start | bytes 196616 | tf_op jit(solution)/shard_map/ppermute | solution.py:49
  132.1 10.6 %all-to-all-start.1 = ((bf16[8,32,512]{2,1,0:T(8,128)(2,1)}), bf16[8,32,512]{2,1,0:T(8,128)(2,1)S(1)}, u32[]{:S(2)}, u32[]{:S(2)}) async-start(bf16[8,32,512]{2,1,0:T(8,128)(2,1)} %broadcast_in_dim.24), calls=%async_computation.1 | async-start | bytes 524288 | tf_op jit(solution)/shard_map/all_to_all | solution.py:299
  135.6 1.6 %copy-start.1 = (f32[2,512,512]{2,1,0:T(8,128)S(1)}, f32[2,512,512]{2,1,0:T(8,128)}, u32[]{:S(2)}) copy-start(f32[2,512,512]{2,1,0:T(8,128)} %cin.3) | copy-start | bytes 6291460
  137.2 1.6 %copy-start.3 = (f32[2,512,512]{2,1,0:T(8,128)S(1)}, f32[2,512,512]{2,1,0:T(8,128)}, u32[]{:S(2)}) copy-start(f32[2,512,512]{2,1,0:T(8,128)} %tin.3) | copy-start | bytes 6291460
  141.8 1.1 copy-start.5
  141.8 1.2 copy-start.7

commit v2 on v1

v2 whole, which is shorter than its diff:
```python
import jax
import jax.numpy as jnp
from jax import lax
from jax.experimental import pallas as pl
from jax.experimental.pallas import tpu as pltpu
from jax.sharding import PartitionSpec as P

noise_clip = 0.5
matrix_rate = 0.004
head_rate = 0.0001
blend_rate = 0.005

bf16 = jnp.bfloat16
f32 = jnp.float32

SPECS = {m: pl.BlockSpec(memory_space=m) for m in (pltpu.VMEM, pltpu.SMEM, pltpu.HBM)}
ANY = pl.BlockSpec(memory_space=pl.ANY)
DMA = pltpu.SemaphoreType.DMA
VMEM, HBM = pltpu.VMEM, pltpu.HBM


def call(
    body, outs, ins, scratch=(), scalars=None, mib=16, flops=0, name=None,
    where=(), to=(), raw=(), aliases=None,
):
    moved = sum(a.size * a.dtype.itemsize for a in ins)
    moved += sum(o.size * o.dtype.itemsize for o in outs)
    raw_out = to == "raw"
    to = range(len(outs)) if raw_out else to
    specs = [SPECS[HBM if i in raw else VMEM] for i in range(len(ins))]
    ins = [
        pltpu.with_memory_space_constraint(a, HBM) if i in raw or i in where else a
        for i, a in enumerate(ins)
    ]
    if scalars is not None:
        ins = [scalars, *ins]
        specs = [SPECS[pltpu.SMEM], *specs]
    return pl.pallas_call(
        body,
        out_shape=tuple(HBM(o.shape, o.dtype) if i in to else o for i, o in enumerate(outs)),
        in_specs=specs,
        out_specs=tuple(SPECS[HBM if raw_out else VMEM] for _ in outs),
        scratch_shapes=list(scratch),
        input_output_aliases=aliases or {},
        compiler_params=pltpu.CompilerParams(vmem_limit_bytes=mib * 2**20),
        cost_estimate=pl.CostEstimate(flops=flops, bytes_accessed=moved, transcendentals=0),
        name=name,
    )(*ins)


def after(x, other):
    return pl.pallas_call(
        lambda x, other, out: None,
        out_shape=jax.ShapeDtypeStruct(x.shape, x.dtype),
        in_specs=[ANY, ANY],
        out_specs=ANY,
        input_output_aliases={0: 0},
        name="after",
    )(x, other)


def shape(*dims, dtype=bf16):
    return jax.ShapeDtypeStruct(dims, dtype)


def dot(a, b):
    return jnp.dot(a, b, preferred_element_type=f32)


def swap(x, axis, bit):
    n = lax.axis_size(axis)
    return lax.ppermute(x, axis, [(i, i ^ bit) for i in range(n)])


def pack_body(obs, nxt, act, mean, noise, out, means, noises, sems):
    copies = [
        pltpu.make_async_copy(src, dst, sems.at[i])
        for i, (src, dst) in enumerate(
            (
                (mean, means),
                (noise, noises),
                (obs, out.at[:, 0:512]),
                (nxt, out.at[:, 512:1024]),
                (act, out.at[:, 1024:1152]),
            )
        )
    ]
    for c in copies:
        c.start()
    copies[0].wait()
    copies[1].wait()
    clipped = jnp.clip(noises[...], -noise_clip, noise_clip)
    out[:, 1152:1280] = jnp.clip(means[...].astype(f32) + clipped, -1.0, 1.0).astype(bf16)
    for c in copies[2:]:
        c.wait()


def weights_body(cin, tin, cact, tact, w, a, p, wide, thin, sems):
    pairs = []
    for k in range(2):
        pairs.append((cact.at[k], thin.at[k]))
        pairs.append((cin.at[k], wide.at[k]))
    for k in range(2):
        pairs.append((tact.at[k], thin.at[2 + k]))
        pairs.append((tin.at[k], wide.at[2 + k]))
    copies = [pltpu.make_async_copy(src, dst, sems.at[i]) for i, (src, dst) in enumerate(pairs)]
    for c in copies:
        c.start()
    for k in range(4):
        copies[2 * k].wait()
        a[k] = thin[k].astype(bf16)
        copies[2 * k + 1].wait()
        w[k] = wide[k].astype(bf16)
        if k == 0:
            p[...] = dot(a[0], w[0]).T.astype(bf16)


def forward_body(at, x0, x1, a, w, mine, out1, out2, out3, left, xs, part):
    core, col = at[0], at[1]
    xs[pl.ds(pl.multiple_of(core * 128, 128), 128), :] = x0[...]
    xs[pl.ds(pl.multiple_of((1 - core) * 128, 128), 128), :] = x1[...]
    turned = xs[:, 1024:1152].T
    for q in range(4):
        s = 0 if q < 2 else 512
        m = 1024 if q < 2 else 1152
        e = (xs[:, s : s + 512].astype(f32) + dot(xs[:, m : m + 128], a[q])).astype(bf16)
        if q < 2:
            left[q, 0:512, :] = e.T
            left[q, 512:640, :] = turned
        part[:, 512 * q : 512 * q + 512] = dot(e, w[q])

    def rows(k):
        return pl.ds(pl.multiple_of((col ^ k) * 64, 64), 64)

    mine[...] = part[rows(0), :]
    out1[...] = part[rows(1), :].astype(bf16)
    out2[...] = part[rows(2), :].astype(bf16)
    out3[...] = part[rows(3), :].astype(bf16)


def hidden_body(at, m1, r11, r12, r13, m2, r21, r22, r23, heads, rew, slope, hidden, packet, vals):
    y_hi = at[2]
    vals[...] = jnp.zeros_like(vals)
    for half, (m, r1, r2, r3) in enumerate(((m1, r11, r12, r13), (m2, r21, r22, r23))):
        rows = slice(64 * half, 64 * half + 64)
        for q in range(4):
            cols = slice(512 * q, 512 * q + 512)
            pre = (m[:, cols] + r1[:, cols].astype(f32)) + (
                r2[:, cols].astype(f32) + r3[:, cols].astype(f32)
            )
            sig = jax.nn.sigmoid(pre)
            hid = pre * sig
            v = heads[q : q + 1, :]
            vals[rows, q : q + 1] = jnp.sum(hid * v, axis=1, keepdims=True)
            if q < 2:
                hidden[rows, cols] = hid
                slope[rows, cols] = (v * (sig * (1.0 + pre * (1.0 - sig)))).astype(bf16)
    turned = vals[...].T[0:8, :]
    swapped = jnp.concatenate([turned[:, 64:128], turned[:, 0:64]], axis=1)
    turned = jnp.where(y_hi == 1, swapped, turned)
    line = lax.broadcasted_iota(jnp.int32, (8, 128), 0)
    turned = jnp.where(line < 4, turned, rew[...])
    for i in range(16):
        packet[i] = turned


def grads_body(
    at, s0, s1, s2, s3, got, left1, left2, hidden, p,
    out, keep, give, terr,
    delta, slope0, grad, errs,
):
    core, col, y_hi, dp = at[0], at[1], at[2], at[3]
    for c in range(4):
        v = (got[c] + got[4 + c]) + (got[8 + c] + got[12 + c])
        lanes = slice(64 * (c % 2), 64 * (c % 2) + 64)
        both = jnp.concatenate([got[c // 2 * 4][:, lanes], got[(2 + c // 2) * 4][:, lanes]], axis=1)
        goal = both[4:5] + both[5:6] * jnp.minimum(v[2:3], v[3:4])
        e = v[0:2] - goal
        e = jnp.where(y_hi == 1, jnp.concatenate([e[:, 64:128], e[:, 0:64]], axis=1), e)
        errs[c, 0:2, :] = e
    lo = jnp.concatenate([errs[0, 0:2, 0:64], errs[1, 0:2, 0:64]], axis=1)
    hi = jnp.concatenate([errs[2, 0:2, 0:64], errs[3, 0:2, 0:64]], axis=1)
    terr[...] = jnp.where(core == 1, hi, lo)
    for k, s in enumerate((s0, s1, s2, s3)):
        c = col ^ k
        block = jnp.concatenate([errs[c], jnp.zeros((120, 128), f32)], axis=0)
        e = 2.0 * block.T
        for half in range(2):
            rows = slice(64 * half, 64 * half + 64)
            to = pl.ds(pl.multiple_of(256 * half + 64 * c, 64), 64)
            slope0[to, :] = s[rows, 0:512]
            for q in range(2):
                cols = slice(512 * q, 512 * q + 512)
                delta[q, to, :] = (e[rows, q : q + 1] * s[rows, cols].astype(f32)).astype(bf16)
        if k == 0:
            heads = [
                jnp.sum(e[:, q : q + 1] * hidden[:, 512 * q : 512 * q + 512], axis=0, keepdims=True)
                for q in range(2)
            ]
    for q in range(2):
        grad[q] = dot(left1[q], delta[q, 0:256]) + dot(left2[q], delta[q, 256:512])
    tail = jnp.concatenate([*heads, jnp.zeros((14, 512), f32)], axis=0).astype(bf16)
    for d in range(8):
        wide = slice(64 * d, 64 * d + 64)
        thin = slice(512 + 16 * d, 528 + 16 * d)
        out[d, 0:64, :] = grad[0, wide, :].astype(bf16)
        out[d, 64:128, :] = grad[1, wide, :].astype(bf16)
        out[d, 128:144, :] = grad[0, thin, :].astype(bf16)
        out[d, 144:160, :] = grad[1, thin, :].astype(bf16)
        out[d, 160:176, :] = tail
    push = dot(slope0[...], p[...])
    first, second = push[0:128], push[128:256]
    keep[0] = jnp.where(core == 1, second, first)
    give[0] = jnp.where(core == 1, first, second)
    first, second = push[256:384], push[384:512]
    keep[1] = jnp.where(core == 1, second, first)
    give[1] = jnp.where(core == 1, first, second)


def total_body(got, w, chunk0, chunk1, act, head):
    def at(rows):
        x = [got[d, rows, :].astype(f32) for d in range(8)]
        return ((x[0] + x[1]) + (x[2] + x[3])) + ((x[4] + x[5]) + (x[6] + x[7]))

    total = at(slice(0, 64)).astype(bf16)
    for d in range(8):
        chunk0[d] = total
    chunk1[...] = at(slice(64, 128)).astype(bf16)
    head[...] = at(slice(160, 168))
    for q in range(2):
        m = at(slice(128 + 16 * q, 144 + 16 * q)).astype(bf16)
        act[16 * q : 16 * q + 16, :] = lax.dot_general(
            m, w[q], (((1,), (1,)), ((), ())), preferred_element_type=f32
        )


def second_body(chunk1, act1, act2, out):
    act = (act1[...] + act2[...]).astype(bf16)
    for d in range(8):
        out[d, 0:64, :] = chunk1[...]
        out[d, 64:96, :] = act


def renew(q, g, cin, tin, fresh, blended, c, t, isems, osems):
    ins, outs = [], []
    for h in range(2):
        rows = slice(256 * h, 256 * h + 256)
        ins.append(pltpu.make_async_copy(cin.at[q, rows], c.at[rows], isems.at[0, h]))
        ins.append(pltpu.make_async_copy(tin.at[q, rows], t.at[rows], isems.at[1, h]))
        outs.append(pltpu.make_async_copy(c.at[rows], fresh.at[q, rows], osems.at[0, h]))
        outs.append(pltpu.make_async_copy(t.at[rows], blended.at[q, rows], osems.at[1, h]))

    def work(h):
        for d in range(4 * h, 4 * h + 4):
            at = slice(64 * d, 64 * d + 64)
            new = c[at, :] - matrix_rate * g[d, 0:64, :].astype(f32)
            c[at, :] = new
            t[at, :] = blend_rate * new + (1.0 - blend_rate) * t[at, :]

    return ins, outs, work


def update0_body(g, cin, tin, fresh, blended, c, t, isems, osems):
    ins, outs, work = renew(0, g, cin, tin, fresh, blended, c, t, isems, osems)
    for copy in ins:
        copy.start()
    for h in range(2):
        ins[2 * h].wait()
        ins[2 * h + 1].wait()
        work(h)
        outs[2 * h].start()
        outs[2 * h + 1].start()
    for copy in outs:
        copy.wait()


def update1_body(
    g, cin, tin, cact, tact, fresh0, blended0, fresh, blended, fresh_act, blended_act,
    c, t, ca, ta, isems, osems, asems,
):
    ins, outs, work = renew(1, g, cin, tin, fresh, blended, c, t, isems, osems)
    more = [
        pltpu.make_async_copy(cact, ca, asems.at[0]),
        pltpu.make_async_copy(tact, ta, asems.at[1]),
    ]
    last = [
        pltpu.make_async_copy(ca, fresh_act, asems.at[2]),
        pltpu.make_async_copy(ta, blended_act, asems.at[3]),
    ]
    for copy in ins + more:
        copy.start()
    for h in range(2):
        ins[2 * h].wait()
        ins[2 * h + 1].wait()
        work(h)
        outs[2 * h].start()
        outs[2 * h + 1].start()
    for copy in more:
        copy.wait()
    for d in range(8):
        for q in range(2):
            rows = slice(16 * d, 16 * d + 16)
            term = g[d, 64 + 16 * q : 80 + 16 * q, :].astype(f32)
            new = ca[q, rows, :] - matrix_rate * term
            ca[q, rows, :] = new
            ta[q, rows, :] = blend_rate * new + (1.0 - blend_rate) * ta[q, rows, :]
    for copy in last:
        copy.start()
    for copy in outs + last:
        copy.wait()


def on_device(
    observed,
    next_observed,
    actions,
    next_mean,
    policy_noise,
    rewards,
    discounts,
    actor_flags,
    critic_in,
    critic_act,
    critic_head,
    target_in,
    target_act,
    target_head,
):
    row, col, dp = lax.axis_index("row"), lax.axis_index("col"), lax.axis_index("dp")
    at = jnp.stack([row % 2, col, row // 2, dp]).astype(jnp.int32)

    (own,) = call(
        pack_body,
        [shape(128, 1280)],
        [observed, next_observed, actions, next_mean, policy_noise],
        scratch=[pltpu.VMEM((128, 128), bf16), pltpu.VMEM((128, 128), f32), DMA((5,))],
        mib=4, raw=range(5), name="pack",
    )
    sib = swap(own, "row", 1)
    far = swap(own, "row", 2)
    w16, a16, p16 = call(
        weights_body,
        [shape(4, 512, 512), shape(4, 128, 512), shape(512, 128)],
        [critic_in, target_in, critic_act, target_act],
        scratch=[pltpu.VMEM((4, 512, 512), f32), pltpu.VMEM((4, 128, 512), f32), DMA((8,))],
        mib=16, flops=2 * 128 * 512 * 512, raw=range(4), to=(2,), name="weights",
    )

    def forward(x0, x1, name):
        return call(
            forward_body,
            [
                shape(64, 2048, dtype=f32), shape(64, 2048), shape(64, 2048), shape(64, 2048),
                shape(2, 640, 256),
            ],
            [x0, x1, a16, w16],
            scratch=[pltpu.VMEM((256, 1280), bf16), pltpu.VMEM((256, 2048), f32)],
            scalars=at, flops=8 * 256 * 640 * 512, to=range(5), name=name,
        )

    mine1, *out1, left1 = forward(own, sib, "forward_near")
    in1 = [None, None, None]
    for k in (2, 1, 3):
        in1[k - 1] = swap(out1[k - 1], "col", k)
    far = after(far, mine1)
    farsib = swap(far, "row", 1)
    mine2, *out2, left2 = forward(far, farsib, "forward_far")
    in2 = [None, None, None]
    for k in (2, 1, 3):
        in2[k - 1] = swap(out2[k - 1], "col", k)
    heads = jnp.concatenate([critic_head, target_head, jnp.zeros((4, 512), f32)], axis=0)
    blank = jnp.zeros((1, 128), f32)
    rew = jnp.concatenate(
        [blank, blank, blank, blank, rewards.astype(f32)[None], discounts.astype(f32)[None], blank, blank]
    )
    slope, hidden, packet = call(
        hidden_body,
        [shape(128, 1024), shape(128, 1024, dtype=f32), shape(16, 8, 128, dtype=f32)],
        [mine1, *in1, mine2, *in2, heads, rew],
        scratch=[pltpu.VMEM((128, 128), f32)],
        scalars=at, where=(0, 4), to=range(3), name="hidden", flops=128 * 2048 * 30,
    )
    slopes = [slope] + [swap(slope, "col", k) for k in (1, 2, 3)]
    got = lax.all_to_all(packet, ("row", "col"), 0, 0, tiled=True)
    grads, keep, give, temporal_errors = call(
        grads_body,
        [
            shape(8, 176, 512), shape(2, 128, 128, dtype=f32),
            shape(2, 128, 128, dtype=f32), shape(2, 128, dtype=f32),
        ],
        [*slopes, got, left1, left2, hidden, p16],
        scratch=[
            pltpu.VMEM((2, 512, 512), bf16), pltpu.VMEM((512, 512), bf16),
            pltpu.VMEM((2, 640, 512), f32), pltpu.VMEM((4, 8, 128), f32),
        ],
        scalars=at, where=(0, 5, 6, 7, 8), to=range(4), name="grads", flops=4 * 640 * 512 * 512,
    )
    parts = lax.all_to_all(grads, "dp", 0, 0, tiled=True)
    push = keep + swap(give, "row", 1)
    push = push[0] + swap(push[1], "row", 2)

    chunk0, chunk1, act, head = call(
        total_body,
        [shape(8, 64, 512), shape(64, 512), shape(32, 512, dtype=f32), shape(8, 512, dtype=f32)],
        [parts, w16], to=range(4), name="total", flops=4 * 16 * 512 * 512,
    )
    grad0 = lax.all_to_all(chunk0, "dp", 0, 0, tiled=True)
    act = act + swap(act, "row", 1)
    (chunk1,) = call(
        second_body, [shape(8, 96, 512)], [chunk1, act, swap(act, "row", 2)],
        where=(0,), to=(0,), name="second",
    )
    grad1 = lax.all_to_all(chunk1, "dp", 0, 0, tiled=True)
    both = jnp.concatenate([push, head[0:2].reshape(8, 128)], axis=0)
    both = both + swap(both, "col", 1)
    both = both + swap(both, "col", 2)
    action_slope = actor_flags.astype(f32)[:, None] * both[0:128]
    head = both[128:136].reshape(2, 512)
    wide, thin = shape(2, 512, 512, dtype=f32), shape(2, 128, 512, dtype=f32)
    big, small = pltpu.VMEM((512, 512), f32), pltpu.VMEM((2, 128, 512), f32)
    new_in, new_target_in = call(
        update0_body, [wide, wide], [grad0, critic_in, target_in],
        scratch=[big, big, DMA((2, 2)), DMA((2, 2))],
        raw=(1, 2), to="raw", mib=8, name="update_first",
    )
    new_in, new_target_in, new_act, new_target_act = call(
        update1_body, [wide, wide, thin, thin],
        [grad1, critic_in, target_in, critic_act, target_act, new_in, new_target_in],
        scratch=[big, big, small, small, DMA((2, 2)), DMA((2, 2)), DMA((4,))],
        raw=range(1, 7), to="raw", mib=8, aliases={5: 0, 6: 1}, name="update_second",
    )
    new_head = critic_head - head_rate * head
    new_target_head = blend_rate * new_head + (1.0 - blend_rate) * target_head
    return (
        new_in,
        new_act,
        new_head,
        new_target_in,
        new_target_act,
        new_target_head,
        temporal_errors,
        action_slope,
    )


def solution(mesh):
    return jax.shard_map(
        on_device,
        mesh=mesh,
        in_specs=(
            P(("row", "dp"), "col"),
            P(("row", "dp"), "col"),
            P(("row", "dp"), None),
            P(("row", "dp"), None),
            P(("row", "dp"), None),
            P(("row", "dp")),
            P(("row", "dp")),
            P(("row", "dp")),
            P(None, "col", "row"),
            P(None, None, "col"),
            P(None, "row"),
            P(None, "col", "row"),
            P(None, None, "col"),
            P(None, "row"),
        ),
        out_specs=(
            P(None, "col", "row"),
            P(None, None, "col"),
            P(None, "row"),
            P(None, "col", "row"),
            P(None, None, "col"),
            P(None, "row"),
            P(None, ("row", "dp")),
            P(("row", "dp"), None),
        ),
        check_vma=False,
    )
```

time: 145 us -> 137 us (0.945)
  starting transfers between devices: 63.2 us -> 40.9 us
  local copies, waits for them, and re-layouts: 20.9 us -> 2.63 us
  Pallas kernels: 13.6 us -> 27 us
  blocking collectives: 0 us -> 12.3 us
  waiting for transfers between devices: 42.6 us -> 46 us
  other arithmetic: 2.83 us -> 5.67 us
    ppermute x34 -> x18, starting transfers between devices: 55.3 us -> 26.7 us  [swap(): return lax.ppermute(x, axis, [(i, i ^ bit) for i in range(n)])]
    unnamed x56 -> x14, local copies, waits for them, and re-layouts: 20 us -> 1.71 us
    pallas_call x9 -> x11, Pallas kernels: 13.6 us -> 27 us  [the longest x10 27 us: call(): pl.pallas_call(body, out_shape=tuple((HBM(o.shape, o.dtype) if i in to el...]
    all_to_all x0 -> x1, blocking collectives: none -> 12.3 us  [on_device(): got = lax.all_to_all(packet, ('row', 'col'), 0, 0, tiled=True)]
    all_to_all x2 -> x3, waiting for transfers between devices: 4.54 us -> 11.5 us  [the longest x1 8.84 us: on_device(): grad1 = lax.all_to_all(chunk1, 'dp', 0, 0, tiled=True)]
    all_to_all x2 -> x3, starting transfers between devices: 7.99 us -> 14.3 us  [the longest x1 6 us: on_device(): grad0 = lax.all_to_all(chunk0, 'dp', 0, 0, tiled=True)]
    ppermute x34 -> x18, waiting for transfers between devices: 38 us -> 34.5 us  [swap(): return lax.ppermute(x, axis, [(i, i ^ bit) for i in range(n)])]
  transfers between devices with their start and end apart: 36 -> 21, of which waited for: 13 -> 11; matrix products, arithmetic and copies ran while one was open for 2% -> 4% of each run, Pallas kernels for 6% -> 11%
where the time goes in v2:
time: 137 us; the launch traced here: 135 us
  waiting for transfers between devices  46 us (34%)
  starting transfers between devices  40.9 us (30%)
  Pallas kernels  27 us (20%)
  blocking collectives  12.3 us (9%)
  other arithmetic  5.67 us (4%)
  local copies, waits for them, and re-layouts  2.63 us (2%)
    ppermute x18, waiting for transfers between devices, swap(): return lax.ppermute(x, axis, [(i, i ^ bit) for i in range(n)])  34.5 us
    pallas_call x10, Pallas kernels, call(): pl.pallas_call(body, out_shape=tuple((HBM(o.shape, o.dtype) if i in to el...  27 us
    ppermute x18, starting transfers between devices, swap(): return lax.ppermute(x, axis, [(i, i ^ bit) for i in range(n)])  26.7 us
    all_to_all x1, blocking collectives, on_device(): got = lax.all_to_all(packet, ('row', 'col'), 0, 0, tiled=True)  12.3 us
    all_to_all x1, waiting for transfers between devices, on_device(): grad1 = lax.all_to_all(chunk1, 'dp', 0, 0, tiled=True)  8.84 us
    all_to_all x1, starting transfers between devices, on_device(): grad0 = lax.all_to_all(chunk0, 'dp', 0, 0, tiled=True)  6 us
    all_to_all x1, starting transfers between devices, on_device(): parts = lax.all_to_all(grads, 'dp', 0, 0, tiled=True)  4.56 us
    all_to_all x1, starting transfers between devices, on_device(): grad1 = lax.all_to_all(chunk1, 'dp', 0, 0, tiled=True)  3.69 us
  transfers between devices with their start and end apart: 21, of which 11 were waited for; matrix products, arithmetic and copies ran while one was open for 4% of the time, Pallas kernels for 11%

profile of v2, /device:TPU:0, one launch (start us, length us, event | category | flops | bytes accessed | tf_op | source)
XLA Modules:
  0.0 135.2 jit_solution(10543905431786444149)
XLA Ops:
  0.6 1.1 pack.1.x0
  1.7 0.1 collective-permute-start
  1.8 3.4 %collective-permute-start.4 = (bf16[128,1280]{1,0:T(8,128)(2,1)S(1)}, bf16[128,1280]{1,0:T(8,128)(2,1)S(1)}, u32[]{:S(2)}, u32[]{:S(2)}) collective-permute-start(bf16[128,1280]{1,0:T(8,128)(2,1)S(1)} %pack.1.x0), channel_id=1, source_target_pairs={{0,64},{32,96},{64,0},{96,32},{1,65},{33,97},{65,1},{97,33},{2,66}... | collective-permute-start | bytes 983048 | tf_op jit(solution)/shard_map/ppermute | solution.py:72
  5.2 0.1 pad.5.clone
  5.2 3.2 %weights.1 = (bf16[4,512,512]{2,1,0:T(8,128)(2,1)S(1)}, bf16[4,128,512]{2,1,0:T(8,128)(2,1)S(1)}, bf16[512,128]{1,0:T(8,128)(2,1)}) custom-call(f32[2,512,512]{2,1,0:T(8,128)} %cin.5, f32[2,512,512]{2,1,0:T(8,128)} %tin.5, f32[2,128,512]{2,1,0:T(8,128)} %cact.3, f32[2,128,512]{2,1,0:T(8,128)} %tact.3), custom_call_target="tpu_custom_call" | custom-call | flops 67108864 | bytes 7995392 | tf_op jit(solution)/shard_map/weights/pallas_call | solution.py:38
  8.5 0.1 pad_add_fusion.at
  8.5 0.0 collective-permute-done.x1
  8.5 3.6 %forward_near.1 = (f32[64,2048]{1,0:T(8,128)}, bf16[64,2048]{1,0:T(8,128)(2,1)}, bf16[64,2048]{1,0:T(8,128)(2,1)}, bf16[64,2048]{1,0:T(8,128)(2,1)}, bf16[2,640,256]{2,1,0:T(8,128)(2,1)}) custom-call(s32[4]{0:T(128)S(1)} %pad_add_fusion.at, bf16[128,1280]{1,0:T(8,128)(2,1)S(1)} %pack.1.x0, bf16[128,1280]{1,0:T(8,128)(2,1)} %collective-permute-done.x1, ...), custom_call_target="tpu_custom_call" | custom-call | flops 671088640 | bytes 5242880 | tf_op jit(solution)/shard_map/forward_near/pallas_call | solution.py:38
  12.2 1.3 collective-permute-done.4.x
  13.5 0.7 copy-done
  14.2 0.1 fusion.2
  14.3 2.0 %collective-permute-start.1 = (bf16[64,2048]{1,0:T(8,128)(2,1)}, bf16[64,2048]{1,0:T(8,128)(2,1)S(1)}, u32[]{:S(2)}, u32[]{:S(2)}) collective-permute-start(bf16[64,2048]{1,0:T(8,128)(2,1)} %get-tuple-element.41), channel_id=1, source_target_pairs={{0,8},{8,0},{16,24},{24,16},{1,9},{9,1},{17,25},{25,17},{2,10},{10... | collective-permute-start | bytes 786440 | tf_op jit(solution)/shard_map/ppermute | solution.py:72
  16.3 3.7 %collective-permute-start.2 = (bf16[64,2048]{1,0:T(8,128)(2,1)}, bf16[64,2048]{1,0:T(8,128)(2,1)S(1)}, u32[]{:S(2)}, u32[]{:S(2)}) collective-permute-start(bf16[64,2048]{1,0:T(8,128)(2,1)} %get-tuple-element.42), channel_id=1, source_target_pairs={{0,16},{8,24},{16,0},{24,8},{1,17},{9,25},{17,1},{25,9},{2,18},{10... | collective-permute-start | bytes 786440 | tf_op jit(solution)/shard_map/ppermute | solution.py:72
  20.0 0.0 collective-permute-start.3
  20.0 0.0 collective-permute-done.5.x1
  20.0 1.0 copy-done.1
  20.9 3.2 %forward_far.1 = (f32[64,2048]{1,0:T(8,128)}, bf16[64,2048]{1,0:T(8,128)(2,1)}, bf16[64,2048]{1,0:T(8,128)(2,1)}, bf16[64,2048]{1,0:T(8,128)(2,1)}, bf16[2,640,256]{2,1,0:T(8,128)(2,1)}) custom-call(s32[4]{0:T(128)S(1)} %pad_add_fusion.at, bf16[128,1280]{1,0:T(8,128)(2,1)S(1)} %copy-done.1, bf16[128,1280]{1,0:T(8,128)(2,1)S(1)} %collective-permute-done.5.x1, ...), custom_call_target="tpu_custom_call" | custom-call | flops 671088640 | bytes 5242880 | tf_op jit(solution)/shard_map/forward_far/pallas_call | solution.py:38
  24.1 0.0 collective-permute-start.6
  24.2 4.6 %collective-permute-start.7 = (bf16[64,2048]{1,0:T(8,128)(2,1)}, bf16[64,2048]{1,0:T(8,128)(2,1)S(1)}, u32[]{:S(2)}, u32[]{:S(2)}) collective-permute-start(bf16[64,2048]{1,0:T(8,128)(2,1)} %get-tuple-element.46), channel_id=1, source_target_pairs={{0,16},{8,24},{16,0},{24,8},{1,17},{9,25},{17,1},{25,9},{2,18},{10... | collective-permute-start | bytes 786440 | tf_op jit(solution)/shard_map/ppermute | solution.py:72
  28.8 0.0 collective-permute-done.1.r11
  28.8 0.0 collective-permute-start.8
  28.8 0.1 maximum_maximum_fusion.1.rew
  28.9 0.1 maximum_maximum_fusion.heads
  29.0 3.9 %collective-permute-done.2.r12 = bf16[64,2048]{1,0:T(8,128)(2,1)S(1)} collective-permute-done((bf16[64,2048]{1,0:T(8,128)(2,1)}, bf16[64,2048]{1,0:T(8,128)(2,1)S(1)}, u32[]{:S(2)}, u32[]{:S(2)}) %collective-permute-start.2) | collective-permute-done | bytes 262176 | tf_op jit(solution)/shard_map/ppermute | solution.py:72
  32.8 3.4 %collective-permute-done.3.r13 = bf16[64,2048]{1,0:T(8,128)(2,1)S(1)} collective-permute-done((bf16[64,2048]{1,0:T(8,128)(2,1)}, bf16[64,2048]{1,0:T(8,128)(2,1)S(1)}, u32[]{:S(2)}, u32[]{:S(2)}) %collective-permute-start.3) | collective-permute-done | bytes 262176 | tf_op jit(solution)/shard_map/ppermute | solution.py:72
  36.2 0.0 collective-permute-done.6.r21
  36.2 7.6 %collective-permute-done.7.r22 = bf16[64,2048]{1,0:T(8,128)(2,1)S(1)} collective-permute-done((bf16[64,2048]{1,0:T(8,128)(2,1)}, bf16[64,2048]{1,0:T(8,128)(2,1)S(1)}, u32[]{:S(2)}, u32[]{:S(2)}) %collective-permute-start.7) | collective-permute-done | bytes 262176 | tf_op jit(solution)/shard_map/ppermute | solution.py:72
  43.8 2.6 %collective-permute-done.8.r23 = bf16[64,2048]{1,0:T(8,128)(2,1)S(1)} collective-permute-done((bf16[64,2048]{1,0:T(8,128)(2,1)}, bf16[64,2048]{1,0:T(8,128)(2,1)S(1)}, u32[]{:S(2)}, u32[]{:S(2)}) %collective-permute-start.8) | collective-permute-done | bytes 262176 | tf_op jit(solution)/shard_map/ppermute | solution.py:72
  46.4 2.6 %hidden.1 = (bf16[128,1024]{1,0:T(8,128)(2,1)}, f32[128,1024]{1,0:T(8,128)}, f32[16,8,128]{2,1,0:T(8,128)}) custom-call(s32[4]{0:T(128)S(1)} %pad_add_fusion.at, f32[64,2048]{1,0:T(8,128)} %get-tuple-element.40.other.m1, bf16[64,2048]{1,0:T(8,128)(2,1)S(1)} %collective-permute-done.1.r11, bf16[64,2048]{1,0:T(8,128)(2,1)S(1)} %collective-permute-done.2.r12, ...), custom_call_target="tpu_custom_call" | custom-call | flops 7864320 | bytes 3493888 | tf_op jit(solution)/shard_map/hidden/pallas_call | solution.py:38
  49.0 0.3 collective-permute-start.11
  49.3 0.4 collective-permute-start.10
  49.6 3.4 %collective-permute-start.9 = (bf16[128,1024]{1,0:T(8,128)(2,1)}, bf16[128,1024]{1,0:T(8,128)(2,1)S(1)}, u32[]{:S(2)}, u32[]{:S(2)}) collective-permute-start(bf16[128,1024]{1,0:T(8,128)(2,1)} %get-tuple-element.48.s0), channel_id=1, source_target_pairs={{0,8},{8,0},{16,24},{24,16},{1,9},{9,1},{17,25},{25,17},{2,10},{10... | collective-permute-start | bytes 786440 | tf_op jit(solution)/shard_map/ppermute | solution.py:72
  53.1 12.3 %all_to_all.20.got = f32[16,8,128]{2,1,0:T(8,128)S(1)} all-to-all(f32[16,8,128]{2,1,0:T(8,128)} %get-tuple-element.49), channel_id=1, replica_groups=mesh['row'=4,'col'=4,'dp'=8] {'row','col'}, dimensions={0} | all-to-all | bytes 131072 | tf_op jit(solution)/shard_map/all_to_all | solution.py:384
  65.3 0.0 collective-permute-done.10.s2
  65.3 0.0 collective-permute-done.9.s1
  65.3 4.3 %grads.1 = (bf16[8,176,512]{2,1,0:T(8,128)(2,1)}, f32[2,128,128]{2,1,0:T(8,128)}, f32[2,128,128]{2,1,0:T(8,128)}, f32[2,128]{1,0:T(2,128)}) custom-call(s32[4]{0:T(128)S(1)} %pad_add_fusion.at, bf16[128,1024]{1,0:T(8,128)(2,1)} %get-tuple-element.48.s0, bf16[128,1024]{1,0:T(8,128)(2,1)S(1)} %collective-permute-done.9.s1, ...), custom_call_target="tpu_custom_call" | custom-call | flops 671088640 | bytes 4785152 | tf_op jit(solution)/shard_map/grads/pallas_call | solution.py:38
  69.7 4.6 %all-to-all-start.1 = ((bf16[8,176,512]{2,1,0:T(8,128)(2,1)}), bf16[8,176,512]{2,1,0:T(8,128)(2,1)S(1)}, u32[]{:S(2)}, u32[]{:S(2)}) async-start(bf16[8,176,512]{2,1,0:T(8,128)(2,1)} %get-tuple-element.54), calls=%async_computation.1 | async-start | bytes 2883584 | tf_op jit(solution)/shard_map/all_to_all | solution.py:398
  74.2 1.6 %collective-permute-done.14 = f32[2,128,128]{2,1,0:T(8,128)S(1)} collective-permute-done((f32[2,128,128]{2,1,0:T(8,128)}, f32[2,128,128]{2,1,0:T(8,128)S(1)}, u32[]{:S(2)}, u32[]{:S(2)}) %collective-permute-start.14) | collective-permute-done | bytes 131104 | tf_op jit(solution)/shard_map/ppermute | solution.py:72
  75.8 0.9 add.25
  76.7 3.0 %collective-permute-start.15 = (f32[128,128]{1,0:T(8,128)S(1)}, f32[128,128]{1,0:T(8,128)S(1)}, u32[]{:S(2)}, u32[]{:S(2)}) collective-permute-start(f32[128,128]{1,0:T(8,128)S(1)} %slice_bitcast_fusion), channel_id=1, source_target_pairs={{0,64},{32,96},{64,0},{96,32},{1,65},{33,97},{65,1},{97,33},{2,66}... | collective-permute-start | bytes 196616 | tf_op jit(solution)/shard_map/ppermute | solution.py:72
  79.7 11.3 %collective-permute-done.15 = f32[128,128]{1,0:T(8,128)S(1)} collective-permute-done((f32[128,128]{1,0:T(8,128)S(1)}, f32[128,128]{1,0:T(8,128)S(1)}, u32[]{:S(2)}, u32[]{:S(2)}) %collective-permute-start.15) | collective-permute-done | bytes 65568 | tf_op jit(solution)/shard_map/ppermute | solution.py:72
  91.0 0.6 fusion
  91.6 2.7 %all-to-all-done.1.got = bf16[8,176,512]{2,1,0:T(8,128)(2,1)S(1)} async-done(((bf16[8,176,512]{2,1,0:T(8,128)(2,1)}), bf16[8,176,512]{2,1,0:T(8,128)(2,1)S(1)}, u32[]{:S(2)}, u32[]{:S(2)}) %all-to-all-start.1) | async-done | bytes 1441824 | tf_op jit(solution)/shard_map/all_to_all | solution.py:398
  94.3 1.3 total.1
  95.6 0.7 slice.17
  96.3 6.0 %all-to-all-start.3 = ((bf16[8,64,512]{2,1,0:T(8,128)(2,1)}), bf16[8,64,512]{2,1,0:T(8,128)(2,1)S(1)}, u32[]{:S(2)}, u32[]{:S(2)}) async-start(bf16[8,64,512]{2,1,0:T(8,128)(2,1)} %get-tuple-element.57), calls=%async_computation.3 | async-start | bytes 1048576 | tf_op jit(solution)/shard_map/all_to_all | solution.py:407
  102.3 0.8 pad_maximum_fusion
  103.2 0.3 collective-permute-start.16
  103.4 1.5 %collective-permute-done.12 = f32[32,512]{1,0:T(8,128)S(1)} collective-permute-done((f32[32,512]{1,0:T(8,128)}, f32[32,512]{1,0:T(8,128)S(1)}, u32[]{:S(2)}, u32[]{:S(2)}) %collective-permute-start.12) | collective-permute-done | bytes 65568 | tf_op jit(solution)/shard_map/ppermute | solution.py:72
  104.9 0.9 add.24.act1
  105.8 2.1 %collective-permute-start.13 = (f32[32,512]{1,0:T(8,128)S(1)}, f32[32,512]{1,0:T(8,128)S(1)}, u32[]{:S(2)}, u32[]{:S(2)}) collective-permute-start(f32[32,512]{1,0:T(8,128)S(1)} %add.24.act1), channel_id=1, source_target_pairs={{0,64},{32,96},{64,0},{96,32},{1,65},{33,97},{65,1},{97,33},{2,66}... | collective-permute-start | bytes 196616 | tf_op jit(solution)/shard_map/ppermute | solution.py:72
  107.9 0.0 collective-permute-done.16
  107.9 0.8 fusion.1
  108.7 3.4 %collective-permute-start.17 = (f32[136,128]{1,0:T(8,128)S(1)}, f32[136,128]{1,0:T(8,128)S(1)}, u32[]{:S(2)}, u32[]{:S(2)}) collective-permute-start(f32[136,128]{1,0:T(8,128)S(1)} %fusion.1), channel_id=1, source_target_pairs={{0,16},{8,24},{16,0},{24,8},{1,17},{9,25},{17,1},{25,9},{2,18},{10... | collective-permute-start | bytes 208904 | tf_op jit(solution)/shard_map/ppermute | solution.py:72
  112.1 1.5 %collective-permute-done.13.act2 = f32[32,512]{1,0:T(8,128)S(1)} collective-permute-done((f32[32,512]{1,0:T(8,128)S(1)}, f32[32,512]{1,0:T(8,128)S(1)}, u32[]{:S(2)}, u32[]{:S(2)}) %collective-permute-start.13) | collective-permute-done | bytes 65568 | tf_op jit(solution)/shard_map/ppermute | solution.py:72
  113.6 1.8 %second.1 = bf16[8,96,512]{2,1,0:T(8,128)(2,1)} custom-call(bf16[64,512]{1,0:T(8,128)(2,1)} %get-tuple-element.55.chunk1, f32[32,512]{1,0:T(8,128)S(1)} %add.24.act1, f32[32,512]{1,0:T(8,128)S(1)} %collective-permute-done.13.act2), custom_call_target="tpu_custom_call" | custom-call | bytes 983040 | tf_op jit(solution)/shard_map/second/pallas_call | solution.py:38
  115.4 0.0 all-to-all-done.3.g
  115.4 3.7 %all-to-all-start.2 = ((bf16[8,96,512]{2,1,0:T(8,128)(2,1)}), bf16[8,96,512]{2,1,0:T(8,128)(2,1)S(1)}, u32[]{:S(2)}, u32[]{:S(2)}) async-start(bf16[8,96,512]{2,1,0:T(8,128)(2,1)} %second.1), calls=%async_computation.2 | async-start | bytes 1572864 | tf_op jit(solution)/shard_map/all_to_all | solution.py:413
  119.1 0.0 collective-permute-done.17
  119.2 0.6 multiply_add_fusion
  119.8 0.7 slice_multiply_fusion
  120.5 2.7 %update_first.1 = (f32[2,512,512]{2,1,0:T(8,128)}, f32[2,512,512]{2,1,0:T(8,128)}) custom-call(bf16[8,64,512]{2,1,0:T(8,128)(2,1)S(1)} %all-to-all-done.3.g, f32[2,512,512]{2,1,0:T(8,128)} %cin.5, f32[2,512,512]{2,1,0:T(8,128)} %tin.5), custom_call_target="tpu_custom_call" | custom-call | bytes 8912896 | tf_op jit(solution)/shard_map/update_first/pallas_call | solution.py:38
  123.2 8.8 %all-to-all-done.2.g = bf16[8,96,512]{2,1,0:T(8,128)(2,1)S(1)} async-done(((bf16[8,96,512]{2,1,0:T(8,128)(2,1)}), bf16[8,96,512]{2,1,0:T(8,128)(2,1)S(1)}, u32[]{:S(2)}, u32[]{:S(2)}) %all-to-all-start.2) | async-done | bytes 786464 | tf_op jit(solution)/shard_map/all_to_all | solution.py:413
  132.0 3.2 %update_second.1 = (f32[2,512,512]{2,1,0:T(8,128)}, f32[2,512,512]{2,1,0:T(8,128)}, f32[2,128,512]{2,1,0:T(8,128)}, f32[2,128,512]{2,1,0:T(8,128)}) custom-call(bf16[8,96,512]{2,1,0:T(8,128)(2,1)S(1)} %all-to-all-done.2.g, f32[2,512,512]{2,1,0:T(8,128)} %cin.5, f32[2,512,512]{2,1,0:T(8,128)} %tin.5, ...), custom_call_target="tpu_custom_call", output_to_operand_aliasing={{0}: (5, {}), {1}: (6, {})} | custom-call | bytes 15466496 | tf_op jit(solution)/shard_map/update_second/pallas_call | solution.py:38
  (26 shorter events, 0.1 us)
Async XLA Ops:
  1.7 6.8 %collective-permute-start = (bf16[128,1280]{1,0:T(8,128)(2,1)S(1)}, bf16[128,1280]{1,0:T(8,128)(2,1)}, u32[]{:S(2)}, u32[]{:S(2)}) collective-permute-start(bf16[128,1280]{1,0:T(8,128)(2,1)S(1)} %pack.1.x0), channel_id=1, source_target_pairs={{0,32},{32,0},{64,96},{96,64},{1,33},{33,1},{65,97},{97,65},{2,34}... | collective-permute-start | bytes 983048 | tf_op jit(solution)/shard_map/ppermute | solution.py:72
  1.8 11.6 %collective-permute-start.4 = (bf16[128,1280]{1,0:T(8,128)(2,1)S(1)}, bf16[128,1280]{1,0:T(8,128)(2,1)S(1)}, u32[]{:S(2)}, u32[]{:S(2)}) collective-permute-start(bf16[128,1280]{1,0:T(8,128)(2,1)S(1)} %pack.1.x0), channel_id=1, source_target_pairs={{0,64},{32,96},{64,0},{96,32},{1,65},{33,97},{65,1},{97,33},{2,66}... | collective-permute-start | bytes 983048 | tf_op jit(solution)/shard_map/ppermute | solution.py:72
  8.5 7.7 %copy-start.4 = (bf16[128]{0:T(256)(128)(2,1)S(1)}, bf16[128]{0:T(256)(128)(2,1)}, u32[]{:S(2)}) copy-start(bf16[128]{0:T(256)(128)(2,1)} %param.20) | copy-start | bytes 772
  8.5 7.7 %copy-start.5 = (bf16[128]{0:T(256)(128)(2,1)S(1)}, bf16[128]{0:T(256)(128)(2,1)}, u32[]{:S(2)}) copy-start(bf16[128]{0:T(256)(128)(2,1)} %param.19) | copy-start | bytes 772
  13.5 0.7 copy-start
  14.2 14.7 %copy-start.2 = (f32[2,512]{1,0:T(2,128)S(1)}, f32[2,512]{1,0:T(2,128)}, u32[]{:S(2)}) copy-start(f32[2,512]{1,0:T(2,128)} %param.27) | copy-start | bytes 12292
  14.2 14.7 %copy-start.3 = (f32[2,512]{1,0:T(2,128)S(1)}, f32[2,512]{1,0:T(2,128)}, u32[]{:S(2)}) copy-start(f32[2,512]{1,0:T(2,128)} %param.24) | copy-start | bytes 12292
  14.2 5.8 %collective-permute-start.5 = (bf16[128,1280]{1,0:T(8,128)(2,1)}, bf16[128,1280]{1,0:T(8,128)(2,1)S(1)}, u32[]{:S(2)}, u32[]{:S(2)}) collective-permute-start(bf16[128,1280]{1,0:T(8,128)(2,1)} %after.1.x0), channel_id=1, source_target_pairs={{0,32},{32,0},{64,96},{96,64},{1,33},{33,1},{65,97},{97,65},{2,34}... | collective-permute-start | bytes 983048 | tf_op jit(solution)/shard_map/ppermute | solution.py:72
  14.3 14.5 %collective-permute-start.1 = (bf16[64,2048]{1,0:T(8,128)(2,1)}, bf16[64,2048]{1,0:T(8,128)(2,1)S(1)}, u32[]{:S(2)}, u32[]{:S(2)}) collective-permute-start(bf16[64,2048]{1,0:T(8,128)(2,1)} %get-tuple-element.41), channel_id=1, source_target_pairs={{0,8},{8,0},{16,24},{24,16},{1,9},{9,1},{17,25},{25,17},{2,10},{10... | collective-permute-start | bytes 786440 | tf_op jit(solution)/shard_map/ppermute | solution.py:72
  16.3 16.5 %collective-permute-start.2 = (bf16[64,2048]{1,0:T(8,128)(2,1)}, bf16[64,2048]{1,0:T(8,128)(2,1)S(1)}, u32[]{:S(2)}, u32[]{:S(2)}) collective-permute-start(bf16[64,2048]{1,0:T(8,128)(2,1)} %get-tuple-element.42), channel_id=1, source_target_pairs={{0,16},{8,24},{16,0},{24,8},{1,17},{9,25},{17,1},{25,9},{2,18},{10... | collective-permute-start | bytes 786440 | tf_op jit(solution)/shard_map/ppermute | solution.py:72
  20.0 16.2 %collective-permute-start.3 = (bf16[64,2048]{1,0:T(8,128)(2,1)}, bf16[64,2048]{1,0:T(8,128)(2,1)S(1)}, u32[]{:S(2)}, u32[]{:S(2)}) collective-permute-start(bf16[64,2048]{1,0:T(8,128)(2,1)} %get-tuple-element.43), channel_id=1, source_target_pairs={{0,24},{8,16},{16,8},{24,0},{1,25},{9,17},{17,9},{25,1},{2,26},{10... | collective-permute-start | bytes 786440 | tf_op jit(solution)/shard_map/ppermute | solution.py:72
  20.0 1.0 copy-start.1
  24.1 12.1 %collective-permute-start.6 = (bf16[64,2048]{1,0:T(8,128)(2,1)}, bf16[64,2048]{1,0:T(8,128)(2,1)S(1)}, u32[]{:S(2)}, u32[]{:S(2)}) collective-permute-start(bf16[64,2048]{1,0:T(8,128)(2,1)} %get-tuple-element.45), channel_id=1, source_target_pairs={{0,8},{8,0},{16,24},{24,16},{1,9},{9,1},{17,25},{25,17},{2,10},{10... | collective-permute-start | bytes 786440 | tf_op jit(solution)/shard_map/ppermute | solution.py:72
  24.2 19.6 %collective-permute-start.7 = (bf16[64,2048]{1,0:T(8,128)(2,1)}, bf16[64,2048]{1,0:T(8,128)(2,1)S(1)}, u32[]{:S(2)}, u32[]{:S(2)}) collective-permute-start(bf16[64,2048]{1,0:T(8,128)(2,1)} %get-tuple-element.46), channel_id=1, source_target_pairs={{0,16},{8,24},{16,0},{24,8},{1,17},{9,25},{17,1},{25,9},{2,18},{10... | collective-permute-start | bytes 786440 | tf_op jit(solution)/shard_map/ppermute | solution.py:72
  28.8 17.6 %collective-permute-start.8 = (bf16[64,2048]{1,0:T(8,128)(2,1)}, bf16[64,2048]{1,0:T(8,128)(2,1)S(1)}, u32[]{:S(2)}, u32[]{:S(2)}) collective-permute-start(bf16[64,2048]{1,0:T(8,128)(2,1)} %get-tuple-element.47), channel_id=1, source_target_pairs={{0,24},{8,16},{16,8},{24,0},{1,25},{9,17},{17,9},{25,1},{2,26},{10... | collective-permute-start | bytes 786440 | tf_op jit(solution)/shard_map/ppermute | solution.py:72
  49.0 16.4 %collective-permute-start.11 = (bf16[128,1024]{1,0:T(8,128)(2,1)}, bf16[128,1024]{1,0:T(8,128)(2,1)S(1)}, u32[]{:S(2)}, u32[]{:S(2)}) collective-permute-start(bf16[128,1024]{1,0:T(8,128)(2,1)} %get-tuple-element.48.s0), channel_id=1, source_target_pairs={{0,24},{8,16},{16,8},{24,0},{1,25},{9,17},{17,9},{25,1},{2,26},{10... | collective-permute-start | bytes 786440 | tf_op jit(solution)/shard_map/ppermute | solution.py:72
  49.3 16.1 %collective-permute-start.10 = (bf16[128,1024]{1,0:T(8,128)(2,1)}, bf16[128,1024]{1,0:T(8,128)(2,1)S(1)}, u32[]{:S(2)}, u32[]{:S(2)}) collective-permute-start(bf16[128,1024]{1,0:T(8,128)(2,1)} %get-tuple-element.48.s0), channel_id=1, source_target_pairs={{0,16},{8,24},{16,0},{24,8},{1,17},{9,25},{17,1},{25,9},{2,18},{10... | collective-permute-start | bytes 786440 | tf_op jit(solution)/shard_map/ppermute | solution.py:72
  49.6 15.7 %collective-permute-start.9 = (bf16[128,1024]{1,0:T(8,128)(2,1)}, bf16[128,1024]{1,0:T(8,128)(2,1)S(1)}, u32[]{:S(2)}, u32[]{:S(2)}) collective-permute-start(bf16[128,1024]{1,0:T(8,128)(2,1)} %get-tuple-element.48.s0), channel_id=1, source_target_pairs={{0,8},{8,0},{16,24},{24,16},{1,9},{9,1},{17,25},{25,17},{2,10},{10... | collective-permute-start | bytes 786440 | tf_op jit(solution)/shard_map/ppermute | solution.py:72
  69.7 24.6 %all-to-all-start.1 = ((bf16[8,176,512]{2,1,0:T(8,128)(2,1)}), bf16[8,176,512]{2,1,0:T(8,128)(2,1)S(1)}, u32[]{:S(2)}, u32[]{:S(2)}) async-start(bf16[8,176,512]{2,1,0:T(8,128)(2,1)} %get-tuple-element.54), calls=%async_computation.1 | async-start | bytes 2883584 | tf_op jit(solution)/shard_map/all_to_all | solution.py:398
  74.2 1.6 %collective-permute-start.14 = (f32[2,128,128]{2,1,0:T(8,128)}, f32[2,128,128]{2,1,0:T(8,128)S(1)}, u32[]{:S(2)}, u32[]{:S(2)}) collective-permute-start(f32[2,128,128]{2,1,0:T(8,128)} %get-tuple-element.63), channel_id=1, source_target_pairs={{0,32},{32,0},{64,96},{96,64},{1,33},{33,1},{65,97},{97,65},{2,34}... | collective-permute-start | bytes 393224 | tf_op jit(solution)/shard_map/ppermute | solution.py:72
  76.7 14.2 %collective-permute-start.15 = (f32[128,128]{1,0:T(8,128)S(1)}, f32[128,128]{1,0:T(8,128)S(1)}, u32[]{:S(2)}, u32[]{:S(2)}) collective-permute-start(f32[128,128]{1,0:T(8,128)S(1)} %slice_bitcast_fusion), channel_id=1, source_target_pairs={{0,64},{32,96},{64,0},{96,32},{1,65},{33,97},{65,1},{97,33},{2,66}... | collective-permute-start | bytes 196616 | tf_op jit(solution)/shard_map/ppermute | solution.py:72
  95.6 23.5 %copy-start.6 = (s32[128]{0:T(128)S(1)}, s32[128]{0:T(128)}, u32[]{:S(2)}) copy-start(s32[128]{0:T(128)} %param.21) | copy-start | bytes 1540
  96.3 19.1 %all-to-all-start.3 = ((bf16[8,64,512]{2,1,0:T(8,128)(2,1)}), bf16[8,64,512]{2,1,0:T(8,128)(2,1)S(1)}, u32[]{:S(2)}, u32[]{:S(2)}) async-start(bf16[8,64,512]{2,1,0:T(8,128)(2,1)} %get-tuple-element.57), calls=%async_computation.3 | async-start | bytes 1048576 | tf_op jit(solution)/shard_map/all_to_all | solution.py:407
  103.2 4.7 %collective-permute-start.16 = (f32[136,128]{1,0:T(8,128)S(1)}, f32[136,128]{1,0:T(8,128)S(1)}, u32[]{:S(2)}, u32[]{:S(2)}) collective-permute-start(f32[136,128]{1,0:T(8,128)S(1)} %pad_maximum_fusion), channel_id=1, source_target_pairs={{0,8},{8,0},{16,24},{24,16},{1,9},{9,1},{17,25},{25,17},{2,10},{10... | collective-permute-start | bytes 208904 | tf_op jit(solution)/shard_map/ppermute | solution.py:72
  103.4 1.5 %collective-permute-start.12 = (f32[32,512]{1,0:T(8,128)}, f32[32,512]{1,0:T(8,128)S(1)}, u32[]{:S(2)}, u32[]{:S(2)}) collective-permute-start(f32[32,512]{1,0:T(8,128)} %get-tuple-element.56), channel_id=1, source_target_pairs={{0,32},{32,0},{64,96},{96,64},{1,33},{33,1},{65,97},{97,65},{2,34}... | collective-permute-start | bytes 196616 | tf_op jit(solution)/shard_map/ppermute | solution.py:72
  105.8 7.9 %collective-permute-start.13 = (f32[32,512]{1,0:T(8,128)S(1)}, f32[32,512]{1,0:T(8,128)S(1)}, u32[]{:S(2)}, u32[]{:S(2)}) collective-permute-start(f32[32,512]{1,0:T(8,128)S(1)} %add.24.act1), channel_id=1, source_target_pairs={{0,64},{32,96},{64,0},{96,32},{1,65},{33,97},{65,1},{97,33},{2,66}... | collective-permute-start | bytes 196616 | tf_op jit(solution)/shard_map/ppermute | solution.py:72
  108.7 10.4 %collective-permute-start.17 = (f32[136,128]{1,0:T(8,128)S(1)}, f32[136,128]{1,0:T(8,128)S(1)}, u32[]{:S(2)}, u32[]{:S(2)}) collective-permute-start(f32[136,128]{1,0:T(8,128)S(1)} %fusion.1), channel_id=1, source_target_pairs={{0,16},{8,24},{16,0},{24,8},{1,17},{9,25},{17,1},{25,9},{2,18},{10... | collective-permute-start | bytes 208904 | tf_op jit(solution)/shard_map/ppermute | solution.py:72
  115.4 16.6 %all-to-all-start.2 = ((bf16[8,96,512]{2,1,0:T(8,128)(2,1)}), bf16[8,96,512]{2,1,0:T(8,128)(2,1)S(1)}, u32[]{:S(2)}, u32[]{:S(2)}) async-start(bf16[8,96,512]{2,1,0:T(8,128)(2,1)} %second.1), calls=%async_computation.2 | async-start | bytes 1572864 | tf_op jit(solution)/shard_map/all_to_all | solution.py:413

commit v3 on v2

v3 whole, which is shorter than its diff:
```python
import jax
import jax.numpy as jnp
from jax import lax
from jax.experimental import pallas as pl
from jax.experimental.pallas import tpu as pltpu
from jax.sharding import PartitionSpec as P

noise_clip = 0.5
matrix_rate = 0.004
head_rate = 0.0001
blend_rate = 0.005

bf16 = jnp.bfloat16
f32 = jnp.float32

SPECS = {m: pl.BlockSpec(memory_space=m) for m in (pltpu.VMEM, pltpu.SMEM, pltpu.HBM)}
DMA = pltpu.SemaphoreType.DMA
VMEM, HBM = pltpu.VMEM, pltpu.HBM


def call(
    body, outs, ins, scratch=(), scalars=None, mib=16, flops=0, name=None,
    where=(), to=(), raw=(), raw_out=(),
):
    moved = sum(a.size * a.dtype.itemsize for a in ins)
    moved += sum(o.size * o.dtype.itemsize for o in outs)
    specs = [SPECS[HBM if i in raw else VMEM] for i in range(len(ins))]
    ins = [
        pltpu.with_memory_space_constraint(a, HBM) if i in raw or i in where else a
        for i, a in enumerate(ins)
    ]
    if scalars is not None:
        ins = [scalars, *ins]
        specs = [SPECS[pltpu.SMEM], *specs]
    return pl.pallas_call(
        body,
        out_shape=tuple(HBM(o.shape, o.dtype) if i in to else o for i, o in enumerate(outs)),
        in_specs=specs,
        out_specs=tuple(SPECS[HBM if i in raw_out else VMEM] for i in range(len(outs))),
        scratch_shapes=list(scratch),
        compiler_params=pltpu.CompilerParams(vmem_limit_bytes=mib * 2**20),
        cost_estimate=pl.CostEstimate(flops=flops, bytes_accessed=moved, transcendentals=0),
        name=name,
    )(*ins)


def after(x, other):
    return pl.pallas_call(
        lambda x, other, out: None,
        out_shape=HBM(x.shape, x.dtype),
        in_specs=[SPECS[HBM], SPECS[HBM]],
        out_specs=SPECS[HBM],
        input_output_aliases={0: 0},
        name="after",
    )(pltpu.with_memory_space_constraint(x, HBM), pltpu.with_memory_space_constraint(other, HBM))


def shape(*dims, dtype=bf16):
    return jax.ShapeDtypeStruct(dims, dtype)


def dot(a, b):
    return jnp.dot(a, b, preferred_element_type=f32)


def swap(x, axis, bit):
    n = lax.axis_size(axis)
    return lax.ppermute(x, axis, [(i, i ^ bit) for i in range(n)])


def pack_body(obs, nxt, act, mean, noise, out, means, noises, sems):
    copies = [
        pltpu.make_async_copy(src, dst, sems.at[i])
        for i, (src, dst) in enumerate(
            (
                (mean, means),
                (noise, noises),
                (obs, out.at[:, 0:512]),
                (nxt, out.at[:, 512:1024]),
                (act, out.at[:, 1024:1152]),
            )
        )
    ]
    for c in copies:
        c.start()
    copies[0].wait()
    copies[1].wait()
    clipped = jnp.clip(noises[...], -noise_clip, noise_clip)
    out[:, 1152:1280] = jnp.clip(means[...].astype(f32) + clipped, -1.0, 1.0).astype(bf16)
    for c in copies[2:]:
        c.wait()


def weights_body(cin, tin, cact, tact, w, a, p, wide, thin, sems):
    pairs = []
    for k in range(2):
        pairs.append((cact.at[k], thin.at[k]))
        pairs.append((cin.at[k], wide.at[k]))
    for k in range(2):
        pairs.append((tact.at[k], thin.at[2 + k]))
        pairs.append((tin.at[k], wide.at[2 + k]))
    copies = [pltpu.make_async_copy(src, dst, sems.at[i]) for i, (src, dst) in enumerate(pairs)]
    for c in copies:
        c.start()
    for k in range(4):
        copies[2 * k].wait()
        a[k] = thin[k].astype(bf16)
        copies[2 * k + 1].wait()
        w[k] = wide[k].astype(bf16)
        if k == 0:
            p[...] = dot(a[0], w[0]).T.astype(bf16)


def forward_body(at, x0, x1, a, w, mine, out1, out2, out3, left, turned, xs, part):
    core, col = at[0], at[1]
    xs[pl.ds(pl.multiple_of(core * 128, 128), 128), :] = x0[...]
    xs[pl.ds(pl.multiple_of((1 - core) * 128, 128), 128), :] = x1[...]
    turned[...] = xs[:, 1024:1152].T
    for q in range(4):
        s = 0 if q < 2 else 512
        m = 1024 if q < 2 else 1152
        e = (xs[:, s : s + 512].astype(f32) + dot(xs[:, m : m + 128], a[q])).astype(bf16)
        if q < 2:
            left[q] = e.T
        part[:, 512 * q : 512 * q + 512] = dot(e, w[q])

    def rows(k):
        return pl.ds(pl.multiple_of((col ^ k) * 64, 64), 64)

    mine[...] = part[rows(0), :]
    out1[...] = part[rows(1), :].astype(bf16)
    out2[...] = part[rows(2), :].astype(bf16)
    out3[...] = part[rows(3), :].astype(bf16)


def hidden_body(at, m1, r11, r12, r13, m2, r21, r22, r23, heads, rew, slope, hidden, packet, vals):
    y_hi = at[2]
    vals[...] = jnp.zeros_like(vals)
    for half, (m, r1, r2, r3) in enumerate(((m1, r11, r12, r13), (m2, r21, r22, r23))):
        rows = slice(64 * half, 64 * half + 64)
        for q in range(4):
            cols = slice(512 * q, 512 * q + 512)
            pre = (m[:, cols] + r1[:, cols].astype(f32)) + (
                r2[:, cols].astype(f32) + r3[:, cols].astype(f32)
            )
            sig = jax.nn.sigmoid(pre)
            hid = pre * sig
            v = heads[q : q + 1, :]
            vals[rows, q : q + 1] = jnp.sum(hid * v, axis=1, keepdims=True)
            if q < 2:
                hidden[rows, cols] = hid
                slope[rows, cols] = (v * (sig * (1.0 + pre * (1.0 - sig)))).astype(bf16)
    turned = vals[...].T[0:8, :]
    swapped = jnp.concatenate([turned[:, 64:128], turned[:, 0:64]], axis=1)
    turned = jnp.where(y_hi == 1, swapped, turned)
    line = lax.broadcasted_iota(jnp.int32, (8, 128), 0)
    turned = jnp.where(line < 4, turned, rew[...])
    for i in range(16):
        packet[i] = turned


def errors_body(
    at, s0, s1, s2, s3, got, turned1, turned2, hidden, p,
    out, delta, keep, give, terr,
    slope0, errs,
):
    core, col, y_hi = at[0], at[1], at[2]
    for c in range(4):
        v = (got[c] + got[4 + c]) + (got[8 + c] + got[12 + c])
        lanes = slice(64 * (c % 2), 64 * (c % 2) + 64)
        both = jnp.concatenate([got[c // 2 * 4][:, lanes], got[(2 + c // 2) * 4][:, lanes]], axis=1)
        goal = both[4:5] + both[5:6] * jnp.minimum(v[2:3], v[3:4])
        e = v[0:2] - goal
        e = jnp.where(y_hi == 1, jnp.concatenate([e[:, 64:128], e[:, 0:64]], axis=1), e)
        errs[c, 0:2, :] = e
    lo = jnp.concatenate([errs[0, 0:2, 0:64], errs[1, 0:2, 0:64]], axis=1)
    hi = jnp.concatenate([errs[2, 0:2, 0:64], errs[3, 0:2, 0:64]], axis=1)
    terr[...] = jnp.where(core == 1, hi, lo)
    for k, s in enumerate((s0, s1, s2, s3)):
        c = col ^ k
        block = jnp.concatenate([errs[c], jnp.zeros((120, 128), f32)], axis=0)
        e = 2.0 * block.T
        for half in range(2):
            rows = slice(64 * half, 64 * half + 64)
            to = pl.ds(pl.multiple_of(256 * half + 64 * c, 64), 64)
            slope0[to, :] = s[rows, 0:512]
            for q in range(2):
                cols = slice(512 * q, 512 * q + 512)
                delta[q, to, :] = (e[rows, q : q + 1] * s[rows, cols].astype(f32)).astype(bf16)
        if k == 0:
            heads = [
                jnp.sum(e[:, q : q + 1] * hidden[:, 512 * q : 512 * q + 512], axis=0, keepdims=True)
                for q in range(2)
            ]
    tail = jnp.concatenate([*heads, jnp.zeros((14, 512), f32)], axis=0).astype(bf16)
    for q in range(2):
        m = dot(turned1[...], delta[q, 0:256]) + dot(turned2[...], delta[q, 256:512])
        for d in range(8):
            out[d, 16 * q : 16 * q + 16, :] = m[16 * d : 16 * d + 16, :].astype(bf16)
    for d in range(8):
        out[d, 32:48, :] = tail
    push = dot(slope0[...], p[...])
    for chip in range(2):
        first, second = push[256 * chip : 256 * chip + 128], push[256 * chip + 128 : 256 * chip + 256]
        rows = slice(128 * chip, 128 * chip + 128)
        keep[rows, :] = jnp.where(core == 1, second, first)
        give[rows, :] = jnp.where(core == 1, first, second)


def grads_body(left1, left2, delta, out):
    for q in range(2):
        grad = dot(left1[q], delta[q, 0:256]) + dot(left2[q], delta[q, 256:512])
        for d in range(8):
            out[d, 64 * q : 64 * q + 64, :] = grad[64 * d : 64 * d + 64, :].astype(bf16)


def summed(got, rows):
    x = [got[d, rows, :].astype(f32) for d in range(8)]
    return ((x[0] + x[1]) + (x[2] + x[3])) + ((x[4] + x[5]) + (x[6] + x[7]))


def action_body(got, w, keep, give, mine, theirs):
    for q in range(2):
        m = summed(got, slice(16 * q, 16 * q + 16)).astype(bf16)
        term = lax.dot_general(m, w[q], (((1,), (1,)), ((), ())), preferred_element_type=f32)
        for j in range(4):
            i = 16 * (4 * q + j)
            mine[i : i + 16, :] = term[:, 128 * j : 128 * j + 128]
            theirs[i : i + 16, :] = term[:, 128 * j : 128 * j + 128]
    mine[128:384, :] = keep[...]
    theirs[128:384, :] = give[...]
    heads = summed(got, slice(32, 40))
    for q in range(2):
        for j in range(4):
            i = 384 + 4 * q + j
            mine[i : i + 1, :] = heads[q : q + 1, 128 * j : 128 * j + 128]
    theirs[384:392, :] = jnp.zeros((8, 128), f32)


def fold_body(mine, other, high, low, own):
    total = mine[0:128, :] + other[0:128, :]
    high[0:128, :] = total
    low[...] = total
    high[128:256, :] = mine[256:384, :] + other[256:384, :]
    own[0:128, :] = mine[128:256, :] + other[128:256, :]
    own[128:136, :] = mine[384:392, :]


def pair_body(high, low, own, from_high, from_low, from_both, pair, rest):
    sums = (low[...] + from_high[0:128, :], from_low[...] + from_both[...])
    for m, total in enumerate(sums):
        for q in range(2):
            for j in range(4):
                i = 16 * (4 * q + j)
                lanes = slice(128 * j, 128 * j + 128)
                pair[m, 16 * q : 16 * q + 16, lanes] = total[i : i + 16, :].astype(bf16)
    rest[0:128, :] = own[0:128, :] + from_high[128:256, :]
    rest[128:136, :] = own[128:136, :]


def total_body(got, pair, chunk):
    total = summed(got, slice(0, 128)).astype(bf16)
    for d in range(8):
        chunk[d] = total


def update_body(
    at, g, g0, g1, g2, g3, cin, tin, cact, tact,
    fresh, blended, fresh_act, blended_act,
    c, t, ca, ta, isems, osems, asems,
):
    dp = at[3]
    places = [(q, slice(256 * h, 256 * h + 256)) for q in range(2) for h in range(2)]
    ins, outs = [], []
    for i, (q, rows) in enumerate(places):
        ins.append(pltpu.make_async_copy(cin.at[q, rows], c.at[q, rows], isems.at[0, i]))
        ins.append(pltpu.make_async_copy(tin.at[q, rows], t.at[q, rows], isems.at[1, i]))
        outs.append(pltpu.make_async_copy(c.at[q, rows], fresh.at[q, rows], osems.at[0, i]))
        outs.append(pltpu.make_async_copy(t.at[q, rows], blended.at[q, rows], osems.at[1, i]))
    more = [
        pltpu.make_async_copy(cact, ca, asems.at[0]),
        pltpu.make_async_copy(tact, ta, asems.at[1]),
    ]
    last = [
        pltpu.make_async_copy(ca, fresh_act, asems.at[2]),
        pltpu.make_async_copy(ta, blended_act, asems.at[3]),
    ]
    for copy in ins + more:
        copy.start()
    for i, (q, rows) in enumerate(places):
        ins[2 * i].wait()
        ins[2 * i + 1].wait()
        for d in range(rows.start // 64, rows.stop // 64):
            part = slice(64 * d, 64 * d + 64)
            new = c[q, part, :] - matrix_rate * g[d, 64 * q : 64 * q + 64, :].astype(f32)
            c[q, part, :] = new
            t[q, part, :] = blend_rate * new + (1.0 - blend_rate) * t[q, part, :]
        outs[2 * i].start()
        outs[2 * i + 1].start()
    for copy in more:
        copy.wait()
    for k, piece in enumerate((g0, g1, g2, g3)):
        for m in range(2):
            rows = pl.ds(pl.multiple_of((dp ^ (4 * m + k)) * 16, 16), 16)
            for q in range(2):
                new = ca[q, rows, :] - matrix_rate * piece[m, 16 * q : 16 * q + 16, :].astype(f32)
                ca[q, rows, :] = new
                ta[q, rows, :] = blend_rate * new + (1.0 - blend_rate) * ta[q, rows, :]
    for copy in last:
        copy.start()
    for copy in last + outs:
        copy.wait()


def on_device(
    observed,
    next_observed,
    actions,
    next_mean,
    policy_noise,
    rewards,
    discounts,
    actor_flags,
    critic_in,
    critic_act,
    critic_head,
    target_in,
    target_act,
    target_head,
):
    row, col, dp = lax.axis_index("row"), lax.axis_index("col"), lax.axis_index("dp")
    at = jnp.stack([row % 2, col, row // 2, dp]).astype(jnp.int32)

    (own,) = call(
        pack_body,
        [shape(128, 1280)],
        [observed, next_observed, actions, next_mean, policy_noise],
        scratch=[pltpu.VMEM((128, 128), bf16), pltpu.VMEM((128, 128), f32), DMA((5,))],
        mib=4, raw=range(5), name="pack",
    )
    sib = swap(own, "row", 1)
    far = swap(own, "row", 2)
    w16, a16, p16 = call(
        weights_body,
        [shape(4, 512, 512), shape(4, 128, 512), shape(512, 128)],
        [critic_in, target_in, critic_act, target_act],
        scratch=[pltpu.VMEM((4, 512, 512), f32), pltpu.VMEM((4, 128, 512), f32), DMA((8,))],
        mib=16, flops=2 * 128 * 512 * 512, raw=range(4), to=(2,), name="weights",
    )

    def forward(x0, x1, name, where, to):
        return call(
            forward_body,
            [
                shape(64, 2048, dtype=f32), shape(64, 2048), shape(64, 2048), shape(64, 2048),
                shape(2, 512, 256), shape(128, 256),
            ],
            [x0, x1, a16, w16],
            scratch=[pltpu.VMEM((256, 1280), bf16), pltpu.VMEM((256, 2048), f32)],
            scalars=at, flops=8 * 256 * 640 * 512, where=where, to=to, name=name,
        )

    mine1, *out1, left1, turned1 = forward(own, sib, "forward_near", (), range(6))
    in1 = [None, None, None]
    for k in (2, 1, 3):
        in1[k - 1] = swap(out1[k - 1], "col", k)
    far = after(far, mine1)
    farsib = swap(far, "row", 1)
    mine2, *out2, left2, turned2 = forward(far, farsib, "forward_far", (0,), (0, 4, 5))
    in2 = [None, None, None]
    for k in (2, 1, 3):
        in2[k - 1] = swap(out2[k - 1], "col", k)
    heads = jnp.concatenate([critic_head, target_head, jnp.zeros((4, 512), f32)], axis=0)
    blank = jnp.zeros((1, 128), f32)
    rew = jnp.concatenate(
        [blank, blank, blank, blank, rewards.astype(f32)[None], discounts.astype(f32)[None], blank, blank]
    )
    slope, hidden, packet = call(
        hidden_body,
        [shape(128, 1024), shape(128, 1024, dtype=f32), shape(16, 8, 128, dtype=f32)],
        [mine1, *in1, mine2, *in2, heads, rew],
        scratch=[pltpu.VMEM((128, 128), f32)],
        scalars=at, where=(0, 4), to=(1,), name="hidden", flops=128 * 2048 * 30,
    )
    slopes = [slope] + [swap(slope, "col", k) for k in (1, 2, 3)]
    got = lax.all_to_all(packet, ("row", "col"), 0, 0, tiled=True)
    moves, delta, keep, give, temporal_errors = call(
        errors_body,
        [
            shape(8, 48, 512), shape(2, 512, 512), shape(256, 128, dtype=f32),
            shape(256, 128, dtype=f32), shape(2, 128, dtype=f32),
        ],
        [*slopes, got, turned1, turned2, hidden, p16],
        scratch=[pltpu.VMEM((512, 512), bf16), pltpu.VMEM((4, 8, 128), f32)],
        scalars=at, where=(5, 6, 7, 8), to=(0, 2, 3), name="errors",
        flops=6 * 128 * 512 * 512,
    )
    moves = lax.all_to_all(moves, "dp", 0, 0, tiled=True)
    (grads,) = call(
        grads_body, [shape(8, 128, 512)], [left1, left2, delta],
        where=(0, 1), name="grads", flops=4 * 512 * 512 * 512,
    )
    parts = lax.all_to_all(grads, "dp", 0, 0, tiled=True)
    mine, theirs = call(
        action_body, [shape(392, 128, dtype=f32)] * 2, [moves, w16, keep, give],
        where=(2, 3), name="action", flops=4 * 16 * 512 * 512,
    )
    high, low, own = call(
        fold_body,
        [shape(256, 128, dtype=f32), shape(128, 128, dtype=f32), shape(136, 128, dtype=f32)],
        [mine, swap(theirs, "row", 1)], name="fold",
    )
    from_high = swap(high, "row", 2)
    from_low = swap(low, "dp", 4)
    from_both = lax.ppermute(low, ("row", "dp"), [(i, i ^ 20) for i in range(32)])
    pair, rest = call(
        pair_body, [shape(2, 32, 512), shape(136, 128, dtype=f32)],
        [high, low, own, from_high, from_low, from_both], name="pair",
    )
    (chunk,) = call(total_body, [shape(8, 128, 512)], [parts, pair], name="total")
    grad_in = lax.all_to_all(chunk, "dp", 0, 0, tiled=True)
    pairs = [pair] + [swap(pair, "dp", k) for k in (1, 2, 3)]
    rest = rest + swap(rest, "col", 1)
    rest = rest + swap(rest, "col", 2)
    action_slope = actor_flags.astype(f32)[:, None] * rest[0:128]
    head = rest[128:136].reshape(2, 512)
    new_head = critic_head - head_rate * head
    new_target_head = blend_rate * new_head + (1.0 - blend_rate) * target_head
    wide, thin = shape(2, 512, 512, dtype=f32), shape(2, 128, 512, dtype=f32)
    big, small = pltpu.VMEM((2, 512, 512), f32), pltpu.VMEM((2, 128, 512), f32)
    new_in, new_target_in, new_act, new_target_act = call(
        update_body, [wide, wide, thin, thin],
        [grad_in, *pairs, critic_in, target_in, critic_act, target_act],
        scratch=[big, big, small, small, DMA((2, 4)), DMA((2, 4)), DMA((4,))],
        scalars=at, raw=range(5, 9), raw_out=range(4), to=range(4), name="update",
    )
    return (
        new_in,
        new_act,
        new_head,
        new_target_in,
        new_target_act,
        new_target_head,
        temporal_errors,
        action_slope,
    )


def solution(mesh):
    return jax.shard_map(
        on_device,
        mesh=mesh,
        in_specs=(
            P(("row", "dp"), "col"),
            P(("row", "dp"), "col"),
            P(("row", "dp"), None),
            P(("row", "dp"), None),
            P(("row", "dp"), None),
            P(("row", "dp")),
            P(("row", "dp")),
            P(("row", "dp")),
            P(None, "col", "row"),
            P(None, None, "col"),
            P(None, "row"),
            P(None, "col", "row"),
            P(None, None, "col"),
            P(None, "row"),
        ),
        out_specs=(
            P(None, "col", "row"),
            P(None, None, "col"),
            P(None, "row"),
            P(None, "col", "row"),
            P(None, None, "col"),
            P(None, "row"),
            P(None, ("row", "dp")),
            P(("row", "dp"), None),
        ),
        check_vma=False,
    )
```

time: 137 us -> 131 us (0.956); the launches traced: 135 us -> 131 us
  other arithmetic: 5.67 us -> 1.57 us
  waiting for transfers between devices: 46 us -> 48.8 us
  local copies, waits for them, and re-layouts: 2.63 us -> 0.19 us
    ppermute x18 -> x20, waiting for transfers between devices: 34.5 us -> 42.7 us  [swap(): return lax.ppermute(x, axis, [(i, i ^ bit) for i in range(n)])]
    add x5 -> x2, other arithmetic: 3.28 us -> 0.02 us  [the longest x1 0.01 us: on_device(): rest = rest + swap(rest, 'col', 2)]
    all_to_all x2, waiting for transfers between devices: 8.85 us -> 6.06 us  [the longest x1 6.06 us: on_device(): moves = lax.all_to_all(moves, 'dp', 0, 0, tiled=True)]
    all_to_all x1, waiting for transfers between devices: 2.68 us -> 0.01 us  [on_device(): parts = lax.all_to_all(grads, 'dp', 0, 0, tiled=True)]
    unnamed x14 -> x10, local copies, waits for them, and re-layouts: 1.71 us -> 0.02 us
    ppermute x18 -> x20, starting transfers between devices: 26.7 us -> 27.8 us  [swap(): return lax.ppermute(x, axis, [(i, i ^ bit) for i in range(n)])]
    pallas_call x10 -> x12, Pallas kernels: 27 us -> 26.3 us  [call(): pl.pallas_call(body, out_shape=tuple((HBM(o.shape, o.dtype) if i in to el...]
  transfers between devices with their start and end apart: 21 -> 24, of which waited for: 11 -> 11; matrix products, arithmetic and copies ran while one was open for 4% -> 1% of each run, Pallas kernels for 11% -> 11%
where the time goes in v3:
time: 131 us
  waiting for transfers between devices  48.8 us (37%)
  starting transfers between devices  40.4 us (31%)
  Pallas kernels  26.3 us (20%)
  blocking collectives  12.6 us (10%)
  other arithmetic  1.57 us (1%)
    ppermute x20, waiting for transfers between devices, swap(): return lax.ppermute(x, axis, [(i, i ^ bit) for i in range(n)])  42.7 us
    ppermute x20, starting transfers between devices, swap(): return lax.ppermute(x, axis, [(i, i ^ bit) for i in range(n)])  27.8 us
    pallas_call x12, Pallas kernels, call(): pl.pallas_call(body, out_shape=tuple((HBM(o.shape, o.dtype) if i in to el...  26.3 us
    all_to_all x1, blocking collectives, on_device(): got = lax.all_to_all(packet, ('row', 'col'), 0, 0, tiled=True)  12.6 us
    all_to_all x1, waiting for transfers between devices, on_device(): moves = lax.all_to_all(moves, 'dp', 0, 0, tiled=True)  6.06 us
    all_to_all x1, starting transfers between devices, on_device(): moves = lax.all_to_all(moves, 'dp', 0, 0, tiled=True)  4.42 us
    all_to_all x1, starting transfers between devices, on_device(): grad_in = lax.all_to_all(chunk, 'dp', 0, 0, tiled=True)  4.01 us
    all_to_all x1, starting transfers between devices, on_device(): parts = lax.all_to_all(grads, 'dp', 0, 0, tiled=True)  3.56 us
  transfers between devices with their start and end apart: 24, of which 11 were waited for; matrix products, arithmetic and copies ran while one was open for 1% of the time, Pallas kernels for 11%

profile of v3, /device:TPU:0, one launch (start us, length us, event | category | flops | bytes accessed | tf_op | source)
XLA Modules:
  0.0 130.6 jit_solution(10612739715179268177)
XLA Ops:
  0.6 1.1 pack.1.x0
  1.7 0.1 collective-permute-start
  1.8 3.4 %collective-permute-start.1 = (bf16[128,1280]{1,0:T(8,128)(2,1)S(1)}, bf16[128,1280]{1,0:T(8,128)(2,1)}, u32[]{:S(2)}, u32[]{:S(2)}) collective-permute-start(bf16[128,1280]{1,0:T(8,128)(2,1)S(1)} %pack.1.x0), channel_id=1, source_target_pairs={{0,64},{32,96},{64,0},{96,32},{1,65},{33,97},{65,1},{97,33},{2,66}... | collective-permute-start | bytes 983048 | tf_op jit(solution)/shard_map/ppermute | solution.py:68
  5.2 0.1 pad.3.clone
  5.2 3.2 %weights.1 = (bf16[4,512,512]{2,1,0:T(8,128)(2,1)S(1)}, bf16[4,128,512]{2,1,0:T(8,128)(2,1)S(1)}, bf16[512,128]{1,0:T(8,128)(2,1)}) custom-call(f32[2,512,512]{2,1,0:T(8,128)} %cin.3, f32[2,512,512]{2,1,0:T(8,128)} %tin.3, f32[2,128,512]{2,1,0:T(8,128)} %cact.3, f32[2,128,512]{2,1,0:T(8,128)} %tact.3), custom_call_target="tpu_custom_call" | custom-call | flops 67108864 | bytes 7995392 | tf_op jit(solution)/shard_map/weights/pallas_call | solution.py:35
  8.5 0.1 pad_add_fusion.at
  8.5 0.0 collective-permute-done.x1
  8.5 3.2 %forward_near.1 = (f32[64,2048]{1,0:T(8,128)}, bf16[64,2048]{1,0:T(8,128)(2,1)}, bf16[64,2048]{1,0:T(8,128)(2,1)}, bf16[64,2048]{1,0:T(8,128)(2,1)}, bf16[2,512,...) custom-call(s32[4]{0:T(128)S(1)} %pad_add_fusion.at, bf16[128,1280]{1,0:T(8,128)(2,1)S(1)} %pack.1.x0, ...), custom_call_target="tpu_custom_call" | custom-call | flops 671088640 | bytes 5177344 | tf_op jit(solution)/shard_map/forward_near/pallas_call | solution.py:35
  11.7 1.9 %collective-permute-done.1.x = bf16[128,1280]{1,0:T(8,128)(2,1)} collective-permute-done((bf16[128,1280]{1,0:T(8,128)(2,1)S(1)}, bf16[128,1280]{1,0:T(8,128)(2,1)}, u32[]{:S(2)}, u32[]{:S(2)}) %collective-permute-start.1) | collective-permute-done | bytes 327712 | tf_op jit(solution)/shard_map/ppermute | solution.py:68
  13.6 0.0 collective-permute-start.2
  13.6 0.1 fusion
  13.7 2.0 %collective-permute-start.3 = (bf16[64,2048]{1,0:T(8,128)(2,1)}, bf16[64,2048]{1,0:T(8,128)(2,1)S(1)}, u32[]{:S(2)}, u32[]{:S(2)}) collective-permute-start(bf16[64,2048]{1,0:T(8,128)(2,1)} %get-tuple-element.47), channel_id=1, source_target_pairs={{0,8},{8,0},{16,24},{24,16},{1,9},{9,1},{17,25},{25,17},{2,10},{10... | collective-permute-start | bytes 786440 | tf_op jit(solution)/shard_map/ppermute | solution.py:68
  15.7 3.7 %collective-permute-start.4 = (bf16[64,2048]{1,0:T(8,128)(2,1)}, bf16[64,2048]{1,0:T(8,128)(2,1)S(1)}, u32[]{:S(2)}, u32[]{:S(2)}) collective-permute-start(bf16[64,2048]{1,0:T(8,128)(2,1)} %get-tuple-element.48), channel_id=1, source_target_pairs={{0,16},{8,24},{16,0},{24,8},{1,17},{9,25},{17,1},{25,9},{2,18},{10... | collective-permute-start | bytes 786440 | tf_op jit(solution)/shard_map/ppermute | solution.py:68
  19.3 0.0 collective-permute-start.5
  19.3 0.0 collective-permute-done.2.x1
  19.3 3.2 %forward_far.1 = (f32[64,2048]{1,0:T(8,128)}, bf16[64,2048]{1,0:T(8,128)(2,1)S(1)}, bf16[64,2048]{1,0:T(8,128)(2,1)S(1)}, bf16[64,2048]{1,0:T(8,128)(2,1)S(1)}, ...) custom-call(s32[4]{0:T(128)S(1)} %pad_add_fusion.at, bf16[128,1280]{1,0:T(8,128)(2,1)} %after.1.x0, ...), custom_call_target="tpu_custom_call" | custom-call | flops 671088640 | bytes 5177344 | tf_op jit(solution)/shard_map/forward_far/pallas_call | solution.py:35
  22.5 0.1 collective-permute-start.6
  22.6 4.6 %collective-permute-start.7 = (bf16[64,2048]{1,0:T(8,128)(2,1)S(1)}, bf16[64,2048]{1,0:T(8,128)(2,1)S(1)}, u32[]{:S(2)}, u32[]{:S(2)}) collective-permute-start(bf16[64,2048]{1,0:T(8,128)(2,1)S(1)} %get-tuple-element.52), channel_id=1, source_target_pairs={{0,16},{8,24},{16,0},{24,8},{1,17},{9,25},{17,1},{25,9},{2,18},{10... | collective-permute-start | bytes 786440 | tf_op jit(solution)/shard_map/ppermute | solution.py:68
  27.2 0.0 collective-permute-done.3.r11
  27.2 0.0 collective-permute-start.8
  27.2 0.1 maximum_maximum_fusion.1.rew
  27.3 0.1 maximum_maximum_fusion.heads
  27.4 4.8 %collective-permute-done.4.r12 = bf16[64,2048]{1,0:T(8,128)(2,1)S(1)} collective-permute-done((bf16[64,2048]{1,0:T(8,128)(2,1)}, bf16[64,2048]{1,0:T(8,128)(2,1)S(1)}, u32[]{:S(2)}, u32[]{:S(2)}) %collective-permute-start.4) | collective-permute-done | bytes 262176 | tf_op jit(solution)/shard_map/ppermute | solution.py:68
  32.2 3.4 %collective-permute-done.5.r13 = bf16[64,2048]{1,0:T(8,128)(2,1)S(1)} collective-permute-done((bf16[64,2048]{1,0:T(8,128)(2,1)}, bf16[64,2048]{1,0:T(8,128)(2,1)S(1)}, u32[]{:S(2)}, u32[]{:S(2)}) %collective-permute-start.5) | collective-permute-done | bytes 262176 | tf_op jit(solution)/shard_map/ppermute | solution.py:68
  35.6 0.0 collective-permute-done.6.r21
  35.6 7.6 %collective-permute-done.7.r22 = bf16[64,2048]{1,0:T(8,128)(2,1)S(1)} collective-permute-done((bf16[64,2048]{1,0:T(8,128)(2,1)S(1)}, bf16[64,2048]{1,0:T(8,128)(2,1)S(1)}, u32[]{:S(2)}, u32[]{:S(2)}) %collective-permute-start.7) | collective-permute-done | bytes 262176 | tf_op jit(solution)/shard_map/ppermute | solution.py:68
  43.1 2.6 %collective-permute-done.8.r23 = bf16[64,2048]{1,0:T(8,128)(2,1)S(1)} collective-permute-done((bf16[64,2048]{1,0:T(8,128)(2,1)S(1)}, bf16[64,2048]{1,0:T(8,128)(2,1)S(1)}, u32[]{:S(2)}, u32[]{:S(2)}) %collective-permute-start.8) | collective-permute-done | bytes 262176 | tf_op jit(solution)/shard_map/ppermute | solution.py:68
  45.7 2.5 %hidden.1 = (bf16[128,1024]{1,0:T(8,128)(2,1)S(1)}, f32[128,1024]{1,0:T(8,128)}, f32[16,8,128]{2,1,0:T(8,128)S(1)}) custom-call(s32[4]{0:T(128)S(1)} %pad_add_fusion.at, f32[64,2048]{1,0:T(8,128)} %get-tuple-element.45.other.m1, bf16[64,2048]{1,0:T(8,128)(2,1)S(1)} %collective-permute-done.3.r11, bf16[64,2048]{1,0:T(8,128)(2,1)S(1)} %collective-permute-done.4.r12, ...), custom_call_target="tpu_custom_call" | custom-call | flops 7864320 | bytes 3493888 | tf_op jit(solution)/shard_map/hidden/pallas_call | solution.py:35
  48.2 0.0 collective-permute-start.10
  48.2 1.3 collective-permute-start.11
  49.5 2.2 %collective-permute-start.9 = (bf16[128,1024]{1,0:T(8,128)(2,1)S(1)}, bf16[128,1024]{1,0:T(8,128)(2,1)S(1)}, u32[]{:S(2)}, u32[]{:S(2)}) collective-permute-start(bf16[128,1024]{1,0:T(8,128)(2,1)S(1)} %get-tuple-element.54.s0), channel_id=1, source_target_pairs={{0,8},{8,0},{16,24},{24,16},{1,9},{9,1},{17,25},{25,17},{2,10},{10... | collective-permute-start | bytes 786440 | tf_op jit(solution)/shard_map/ppermute | solution.py:68
  51.7 12.6 %all_to_all.20.got = f32[16,8,128]{2,1,0:T(8,128)S(1)} all-to-all(f32[16,8,128]{2,1,0:T(8,128)S(1)} %get-tuple-element.55), channel_id=1, replica_groups=mesh['row'=4,'col'=4,'dp'=8] {'row','col'}, dimensions={0} | all-to-all | bytes 131072 | tf_op jit(solution)/shard_map/all_to_all | solution.py:386
  64.3 0.0 collective-permute-done.10.s2
  64.3 0.0 collective-permute-done.11.s3
  64.4 0.0 collective-permute-done.9.s1
  64.4 2.9 %errors.1 = (bf16[8,48,512]{2,1,0:T(8,128)(2,1)}, bf16[2,512,512]{2,1,0:T(8,128)(2,1)S(1)}, f32[256,128]{1,0:T(8,128)}, f32[256,128]{1,0:T(8,128)}, f32[2,128]{1,0:T(2,128)}) custom-call(s32[4]{0:T(128)S(1)} %pad_add_fusion.at, bf16[128,1024]{1,0:T(8,128)(2,1)S(1)} %get-tuple-element.54.s0, bf16[128,1024]{1,0:T(8,128)(2,1)S(1)} %collective-permute-done.9.s1, ...), custom_call_target="tpu_custom_call" | custom-call | flops 201326592 | bytes 3605504 | tf_op jit(solution)/shard_map/errors/pallas_call | solution.py:35
  67.3 4.4 %all-to-all-start.2 = ((bf16[8,48,512]{2,1,0:T(8,128)(2,1)}), bf16[8,48,512]{2,1,0:T(8,128)(2,1)S(1)}, u32[]{:S(2)}, u32[]{:S(2)}) async-start(bf16[8,48,512]{2,1,0:T(8,128)(2,1)} %get-tuple-element.61), calls=%async_computation.2 | async-start | bytes 786432 | tf_op jit(solution)/shard_map/all_to_all | solution.py:398
  71.7 2.9 %grads.1 = bf16[8,128,512]{2,1,0:T(8,128)(2,1)} custom-call(bf16[2,512,256]{2,1,0:T(8,128)(2,1)} %get-tuple-element.44.left1, bf16[2,512,256]{2,1,0:T(8,128)(2,1)} %get-tuple-element.46.left2, bf16[2,512,512]{2,1,0:T(8,128)(2,1)S(1)} %get-tuple-element.60.delta), custom_call_target="tpu_custom_call" | custom-call | flops 536870912 | bytes 3145728 | tf_op jit(solution)/shard_map/grads/pallas_call | solution.py:35
  74.6 6.1 %all-to-all-done.2.got = bf16[8,48,512]{2,1,0:T(8,128)(2,1)S(1)} async-done(((bf16[8,48,512]{2,1,0:T(8,128)(2,1)}), bf16[8,48,512]{2,1,0:T(8,128)(2,1)S(1)}, u32[]{:S(2)}, u32[]{:S(2)}) %all-to-all-start.2) | async-done | bytes 393248 | tf_op jit(solution)/shard_map/all_to_all | solution.py:398
  80.7 3.6 %all-to-all-start.1 = ((bf16[8,128,512]{2,1,0:T(8,128)(2,1)}), bf16[8,128,512]{2,1,0:T(8,128)(2,1)S(1)}, u32[]{:S(2)}, u32[]{:S(2)}) async-start(bf16[8,128,512]{2,1,0:T(8,128)(2,1)} %grads.1), calls=%async_computation.1 | async-start | bytes 2097152 | tf_op jit(solution)/shard_map/all_to_all | solution.py:403
  84.2 1.4 %action.1 = (f32[392,128]{1,0:T(8,128)S(1)}, f32[392,128]{1,0:T(8,128)S(1)}) custom-call(bf16[8,48,512]{2,1,0:T(8,128)(2,1)S(1)} %all-to-all-done.2.got, bf16[4,512,512]{2,1,0:T(8,128)(2,1)S(1)} %get-tuple-element.43.w, f32[256,128]{1,0:T(8,128)} %get-tuple-element.62.keep, f32[256,128]{1,0:T(8,128)} %get-tuple-element.63.give), custom_call_target="tpu_custom_call" | custom-call | flops 16777216 | bytes 3153920 | tf_op jit(solution)/shard_map/action/pallas_call | solution.py:35
  85.6 1.5 %collective-permute-done.12.other = f32[392,128]{1,0:T(8,128)S(1)} collective-permute-done((f32[392,128]{1,0:T(8,128)S(1)}, f32[392,128]{1,0:T(8,128)S(1)}, u32[]{:S(2)}, u32[]{:S(2)}) %collective-permute-start.12) | collective-permute-done | bytes 200736 | tf_op jit(solution)/shard_map/ppermute | solution.py:68
  87.1 2.8 %collective-permute-start.13 = (f32[256,128]{1,0:T(8,128)S(1)}, f32[256,128]{1,0:T(8,128)S(1)}, u32[]{:S(2)}, u32[]{:S(2)}) collective-permute-start(f32[256,128]{1,0:T(8,128)S(1)} %get-tuple-element.66.high), channel_id=1, source_target_pairs={{0,64},{32,96},{64,0},{96,32},{1,65},{33,97},{65,1},{97,33},{2,66}... | collective-permute-start | bytes 393224 | tf_op jit(solution)/shard_map/ppermute | solution.py:68
  89.9 1.3 %collective-permute-start.14 = (f32[128,128]{1,0:T(8,128)S(1)}, f32[128,128]{1,0:T(8,128)S(1)}, u32[]{:S(2)}, u32[]{:S(2)}) collective-permute-start(f32[128,128]{1,0:T(8,128)S(1)} %get-tuple-element.67.low), channel_id=1, source_target_pairs={{0,4},{1,5},{2,6},{3,7},{4,0},{5,1},{6,2},{7,3},{8,12},{9,13},{10,... | collective-permute-start | bytes 196616 | tf_op jit(solution)/shard_map/ppermute | solution.py:68
  91.2 0.6 collective-permute-start.15
  91.8 10.8 %collective-permute-done.14.from_low = f32[128,128]{1,0:T(8,128)S(1)} collective-permute-done((f32[128,128]{1,0:T(8,128)S(1)}, f32[128,128]{1,0:T(8,128)S(1)}, u32[]{:S(2)}, u32[]{:S(2)}) %collective-permute-start.14) | collective-permute-done | bytes 65568 | tf_op jit(solution)/shard_map/ppermute | solution.py:68
  102.5 0.0 collective-permute-done.15.from_both
  102.5 0.0 collective-permute-done.13.from_high
  102.6 0.0 all-to-all-done.1.got
  102.6 0.0 copy-start.4
  102.6 1.1 total.1
  103.7 4.0 %all-to-all-start.3 = ((bf16[8,128,512]{2,1,0:T(8,128)(2,1)}), bf16[8,128,512]{2,1,0:T(8,128)(2,1)S(1)}, u32[]{:S(2)}, u32[]{:S(2)}) async-start(bf16[8,128,512]{2,1,0:T(8,128)(2,1)} %total.1), calls=%async_computation.3 | async-start | bytes 2097152 | tf_op jit(solution)/shard_map/all_to_all | solution.py:421
  107.7 0.4 collective-permute-start.19
  108.1 3.9 %collective-permute-done.19 = f32[136,128]{1,0:T(8,128)S(1)} collective-permute-done((f32[136,128]{1,0:T(8,128)S(1)}, f32[136,128]{1,0:T(8,128)S(1)}, u32[]{:S(2)}, u32[]{:S(2)}) %collective-permute-start.19) | collective-permute-done | bytes 69664 | tf_op jit(solution)/shard_map/ppermute | solution.py:68
  112.0 1.3 collective-permute-start.20
  113.3 2.0 %collective-permute-start.16 = (bf16[2,32,512]{2,1,0:T(8,128)(2,1)S(1)}, bf16[2,32,512]{2,1,0:T(8,128)(2,1)S(1)}, u32[]{:S(2)}, u32[]{:S(2)}) collective-permute-start(bf16[2,32,512]{2,1,0:T(8,128)(2,1)S(1)} %get-tuple-element.69.pair.g0), channel_id=1, source_target_pairs={{0,1},{1,0},{2,3},{3,2},{4,5},{5,4},{6,7},{7,6},{8,9},{9,8},{10,11... | collective-permute-start | bytes 196616 | tf_op jit(solution)/shard_map/ppermute | solution.py:68
  115.3 2.7 %collective-permute-start.17 = (bf16[2,32,512]{2,1,0:T(8,128)(2,1)S(1)}, bf16[2,32,512]{2,1,0:T(8,128)(2,1)S(1)}, u32[]{:S(2)}, u32[]{:S(2)}) collective-permute-start(bf16[2,32,512]{2,1,0:T(8,128)(2,1)S(1)} %get-tuple-element.69.pair.g0), channel_id=1, source_target_pairs={{0,2},{1,3},{2,0},{3,1},{4,6},{5,7},{6,4},{7,5},{8,10},{9,11},{10,... | collective-permute-start | bytes 196616 | tf_op jit(solution)/shard_map/ppermute | solution.py:68
  118.0 0.1 collective-permute-start.18
  118.1 0.0 collective-permute-done.20
  118.1 0.7 slice_multiply_fusion
  118.8 0.6 multiply_add_fusion
  119.4 4.1 %collective-permute-done.16.g1 = bf16[2,32,512]{2,1,0:T(8,128)(2,1)S(1)} collective-permute-done((bf16[2,32,512]{2,1,0:T(8,128)(2,1)S(1)}, bf16[2,32,512]{2,1,0:T(8,128)(2,1)S(1)}, u32[]{:S(2)}, u32[]{:S(2)}) %collective-permute-start.16) | collective-permute-done | bytes 65568 | tf_op jit(solution)/shard_map/ppermute | solution.py:68
  123.5 2.2 %collective-permute-done.17.g2 = bf16[2,32,512]{2,1,0:T(8,128)(2,1)S(1)} collective-permute-done((bf16[2,32,512]{2,1,0:T(8,128)(2,1)S(1)}, bf16[2,32,512]{2,1,0:T(8,128)(2,1)S(1)}, u32[]{:S(2)}, u32[]{:S(2)}) %collective-permute-start.17) | collective-permute-done | bytes 65568 | tf_op jit(solution)/shard_map/ppermute | solution.py:68
  125.8 4.9 %update.1 = (f32[2,512,512]{2,1,0:T(8,128)}, f32[2,512,512]{2,1,0:T(8,128)}, f32[2,128,512]{2,1,0:T(8,128)}, f32[2,128,512]{2,1,0:T(8,128)}) custom-call(s32[4]{0:T(128)S(1)} %pad_add_fusion.at, bf16[8,128,512]{2,1,0:T(8,128)(2,1)S(1)} %all-to-all-done.3.g, bf16[2,32,512]{2,1,0:T(8,128)(2,1)S(1)} %get-tuple-element.69.pair.g0, ...), custom_call_target="tpu_custom_call" | custom-call | bytes 11796480 | tf_op jit(solution)/shard_map/update/pallas_call | solution.py:35
  (23 shorter events, 0.1 us)
Async XLA Ops:
  1.7 6.8 %collective-permute-start = (bf16[128,1280]{1,0:T(8,128)(2,1)S(1)}, bf16[128,1280]{1,0:T(8,128)(2,1)S(1)}, u32[]{:S(2)}, u32[]{:S(2)}) collective-permute-start(bf16[128,1280]{1,0:T(8,128)(2,1)S(1)} %pack.1.x0), channel_id=1, source_target_pairs={{0,32},{32,0},{64,96},{96,64},{1,33},{33,1},{65,97},{97,65},{2,34}... | collective-permute-start | bytes 983048 | tf_op jit(solution)/shard_map/ppermute | solution.py:68
  1.8 11.8 %collective-permute-start.1 = (bf16[128,1280]{1,0:T(8,128)(2,1)S(1)}, bf16[128,1280]{1,0:T(8,128)(2,1)}, u32[]{:S(2)}, u32[]{:S(2)}) collective-permute-start(bf16[128,1280]{1,0:T(8,128)(2,1)S(1)} %pack.1.x0), channel_id=1, source_target_pairs={{0,64},{32,96},{64,0},{96,32},{1,65},{33,97},{65,1},{97,33},{2,66}... | collective-permute-start | bytes 983048 | tf_op jit(solution)/shard_map/ppermute | solution.py:68
  8.5 7.1 %copy-start.2 = (bf16[128]{0:T(256)(128)(2,1)S(1)}, bf16[128]{0:T(256)(128)(2,1)}, u32[]{:S(2)}) copy-start(bf16[128]{0:T(256)(128)(2,1)} %param.20) | copy-start | bytes 772
  8.5 7.1 %copy-start.3 = (bf16[128]{0:T(256)(128)(2,1)S(1)}, bf16[128]{0:T(256)(128)(2,1)}, u32[]{:S(2)}) copy-start(bf16[128]{0:T(256)(128)(2,1)} %param.19) | copy-start | bytes 772
  13.6 13.8 %copy-start = (f32[2,512]{1,0:T(2,128)S(1)}, f32[2,512]{1,0:T(2,128)}, u32[]{:S(2)}) copy-start(f32[2,512]{1,0:T(2,128)} %param.27) | copy-start | bytes 12292
  13.6 13.8 %copy-start.1 = (f32[2,512]{1,0:T(2,128)S(1)}, f32[2,512]{1,0:T(2,128)}, u32[]{:S(2)}) copy-start(f32[2,512]{1,0:T(2,128)} %param.24) | copy-start | bytes 12292
  13.6 5.8 %collective-permute-start.2 = (bf16[128,1280]{1,0:T(8,128)(2,1)}, bf16[128,1280]{1,0:T(8,128)(2,1)S(1)}, u32[]{:S(2)}, u32[]{:S(2)}) collective-permute-start(bf16[128,1280]{1,0:T(8,128)(2,1)} %after.1.x0), channel_id=1, source_target_pairs={{0,32},{32,0},{64,96},{96,64},{1,33},{33,1},{65,97},{97,65},{2,34}... | collective-permute-start | bytes 983048 | tf_op jit(solution)/shard_map/ppermute | solution.py:68
  13.7 13.6 %collective-permute-start.3 = (bf16[64,2048]{1,0:T(8,128)(2,1)}, bf16[64,2048]{1,0:T(8,128)(2,1)S(1)}, u32[]{:S(2)}, u32[]{:S(2)}) collective-permute-start(bf16[64,2048]{1,0:T(8,128)(2,1)} %get-tuple-element.47), channel_id=1, source_target_pairs={{0,8},{8,0},{16,24},{24,16},{1,9},{9,1},{17,25},{25,17},{2,10},{10... | collective-permute-start | bytes 786440 | tf_op jit(solution)/shard_map/ppermute | solution.py:68
  15.7 16.5 %collective-permute-start.4 = (bf16[64,2048]{1,0:T(8,128)(2,1)}, bf16[64,2048]{1,0:T(8,128)(2,1)S(1)}, u32[]{:S(2)}, u32[]{:S(2)}) collective-permute-start(bf16[64,2048]{1,0:T(8,128)(2,1)} %get-tuple-element.48), channel_id=1, source_target_pairs={{0,16},{8,24},{16,0},{24,8},{1,17},{9,25},{17,1},{25,9},{2,18},{10... | collective-permute-start | bytes 786440 | tf_op jit(solution)/shard_map/ppermute | solution.py:68
  19.3 16.2 %collective-permute-start.5 = (bf16[64,2048]{1,0:T(8,128)(2,1)}, bf16[64,2048]{1,0:T(8,128)(2,1)S(1)}, u32[]{:S(2)}, u32[]{:S(2)}) collective-permute-start(bf16[64,2048]{1,0:T(8,128)(2,1)} %get-tuple-element.49), channel_id=1, source_target_pairs={{0,24},{8,16},{16,8},{24,0},{1,25},{9,17},{17,9},{25,1},{2,26},{10... | collective-permute-start | bytes 786440 | tf_op jit(solution)/shard_map/ppermute | solution.py:68
  22.5 13.0 %collective-permute-start.6 = (bf16[64,2048]{1,0:T(8,128)(2,1)S(1)}, bf16[64,2048]{1,0:T(8,128)(2,1)S(1)}, u32[]{:S(2)}, u32[]{:S(2)}) collective-permute-start(bf16[64,2048]{1,0:T(8,128)(2,1)S(1)} %get-tuple-element.51), channel_id=1, source_target_pairs={{0,8},{8,0},{16,24},{24,16},{1,9},{9,1},{17,25},{25,17},{2,10},{10... | collective-permute-start | bytes 786440 | tf_op jit(solution)/shard_map/ppermute | solution.py:68
  22.6 20.5 %collective-permute-start.7 = (bf16[64,2048]{1,0:T(8,128)(2,1)S(1)}, bf16[64,2048]{1,0:T(8,128)(2,1)S(1)}, u32[]{:S(2)}, u32[]{:S(2)}) collective-permute-start(bf16[64,2048]{1,0:T(8,128)(2,1)S(1)} %get-tuple-element.52), channel_id=1, source_target_pairs={{0,16},{8,24},{16,0},{24,8},{1,17},{9,25},{17,1},{25,9},{2,18},{10... | collective-permute-start | bytes 786440 | tf_op jit(solution)/shard_map/ppermute | solution.py:68
  27.2 18.5 %collective-permute-start.8 = (bf16[64,2048]{1,0:T(8,128)(2,1)S(1)}, bf16[64,2048]{1,0:T(8,128)(2,1)S(1)}, u32[]{:S(2)}, u32[]{:S(2)}) collective-permute-start(bf16[64,2048]{1,0:T(8,128)(2,1)S(1)} %get-tuple-element.53), channel_id=1, source_target_pairs={{0,24},{8,16},{16,8},{24,0},{1,25},{9,17},{17,9},{25,1},{2,26},{10... | collective-permute-start | bytes 786440 | tf_op jit(solution)/shard_map/ppermute | solution.py:68
  48.2 16.1 %collective-permute-start.10 = (bf16[128,1024]{1,0:T(8,128)(2,1)S(1)}, bf16[128,1024]{1,0:T(8,128)(2,1)S(1)}, u32[]{:S(2)}, u32[]{:S(2)}) collective-permute-start(bf16[128,1024]{1,0:T(8,128)(2,1)S(1)} %get-tuple-element.54.s0), channel_id=1, source_target_pairs={{0,16},{8,24},{16,0},{24,8},{1,17},{9,25},{17,1},{25,9},{2,18},{10... | collective-permute-start | bytes 786440 | tf_op jit(solution)/shard_map/ppermute | solution.py:68
  48.2 16.1 %collective-permute-start.11 = (bf16[128,1024]{1,0:T(8,128)(2,1)S(1)}, bf16[128,1024]{1,0:T(8,128)(2,1)S(1)}, u32[]{:S(2)}, u32[]{:S(2)}) collective-permute-start(bf16[128,1024]{1,0:T(8,128)(2,1)S(1)} %get-tuple-element.54.s0), channel_id=1, source_target_pairs={{0,24},{8,16},{16,8},{24,0},{1,25},{9,17},{17,9},{25,1},{2,26},{10... | collective-permute-start | bytes 786440 | tf_op jit(solution)/shard_map/ppermute | solution.py:68
  49.5 14.9 %collective-permute-start.9 = (bf16[128,1024]{1,0:T(8,128)(2,1)S(1)}, bf16[128,1024]{1,0:T(8,128)(2,1)S(1)}, u32[]{:S(2)}, u32[]{:S(2)}) collective-permute-start(bf16[128,1024]{1,0:T(8,128)(2,1)S(1)} %get-tuple-element.54.s0), channel_id=1, source_target_pairs={{0,8},{8,0},{16,24},{24,16},{1,9},{9,1},{17,25},{25,17},{2,10},{10... | collective-permute-start | bytes 786440 | tf_op jit(solution)/shard_map/ppermute | solution.py:68
  67.3 13.4 %all-to-all-start.2 = ((bf16[8,48,512]{2,1,0:T(8,128)(2,1)}), bf16[8,48,512]{2,1,0:T(8,128)(2,1)S(1)}, u32[]{:S(2)}, u32[]{:S(2)}) async-start(bf16[8,48,512]{2,1,0:T(8,128)(2,1)} %get-tuple-element.61), calls=%async_computation.2 | async-start | bytes 786432 | tf_op jit(solution)/shard_map/all_to_all | solution.py:398
  80.7 21.9 %all-to-all-start.1 = ((bf16[8,128,512]{2,1,0:T(8,128)(2,1)}), bf16[8,128,512]{2,1,0:T(8,128)(2,1)S(1)}, u32[]{:S(2)}, u32[]{:S(2)}) async-start(bf16[8,128,512]{2,1,0:T(8,128)(2,1)} %grads.1), calls=%async_computation.1 | async-start | bytes 2097152 | tf_op jit(solution)/shard_map/all_to_all | solution.py:403
  85.6 1.5 %collective-permute-start.12 = (f32[392,128]{1,0:T(8,128)S(1)}, f32[392,128]{1,0:T(8,128)S(1)}, u32[]{:S(2)}, u32[]{:S(2)}) collective-permute-start(f32[392,128]{1,0:T(8,128)S(1)} %get-tuple-element.65), channel_id=1, source_target_pairs={{0,32},{32,0},{64,96},{96,64},{1,33},{33,1},{65,97},{97,65},{2,34}... | collective-permute-start | bytes 602120 | tf_op jit(solution)/shard_map/ppermute | solution.py:68
  87.1 15.5 %collective-permute-start.13 = (f32[256,128]{1,0:T(8,128)S(1)}, f32[256,128]{1,0:T(8,128)S(1)}, u32[]{:S(2)}, u32[]{:S(2)}) collective-permute-start(f32[256,128]{1,0:T(8,128)S(1)} %get-tuple-element.66.high), channel_id=1, source_target_pairs={{0,64},{32,96},{64,0},{96,32},{1,65},{33,97},{65,1},{97,33},{2,66}... | collective-permute-start | bytes 393224 | tf_op jit(solution)/shard_map/ppermute | solution.py:68
  89.9 12.7 %collective-permute-start.14 = (f32[128,128]{1,0:T(8,128)S(1)}, f32[128,128]{1,0:T(8,128)S(1)}, u32[]{:S(2)}, u32[]{:S(2)}) collective-permute-start(f32[128,128]{1,0:T(8,128)S(1)} %get-tuple-element.67.low), channel_id=1, source_target_pairs={{0,4},{1,5},{2,6},{3,7},{4,0},{5,1},{6,2},{7,3},{8,12},{9,13},{10,... | collective-permute-start | bytes 196616 | tf_op jit(solution)/shard_map/ppermute | solution.py:68
  91.2 11.3 %collective-permute-start.15 = (f32[128,128]{1,0:T(8,128)S(1)}, f32[128,128]{1,0:T(8,128)S(1)}, u32[]{:S(2)}, u32[]{:S(2)}) collective-permute-start(f32[128,128]{1,0:T(8,128)S(1)} %get-tuple-element.67.low), channel_id=1, source_target_pairs={{0,68},{1,69},{2,70},{3,71},{4,64},{5,65},{6,66},{7,67},{32,100},{... | collective-permute-start | bytes 196616 | tf_op jit(solution)/shard_map/ppermute | solution.py:415
  102.6 10.7 %copy-start.4 = (s32[128]{0:T(128)S(1)}, s32[128]{0:T(128)}, u32[]{:S(2)}) copy-start(s32[128]{0:T(128)} %param.21) | copy-start | bytes 1540
  103.7 22.1 %all-to-all-start.3 = ((bf16[8,128,512]{2,1,0:T(8,128)(2,1)}), bf16[8,128,512]{2,1,0:T(8,128)(2,1)S(1)}, u32[]{:S(2)}, u32[]{:S(2)}) async-start(bf16[8,128,512]{2,1,0:T(8,128)(2,1)} %total.1), calls=%async_computation.3 | async-start | bytes 2097152 | tf_op jit(solution)/shard_map/all_to_all | solution.py:421
  107.7 4.3 %collective-permute-start.19 = (f32[136,128]{1,0:T(8,128)S(1)}, f32[136,128]{1,0:T(8,128)S(1)}, u32[]{:S(2)}, u32[]{:S(2)}) collective-permute-start(f32[136,128]{1,0:T(8,128)S(1)} %get-tuple-element.72), channel_id=1, source_target_pairs={{0,8},{8,0},{16,24},{24,16},{1,9},{9,1},{17,25},{25,17},{2,10},{10... | collective-permute-start | bytes 208904 | tf_op jit(solution)/shard_map/ppermute | solution.py:68
  112.0 6.1 %collective-permute-start.20 = (f32[136,128]{1,0:T(8,128)S(1)}, f32[136,128]{1,0:T(8,128)S(1)}, u32[]{:S(2)}, u32[]{:S(2)}) collective-permute-start(f32[136,128]{1,0:T(8,128)S(1)} %add.15), channel_id=1, source_target_pairs={{0,16},{8,24},{16,0},{24,8},{1,17},{9,25},{17,1},{25,9},{2,18},{10... | collective-permute-start | bytes 208904 | tf_op jit(solution)/shard_map/ppermute | solution.py:68
  113.3 10.2 %collective-permute-start.16 = (bf16[2,32,512]{2,1,0:T(8,128)(2,1)S(1)}, bf16[2,32,512]{2,1,0:T(8,128)(2,1)S(1)}, u32[]{:S(2)}, u32[]{:S(2)}) collective-permute-start(bf16[2,32,512]{2,1,0:T(8,128)(2,1)S(1)} %get-tuple-element.69.pair.g0), channel_id=1, source_target_pairs={{0,1},{1,0},{2,3},{3,2},{4,5},{5,4},{6,7},{7,6},{8,9},{9,8},{10,11... | collective-permute-start | bytes 196616 | tf_op jit(solution)/shard_map/ppermute | solution.py:68
  115.3 10.4 %collective-permute-start.17 = (bf16[2,32,512]{2,1,0:T(8,128)(2,1)S(1)}, bf16[2,32,512]{2,1,0:T(8,128)(2,1)S(1)}, u32[]{:S(2)}, u32[]{:S(2)}) collective-permute-start(bf16[2,32,512]{2,1,0:T(8,128)(2,1)S(1)} %get-tuple-element.69.pair.g0), channel_id=1, source_target_pairs={{0,2},{1,3},{2,0},{3,1},{4,6},{5,7},{6,4},{7,5},{8,10},{9,11},{10,... | collective-permute-start | bytes 196616 | tf_op jit(solution)/shard_map/ppermute | solution.py:68
  118.0 7.7 %collective-permute-start.18 = (bf16[2,32,512]{2,1,0:T(8,128)(2,1)S(1)}, bf16[2,32,512]{2,1,0:T(8,128)(2,1)S(1)}, u32[]{:S(2)}, u32[]{:S(2)}) collective-permute-start(bf16[2,32,512]{2,1,0:T(8,128)(2,1)S(1)} %get-tuple-element.69.pair.g0), channel_id=1, source_target_pairs={{0,3},{1,2},{2,1},{3,0},{4,7},{5,6},{6,5},{7,4},{8,11},{9,10},{10,... | collective-permute-start | bytes 196616 | tf_op jit(solution)/shard_map/ppermute | solution.py:68

commit v4 on v2

--- a/solution.py
+++ b/solution.py
@@ -14,19 +14,16 @@
 f32 = jnp.float32
 
 SPECS = {m: pl.BlockSpec(memory_space=m) for m in (pltpu.VMEM, pltpu.SMEM, pltpu.HBM)}
-ANY = pl.BlockSpec(memory_space=pl.ANY)
 DMA = pltpu.SemaphoreType.DMA
 VMEM, HBM = pltpu.VMEM, pltpu.HBM
 
 
 def call(
     body, outs, ins, scratch=(), scalars=None, mib=16, flops=0, name=None,
-    where=(), to=(), raw=(), aliases=None,
+    where=(), to=(), raw=(), raw_out=(), aliases=None,
 ):
     moved = sum(a.size * a.dtype.itemsize for a in ins)
     moved += sum(o.size * o.dtype.itemsize for o in outs)
-    raw_out = to == "raw"
-    to = range(len(outs)) if raw_out else to
     specs = [SPECS[HBM if i in raw else VMEM] for i in range(len(ins))]
     ins = [
         pltpu.with_memory_space_constraint(a, HBM) if i in raw or i in where else a
@@ -39,7 +36,7 @@
         body,
         out_shape=tuple(HBM(o.shape, o.dtype) if i in to else o for i, o in enumerate(outs)),
         in_specs=specs,
-        out_specs=tuple(SPECS[HBM if raw_out else VMEM] for _ in outs),
+        out_specs=tuple(SPECS[HBM if i in raw_out else VMEM] for i in range(len(outs))),
         scratch_shapes=list(scratch),
         input_output_aliases=aliases or {},
         compiler_params=pltpu.CompilerParams(vmem_limit_bytes=mib * 2**20),
@@ -51,12 +48,12 @@
 def after(x, other):
     return pl.pallas_call(
         lambda x, other, out: None,
-        out_shape=jax.ShapeDtypeStruct(x.shape, x.dtype),
-        in_specs=[ANY, ANY],
-        out_specs=ANY,
+        out_shape=HBM(x.shape, x.dtype),
+        in_specs=[SPECS[HBM], SPECS[HBM]],
+        out_specs=SPECS[HBM],
         input_output_aliases={0: 0},
         name="after",
-    )(x, other)
+    )(pltpu.with_memory_space_constraint(x, HBM), pltpu.with_memory_space_constraint(other, HBM))
 
 
 def shape(*dims, dtype=bf16):
@@ -169,7 +166,7 @@
     out, keep, give, terr,
     delta, slope0, grad, errs,
 ):
-    core, col, y_hi, dp = at[0], at[1], at[2], at[3]
+    core, col, y_hi = at[0], at[1], at[2]
     for c in range(4):
         v = (got[c] + got[4 + c]) + (got[8 + c] + got[12 + c])
         lanes = slice(64 * (c % 2), 64 * (c % 2) + 64)
@@ -199,7 +196,6 @@
             ]
     for q in range(2):
         grad[q] = dot(left1[q], delta[q, 0:256]) + dot(left2[q], delta[q, 256:512])
-    tail = jnp.concatenate([*heads, jnp.zeros((14, 512), f32)], axis=0).astype(bf16)
     for d in range(8):
         wide = slice(64 * d, 64 * d + 64)
         thin = slice(512 + 16 * d, 528 + 16 * d)
@@ -207,41 +203,62 @@
         out[d, 64:128, :] = grad[1, wide, :].astype(bf16)
         out[d, 128:144, :] = grad[0, thin, :].astype(bf16)
         out[d, 144:160, :] = grad[1, thin, :].astype(bf16)
-        out[d, 160:176, :] = tail
     push = dot(slope0[...], p[...])
-    first, second = push[0:128], push[128:256]
-    keep[0] = jnp.where(core == 1, second, first)
-    give[0] = jnp.where(core == 1, first, second)
-    first, second = push[256:384], push[384:512]
-    keep[1] = jnp.where(core == 1, second, first)
-    give[1] = jnp.where(core == 1, first, second)
-
-
-def total_body(got, w, chunk0, chunk1, act, head):
-    def at(rows):
-        x = [got[d, rows, :].astype(f32) for d in range(8)]
-        return ((x[0] + x[1]) + (x[2] + x[3])) + ((x[4] + x[5]) + (x[6] + x[7]))
-
-    total = at(slice(0, 64)).astype(bf16)
+    for chip in range(2):
+        first, second = push[256 * chip : 256 * chip + 128], push[256 * chip + 128 : 256 * chip + 256]
+        rows = slice(128 * chip, 128 * chip + 128)
+        keep[rows, :] = jnp.where(core == 1, second, first)
+        give[rows, :] = jnp.where(core == 1, first, second)
+    for q in range(2):
+        for j in range(4):
+            i = 256 + 4 * q + j
+            keep[i : i + 1, :] = heads[q][:, 128 * j : 128 * j + 128]
+    give[256:264, :] = jnp.zeros((8, 128), f32)
+
+
+def summed(got, rows):
+    x = [got[d, rows, :].astype(f32) for d in range(8)]
+    return ((x[0] + x[1]) + (x[2] + x[3])) + ((x[4] + x[5]) + (x[6] + x[7]))
+
+
+def action_body(got, w, t, act):
+    for q in range(2):
+        m = summed(got, slice(128 + 16 * q, 144 + 16 * q)).astype(bf16)
+        term = lax.dot_general(m, w[q], (((1,), (1,)), ((), ())), preferred_element_type=f32)
+        for j in range(4):
+            i = 16 * (4 * q + j)
+            act[i : i + 16, :] = term[:, 128 * j : 128 * j + 128]
+
+
+def fold_body(act, other, t, high):
+    high[0:128, :] = act[...] + other[...]
+    high[128:256, :] = t[128:256, :]
+
+
+def first_body(got, act, chunk):
+    total = summed(got, slice(0, 64)).astype(bf16)
     for d in range(8):
-        chunk0[d] = total
-    chunk1[...] = at(slice(64, 128)).astype(bf16)
-    head[...] = at(slice(160, 168))
+        chunk[d] = total
+
+
+def second_body(got, high, from_high, t, chunk):
+    total = summed(got, slice(64, 128)).astype(bf16)
+    act = (high[0:128, :] + from_high[0:128, :]).astype(bf16)
+    lines = []
     for q in range(2):
-        m = at(slice(128 + 16 * q, 144 + 16 * q)).astype(bf16)
-        act[16 * q : 16 * q + 16, :] = lax.dot_general(
-            m, w[q], (((1,), (1,)), ((), ())), preferred_element_type=f32
-        )
-
-
-def second_body(chunk1, act1, act2, out):
-    act = (act1[...] + act2[...]).astype(bf16)
+        line = jnp.concatenate([t[256 + 4 * q + j : 257 + 4 * q + j, :] for j in range(4)], axis=1)
+        lines.append(jnp.broadcast_to(line, (8, 512)))
+    heads = jnp.concatenate(lines, axis=0).astype(bf16)
     for d in range(8):
-        out[d, 0:64, :] = chunk1[...]
-        out[d, 64:96, :] = act
-
-
-def renew(q, g, cin, tin, fresh, blended, c, t, isems, osems):
+        chunk[d, 0:64, :] = total
+        for q in range(2):
+            for j in range(4):
+                i = 16 * (4 * q + j)
+                chunk[d, 64 + 16 * q : 80 + 16 * q, 128 * j : 128 * j + 128] = act[i : i + 16, :]
+        chunk[d, 96:112, :] = heads
+
+
+def renew(q, g, cin, tin, fresh, blended, c, t, isems, osems, between=None):
     ins, outs = [], []
     for h in range(2):
         rows = slice(256 * h, 256 * h + 256)
@@ -249,36 +266,33 @@
         ins.append(pltpu.make_async_copy(tin.at[q, rows], t.at[rows], isems.at[1, h]))
         outs.append(pltpu.make_async_copy(c.at[rows], fresh.at[q, rows], osems.at[0, h]))
         outs.append(pltpu.make_async_copy(t.at[rows], blended.at[q, rows], osems.at[1, h]))
-
-    def work(h):
-        for d in range(4 * h, 4 * h + 4):
-            at = slice(64 * d, 64 * d + 64)
-            new = c[at, :] - matrix_rate * g[d, 0:64, :].astype(f32)
-            c[at, :] = new
-            t[at, :] = blend_rate * new + (1.0 - blend_rate) * t[at, :]
-
-    return ins, outs, work
-
-
-def update0_body(g, cin, tin, fresh, blended, c, t, isems, osems):
-    ins, outs, work = renew(0, g, cin, tin, fresh, blended, c, t, isems, osems)
     for copy in ins:
         copy.start()
     for h in range(2):
         ins[2 * h].wait()
         ins[2 * h + 1].wait()
-        work(h)
+        for d in range(4 * h, 4 * h + 4):
+            part = slice(64 * d, 64 * d + 64)
+            new = c[part, :] - matrix_rate * g[d, 0:64, :].astype(f32)
+            c[part, :] = new
+            t[part, :] = blend_rate * new + (1.0 - blend_rate) * t[part, :]
         outs[2 * h].start()
         outs[2 * h + 1].start()
+    if between is not None:
+        between()
     for copy in outs:
         copy.wait()
 
 
-def update1_body(
-    g, cin, tin, cact, tact, fresh0, blended0, fresh, blended, fresh_act, blended_act,
+def update_first_body(g, cin, tin, fresh, blended, c, t, isems, osems):
+    renew(0, g, cin, tin, fresh, blended, c, t, isems, osems)
+
+
+def update_second_body(
+    g, chead, thead, cin, tin, cact, tact, fresh0, blended0,
+    fresh, blended, fresh_act, blended_act, fresh_head, blended_head,
     c, t, ca, ta, isems, osems, asems,
 ):
-    ins, outs, work = renew(1, g, cin, tin, fresh, blended, c, t, isems, osems)
     more = [
         pltpu.make_async_copy(cact, ca, asems.at[0]),
         pltpu.make_async_copy(tact, ta, asems.at[1]),
@@ -287,26 +301,29 @@
         pltpu.make_async_copy(ca, fresh_act, asems.at[2]),
         pltpu.make_async_copy(ta, blended_act, asems.at[3]),
     ]
-    for copy in ins + more:
+    for copy in more:
         copy.start()
-    for h in range(2):
-        ins[2 * h].wait()
-        ins[2 * h + 1].wait()
-        work(h)
-        outs[2 * h].start()
-        outs[2 * h + 1].start()
-    for copy in more:
-        copy.wait()
-    for d in range(8):
-        for q in range(2):
+    for q in range(2):
+        total = summed(g, slice(96 + 8 * q, 104 + 8 * q))
+        new = chead[q : q + 1, :] - head_rate * total[0:1, :]
+        fresh_head[q : q + 1, :] = new
+        blended_head[q : q + 1, :] = blend_rate * new + (1.0 - blend_rate) * thead[q : q + 1, :]
+
+    def action_part():
+        for copy in more:
+            copy.wait()
+        for d in range(8):
             rows = slice(16 * d, 16 * d + 16)
-            term = g[d, 64 + 16 * q : 80 + 16 * q, :].astype(f32)
-            new = ca[q, rows, :] - matrix_rate * term
-            ca[q, rows, :] = new
-            ta[q, rows, :] = blend_rate * new + (1.0 - blend_rate) * ta[q, rows, :]
+            for q in range(2):
+                part = g[d, 64 + 16 * q : 80 + 16 * q, :].astype(f32)
+                new = ca[q, rows, :] - matrix_rate * part
+                ca[q, rows, :] = new
+                ta[q, rows, :] = blend_rate * new + (1.0 - blend_rate) * ta[q, rows, :]
+        for copy in last:
+            copy.start()
+
+    renew(1, g, cin, tin, fresh, blended, c, t, isems, osems, action_part)
     for copy in last:
-        copy.start()
-    for copy in outs + last:
         copy.wait()
 
 
@@ -346,7 +363,7 @@
         mib=16, flops=2 * 128 * 512 * 512, raw=range(4), to=(2,), name="weights",
     )
 
-    def forward(x0, x1, name):
+    def forward(x0, x1, name, where, to):
         return call(
             forward_body,
             [
@@ -355,16 +372,16 @@
             ],
             [x0, x1, a16, w16],
             scratch=[pltpu.VMEM((256, 1280), bf16), pltpu.VMEM((256, 2048), f32)],
-            scalars=at, flops=8 * 256 * 640 * 512, to=range(5), name=name,
+            scalars=at, flops=8 * 256 * 640 * 512, where=where, to=to, name=name,
         )
 
-    mine1, *out1, left1 = forward(own, sib, "forward_near")
+    mine1, *out1, left1 = forward(own, sib, "forward_near", (), range(5))
     in1 = [None, None, None]
     for k in (2, 1, 3):
         in1[k - 1] = swap(out1[k - 1], "col", k)
     far = after(far, mine1)
     farsib = swap(far, "row", 1)
-    mine2, *out2, left2 = forward(far, farsib, "forward_far")
+    mine2, *out2, left2 = forward(far, farsib, "forward_far", (0,), (0, 4))
     in2 = [None, None, None]
     for k in (2, 1, 3):
         in2[k - 1] = swap(out2[k - 1], "col", k)
@@ -378,59 +395,60 @@
         [shape(128, 1024), shape(128, 1024, dtype=f32), shape(16, 8, 128, dtype=f32)],
         [mine1, *in1, mine2, *in2, heads, rew],
         scratch=[pltpu.VMEM((128, 128), f32)],
-        scalars=at, where=(0, 4), to=range(3), name="hidden", flops=128 * 2048 * 30,
+        scalars=at, where=(0, 4), to=(1,), name="hidden", flops=128 * 2048 * 30,
     )
     slopes = [slope] + [swap(slope, "col", k) for k in (1, 2, 3)]
     got = lax.all_to_all(packet, ("row", "col"), 0, 0, tiled=True)
     grads, keep, give, temporal_errors = call(
         grads_body,
         [
-            shape(8, 176, 512), shape(2, 128, 128, dtype=f32),
-            shape(2, 128, 128, dtype=f32), shape(2, 128, dtype=f32),
+            shape(8, 160, 512), shape(264, 128, dtype=f32),
+            shape(264, 128, dtype=f32), shape(2, 128, dtype=f32),
         ],
         [*slopes, got, left1, left2, hidden, p16],
         scratch=[
             pltpu.VMEM((2, 512, 512), bf16), pltpu.VMEM((512, 512), bf16),
             pltpu.VMEM((2, 640, 512), f32), pltpu.VMEM((4, 8, 128), f32),
         ],
-        scalars=at, where=(0, 5, 6, 7, 8), to=range(4), name="grads", flops=4 * 640 * 512 * 512,
+        scalars=at, where=(5, 6, 7, 8), to=range(4), name="grads", flops=4 * 640 * 512 * 512,
     )
     parts = lax.all_to_all(grads, "dp", 0, 0, tiled=True)
-    push = keep + swap(give, "row", 1)
-    push = push[0] + swap(push[1], "row", 2)
-
-    chunk0, chunk1, act, head = call(
-        total_body,
-        [shape(8, 64, 512), shape(64, 512), shape(32, 512, dtype=f32), shape(8, 512, dtype=f32)],
-        [parts, w16], to=range(4), name="total", flops=4 * 16 * 512 * 512,
-    )
+    t = keep + swap(give, "row", 1)
+    t = t + swap(t, "col", 1)
+    t = t + swap(t, "col", 2)
+
+    (act,) = call(
+        action_body, [shape(128, 128, dtype=f32)], [parts, w16, t],
+        to=(0,), name="action", flops=4 * 16 * 512 * 512,
+    )
+    (chunk0,) = call(first_body, [shape(8, 64, 512)], [parts, act], where=(1,), to=(0,), name="first")
     grad0 = lax.all_to_all(chunk0, "dp", 0, 0, tiled=True)
-    act = act + swap(act, "row", 1)
+    (high,) = call(
+        fold_body, [shape(256, 128, dtype=f32)], [act, swap(act, "row", 1), t], where=(0,), name="fold"
+    )
+    from_high = swap(high, "row", 2)
     (chunk1,) = call(
-        second_body, [shape(8, 96, 512)], [chunk1, act, swap(act, "row", 2)],
-        where=(0,), to=(0,), name="second",
+        second_body, [shape(8, 112, 512)], [parts, high, from_high, t], to=(0,), name="second"
     )
     grad1 = lax.all_to_all(chunk1, "dp", 0, 0, tiled=True)
-    both = jnp.concatenate([push, head[0:2].reshape(8, 128)], axis=0)
-    both = both + swap(both, "col", 1)
-    both = both + swap(both, "col", 2)
-    action_slope = actor_flags.astype(f32)[:, None] * both[0:128]
-    head = both[128:136].reshape(2, 512)
-    wide, thin = shape(2, 512, 512, dtype=f32), shape(2, 128, 512, dtype=f32)
+    action_slope = actor_flags.astype(f32)[:, None] * (t[0:128] + from_high[128:256])
+    wide, thin, line = shape(2, 512, 512, dtype=f32), shape(2, 128, 512, dtype=f32), shape(2, 512, dtype=f32)
     big, small = pltpu.VMEM((512, 512), f32), pltpu.VMEM((2, 128, 512), f32)
     new_in, new_target_in = call(
-        update0_body, [wide, wide], [grad0, critic_in, target_in],
+        update_first_body, [wide, wide], [grad0, critic_in, target_in],
         scratch=[big, big, DMA((2, 2)), DMA((2, 2))],
-        raw=(1, 2), to="raw", mib=8, name="update_first",
-    )
-    new_in, new_target_in, new_act, new_target_act = call(
-        update1_body, [wide, wide, thin, thin],
-        [grad1, critic_in, target_in, critic_act, target_act, new_in, new_target_in],
+        raw=(1, 2), raw_out=range(2), to=range(2), mib=8, name="update_first",
+    )
+    new_in, new_target_in, new_act, new_target_act, new_head, new_target_head = call(
+        update_second_body, [wide, wide, thin, thin, line, line],
+        [
+            grad1, critic_head, target_head,
+            critic_in, target_in, critic_act, target_act, new_in, new_target_in,
+        ],
         scratch=[big, big, small, small, DMA((2, 2)), DMA((2, 2)), DMA((4,))],
-        raw=range(1, 7), to="raw", mib=8, aliases={5: 0, 6: 1}, name="update_second",
-    )
-    new_head = critic_head - head_rate * head
-    new_target_head = blend_rate * new_head + (1.0 - blend_rate) * target_head
+        where=(1, 2), raw=range(3, 9), raw_out=range(4), to=range(6), mib=8,
+        aliases={7: 0, 8: 1}, name="update_second",
+    )
     return (
         new_in,
         new_act,

time: 137 us -> 136 us (level)
  waiting for transfers between devices: 46 us -> 55 us
  other arithmetic: 5.67 us -> 1 us
  starting transfers between devices: 40.9 us -> 36.3 us
  Pallas kernels: 27 us -> 29.6 us
  local copies, waits for them, and re-layouts: 2.63 us -> 0.18 us
    ppermute x18 -> x17, waiting for transfers between devices: 34.5 us -> 39.7 us  [swap(): return lax.ppermute(x, axis, [(i, i ^ bit) for i in range(n)])]
    add x6 -> x3, other arithmetic: 3.88 us -> 0.05 us  [the longest x1 0.02 us: on_device(): t = keep + swap(give, 'row', 1)]
    pallas_call x10 -> x12, Pallas kernels: 27 us -> 29.6 us  [call(): pl.pallas_call(body, out_shape=tuple((HBM(o.shape, o.dtype) if i in to el...]
    ppermute x18 -> x17, starting transfers between devices: 26.7 us -> 24.1 us  [swap(): return lax.ppermute(x, axis, [(i, i ^ bit) for i in range(n)])]
    all_to_all x1, starting transfers between devices: 6 us -> 3.49 us  [on_device(): grad0 = lax.all_to_all(chunk0, 'dp', 0, 0, tiled=True)]
    all_to_all x1, waiting for transfers between devices: 2.68 us -> 4.71 us  [on_device(): parts = lax.all_to_all(grads, 'dp', 0, 0, tiled=True)]
    all_to_all x1, waiting for transfers between devices: 8.84 us -> 10.6 us  [on_device(): grad1 = lax.all_to_all(chunk1, 'dp', 0, 0, tiled=True)]
    unnamed x14, local copies, waits for them, and re-layouts: 1.71 us -> 0.03 us
  transfers between devices with their start and end apart: 21 -> 20, of which waited for: 11 -> 12; matrix products, arithmetic and copies ran while one was open for 4% -> 1% of each run, Pallas kernels for 11% -> 11%
where the time goes in v4:
time: 136 us; the launch traced here: 135 us
  waiting for transfers between devices  55 us (40%)
  starting transfers between devices  36.3 us (27%)
  Pallas kernels  29.6 us (22%)
  blocking collectives  12 us (9%)
    ppermute x17, waiting for transfers between devices, swap(): return lax.ppermute(x, axis, [(i, i ^ bit) for i in range(n)])  39.7 us
    pallas_call x12, Pallas kernels, call(): pl.pallas_call(body, out_shape=tuple((HBM(o.shape, o.dtype) if i in to el...  29.6 us
    ppermute x17, starting transfers between devices, swap(): return lax.ppermute(x, axis, [(i, i ^ bit) for i in range(n)])  24.1 us
    all_to_all x1, blocking collectives, on_device(): got = lax.all_to_all(packet, ('row', 'col'), 0, 0, tiled=True)  12 us
    all_to_all x1, waiting for transfers between devices, on_device(): grad1 = lax.all_to_all(chunk1, 'dp', 0, 0, tiled=True)  10.6 us
    all_to_all x1, waiting for transfers between devices, on_device(): parts = lax.all_to_all(grads, 'dp', 0, 0, tiled=True)  4.71 us
    all_to_all x1, starting transfers between devices, on_device(): parts = lax.all_to_all(grads, 'dp', 0, 0, tiled=True)  4.69 us
    all_to_all x1, starting transfers between devices, on_device(): grad1 = lax.all_to_all(chunk1, 'dp', 0, 0, tiled=True)  4.04 us
  transfers between devices with their start and end apart: 20, of which 12 were waited for; matrix products, arithmetic and copies ran while one was open for 1% of the time, Pallas kernels for 11%

profile of v4, /device:TPU:0, one launch (start us, length us, event | category | flops | bytes accessed | tf_op | source)
XLA Modules:
  0.0 134.9 jit_solution(13346700572353714985)
XLA Ops:
  0.6 1.1 pack.1.x0
  1.7 0.1 collective-permute-start
  1.8 3.4 %collective-permute-start.4 = (bf16[128,1280]{1,0:T(8,128)(2,1)S(1)}, bf16[128,1280]{1,0:T(8,128)(2,1)}, u32[]{:S(2)}, u32[]{:S(2)}) collective-permute-start(bf16[128,1280]{1,0:T(8,128)(2,1)S(1)} %pack.1.x0), channel_id=1, source_target_pairs={{0,64},{32,96},{64,0},{96,32},{1,65},{33,97},{65,1},{97,33},{2,66}... | collective-permute-start | bytes 983048 | tf_op jit(solution)/shard_map/ppermute | solution.py:69
  5.2 0.1 pad.3.clone
  5.2 3.2 %weights.1 = (bf16[4,512,512]{2,1,0:T(8,128)(2,1)S(1)}, bf16[4,128,512]{2,1,0:T(8,128)(2,1)S(1)}, bf16[512,128]{1,0:T(8,128)(2,1)}) custom-call(f32[2,512,512]{2,1,0:T(8,128)} %cin.5, f32[2,512,512]{2,1,0:T(8,128)} %tin.5, f32[2,128,512]{2,1,0:T(8,128)} %cact.3, f32[2,128,512]{2,1,0:T(8,128)} %tact.3), custom_call_target="tpu_custom_call" | custom-call | flops 67108864 | bytes 7995392 | tf_op jit(solution)/shard_map/weights/pallas_call | solution.py:35
  8.5 0.1 pad_add_fusion.at
  8.6 0.0 collective-permute-done.x1
  8.6 3.1 %forward_near.1 = (f32[64,2048]{1,0:T(8,128)}, bf16[64,2048]{1,0:T(8,128)(2,1)}, bf16[64,2048]{1,0:T(8,128)(2,1)}, bf16[64,2048]{1,0:T(8,128)(2,1)}, bf16[2,640,256]{2,1,0:T(8,128)(2,1)}) custom-call(s32[4]{0:T(128)S(1)} %pad_add_fusion.at, bf16[128,1280]{1,0:T(8,128)(2,1)S(1)} %pack.1.x0, bf16[128,1280]{1,0:T(8,128)(2,1)S(1)} %collective-permute-done.x1, ...), custom_call_target="tpu_custom_call" | custom-call | flops 671088640 | bytes 5242880 | tf_op jit(solution)/shard_map/forward_near/pallas_call | solution.py:35
  11.7 1.9 %collective-permute-done.4.x = bf16[128,1280]{1,0:T(8,128)(2,1)} collective-permute-done((bf16[128,1280]{1,0:T(8,128)(2,1)S(1)}, bf16[128,1280]{1,0:T(8,128)(2,1)}, u32[]{:S(2)}, u32[]{:S(2)}) %collective-permute-start.4) | collective-permute-done | bytes 327712 | tf_op jit(solution)/shard_map/ppermute | solution.py:69
  13.6 0.0 collective-permute-start.5
  13.6 0.1 fusion.1
  13.7 2.0 %collective-permute-start.1 = (bf16[64,2048]{1,0:T(8,128)(2,1)}, bf16[64,2048]{1,0:T(8,128)(2,1)S(1)}, u32[]{:S(2)}, u32[]{:S(2)}) collective-permute-start(bf16[64,2048]{1,0:T(8,128)(2,1)} %get-tuple-element.39), channel_id=1, source_target_pairs={{0,8},{8,0},{16,24},{24,16},{1,9},{9,1},{17,25},{25,17},{2,10},{10... | collective-permute-start | bytes 786440 | tf_op jit(solution)/shard_map/ppermute | solution.py:69
  15.7 0.0 copy-done.4
  15.7 0.0 copy-done.5
  15.7 3.7 %collective-permute-start.2 = (bf16[64,2048]{1,0:T(8,128)(2,1)}, bf16[64,2048]{1,0:T(8,128)(2,1)S(1)}, u32[]{:S(2)}, u32[]{:S(2)}) collective-permute-start(bf16[64,2048]{1,0:T(8,128)(2,1)} %get-tuple-element.40), channel_id=1, source_target_pairs={{0,16},{8,24},{16,0},{24,8},{1,17},{9,25},{17,1},{25,9},{2,18},{10... | collective-permute-start | bytes 786440 | tf_op jit(solution)/shard_map/ppermute | solution.py:69
  19.3 0.0 collective-permute-start.3
  19.3 0.0 collective-permute-done.5.x1
  19.3 3.4 %forward_far.1 = (f32[64,2048]{1,0:T(8,128)}, bf16[64,2048]{1,0:T(8,128)(2,1)S(1)}, bf16[64,2048]{1,0:T(8,128)(2,1)S(1)}, bf16[64,2048]{1,0:T(8,128)(2,1)S(1)}, bf16[2,640,256]{2,1,0:T(8,128)(2,1)}) custom-call(s32[4]{0:T(128)S(1)} %pad_add_fusion.at, bf16[128,1280]{1,0:T(8,128)(2,1)} %after.1.x0, bf16[128,1280]{1,0:T(8,128)(2,1)S(1)} %collective-permute-done.5.x1, ...), custom_call_target="tpu_custom_call" | custom-call | flops 671088640 | bytes 5242880 | tf_op jit(solution)/shard_map/forward_far/pallas_call | solution.py:35
  22.8 0.1 collective-permute-start.6
  22.8 4.6 %collective-permute-start.7 = (bf16[64,2048]{1,0:T(8,128)(2,1)S(1)}, bf16[64,2048]{1,0:T(8,128)(2,1)S(1)}, u32[]{:S(2)}, u32[]{:S(2)}) collective-permute-start(bf16[64,2048]{1,0:T(8,128)(2,1)S(1)} %get-tuple-element.44), channel_id=1, source_target_pairs={{0,16},{8,24},{16,0},{24,8},{1,17},{9,25},{17,1},{25,9},{2,18},{10... | collective-permute-start | bytes 786440 | tf_op jit(solution)/shard_map/ppermute | solution.py:69
  27.5 0.0 collective-permute-done.1.r11
  27.5 0.0 collective-permute-start.8
  27.5 0.1 maximum_maximum_fusion.1.rew
  27.5 0.0 copy-done.2
  27.5 0.1 maximum_maximum_fusion.heads
  27.6 4.6 %collective-permute-done.2.r12 = bf16[64,2048]{1,0:T(8,128)(2,1)S(1)} collective-permute-done((bf16[64,2048]{1,0:T(8,128)(2,1)}, bf16[64,2048]{1,0:T(8,128)(2,1)S(1)}, u32[]{:S(2)}, u32[]{:S(2)}) %collective-permute-start.2) | collective-permute-done | bytes 262176 | tf_op jit(solution)/shard_map/ppermute | solution.py:69
  32.2 3.4 %collective-permute-done.3.r13 = bf16[64,2048]{1,0:T(8,128)(2,1)S(1)} collective-permute-done((bf16[64,2048]{1,0:T(8,128)(2,1)}, bf16[64,2048]{1,0:T(8,128)(2,1)S(1)}, u32[]{:S(2)}, u32[]{:S(2)}) %collective-permute-start.3) | collective-permute-done | bytes 262176 | tf_op jit(solution)/shard_map/ppermute | solution.py:69
  35.6 0.0 collective-permute-done.6.r21
  35.6 7.6 %collective-permute-done.7.r22 = bf16[64,2048]{1,0:T(8,128)(2,1)S(1)} collective-permute-done((bf16[64,2048]{1,0:T(8,128)(2,1)S(1)}, bf16[64,2048]{1,0:T(8,128)(2,1)S(1)}, u32[]{:S(2)}, u32[]{:S(2)}) %collective-permute-start.7) | collective-permute-done | bytes 262176 | tf_op jit(solution)/shard_map/ppermute | solution.py:69
  43.1 2.6 %collective-permute-done.8.r23 = bf16[64,2048]{1,0:T(8,128)(2,1)S(1)} collective-permute-done((bf16[64,2048]{1,0:T(8,128)(2,1)S(1)}, bf16[64,2048]{1,0:T(8,128)(2,1)S(1)}, u32[]{:S(2)}, u32[]{:S(2)}) %collective-permute-start.8) | collective-permute-done | bytes 262176 | tf_op jit(solution)/shard_map/ppermute | solution.py:69
  45.7 2.5 %hidden.1 = (bf16[128,1024]{1,0:T(8,128)(2,1)S(1)}, f32[128,1024]{1,0:T(8,128)}, f32[16,8,128]{2,1,0:T(8,128)S(1)}) custom-call(s32[4]{0:T(128)S(1)} %pad_add_fusion.at, f32[64,2048]{1,0:T(8,128)} %get-tuple-element.38.other.m1, bf16[64,2048]{1,0:T(8,128)(2,1)S(1)} %collective-permute-done.1.r11, bf16[64,2048]{1,0:T(8,128)(2,1)S(1)} %collective-permute-done.2.r12, ...), custom_call_target="tpu_custom_call" | custom-call | flops 7864320 | bytes 3493888 | tf_op jit(solution)/shard_map/hidden/pallas_call | solution.py:35
  48.3 0.3 collective-permute-start.11
  48.5 0.4 collective-permute-start.10
  48.9 3.4 %collective-permute-start.9 = (bf16[128,1024]{1,0:T(8,128)(2,1)S(1)}, bf16[128,1024]{1,0:T(8,128)(2,1)S(1)}, u32[]{:S(2)}, u32[]{:S(2)}) collective-permute-start(bf16[128,1024]{1,0:T(8,128)(2,1)S(1)} %get-tuple-element.46.s0), channel_id=1, source_target_pairs={{0,8},{8,0},{16,24},{24,16},{1,9},{9,1},{17,25},{25,17},{2,10},{10... | collective-permute-start | bytes 786440 | tf_op jit(solution)/shard_map/ppermute | solution.py:69
  52.3 12.0 %all_to_all.20.got = f32[16,8,128]{2,1,0:T(8,128)S(1)} all-to-all(f32[16,8,128]{2,1,0:T(8,128)S(1)} %get-tuple-element.47), channel_id=1, replica_groups=mesh['row'=4,'col'=4,'dp'=8] {'row','col'}, dimensions={0} | all-to-all | bytes 131072 | tf_op jit(solution)/shard_map/all_to_all | solution.py:401
  64.4 0.0 collective-permute-done.11.s3
  64.4 0.0 collective-permute-done.10.s2
  64.4 0.0 collective-permute-done.9.s1
  64.4 4.2 %grads.1 = (bf16[8,160,512]{2,1,0:T(8,128)(2,1)}, f32[264,128]{1,0:T(8,128)}, f32[264,128]{1,0:T(8,128)}, f32[2,128]{1,0:T(2,128)}) custom-call(s32[4]{0:T(128)S(1)} %pad_add_fusion.at, bf16[128,1024]{1,0:T(8,128)(2,1)S(1)} %get-tuple-element.46.s0, bf16[128,1024]{1,0:T(8,128)(2,1)S(1)} %collective-permute-done.9.s1, ...), custom_call_target="tpu_custom_call" | custom-call | flops 671088640 | bytes 4662272 | tf_op jit(solution)/shard_map/grads/pallas_call | solution.py:35
  68.6 4.7 %all-to-all-start.1 = ((bf16[8,160,512]{2,1,0:T(8,128)(2,1)}), bf16[8,160,512]{2,1,0:T(8,128)(2,1)S(1)}, u32[]{:S(2)}, u32[]{:S(2)}) async-start(bf16[8,160,512]{2,1,0:T(8,128)(2,1)} %get-tuple-element.52), calls=%async_computation.1 | async-start | bytes 2621440 | tf_op jit(solution)/shard_map/all_to_all | solution.py:415
  73.3 0.0 collective-permute-start.12
  73.3 1.6 %collective-permute-done.12 = f32[264,128]{1,0:T(8,128)S(1)} collective-permute-done((f32[264,128]{1,0:T(8,128)}, f32[264,128]{1,0:T(8,128)S(1)}, u32[]{:S(2)}, u32[]{:S(2)}) %collective-permute-start.12) | collective-permute-done | bytes 135200 | tf_op jit(solution)/shard_map/ppermute | solution.py:69
  74.9 0.5 collective-permute-start.13
  75.4 5.2 %collective-permute-done.13 = f32[264,128]{1,0:T(8,128)S(1)} collective-permute-done((f32[264,128]{1,0:T(8,128)S(1)}, f32[264,128]{1,0:T(8,128)S(1)}, u32[]{:S(2)}, u32[]{:S(2)}) %collective-permute-start.13) | collective-permute-done | bytes 135200 | tf_op jit(solution)/shard_map/ppermute | solution.py:69
  80.6 2.5 %collective-permute-start.14 = (f32[264,128]{1,0:T(8,128)S(1)}, f32[264,128]{1,0:T(8,128)S(1)}, u32[]{:S(2)}, u32[]{:S(2)}) collective-permute-start(f32[264,128]{1,0:T(8,128)S(1)} %add.19), channel_id=1, source_target_pairs={{0,16},{8,24},{16,0},{24,8},{1,17},{9,25},{17,1},{25,9},{2,18},{10... | collective-permute-start | bytes 405512 | tf_op jit(solution)/shard_map/ppermute | solution.py:69
  83.1 4.1 %collective-permute-done.14 = f32[264,128]{1,0:T(8,128)S(1)} collective-permute-done((f32[264,128]{1,0:T(8,128)S(1)}, f32[264,128]{1,0:T(8,128)S(1)}, u32[]{:S(2)}, u32[]{:S(2)}) %collective-permute-start.14) | collective-permute-done | bytes 135200 | tf_op jit(solution)/shard_map/ppermute | solution.py:69
  87.2 4.7 %all-to-all-done.1.got = bf16[8,160,512]{2,1,0:T(8,128)(2,1)S(1)} async-done(((bf16[8,160,512]{2,1,0:T(8,128)(2,1)}), bf16[8,160,512]{2,1,0:T(8,128)(2,1)S(1)}, u32[]{:S(2)}, u32[]{:S(2)}) %all-to-all-start.1) | async-done | bytes 1310752 | tf_op jit(solution)/shard_map/all_to_all | solution.py:415
  92.0 1.0 action.1.act
  93.0 1.8 %first.1 = bf16[8,64,512]{2,1,0:T(8,128)(2,1)} custom-call(bf16[8,160,512]{2,1,0:T(8,128)(2,1)S(1)} %all-to-all-done.1.got, f32[128,128]{1,0:T(8,128)} %action.1.act), custom_call_target="tpu_custom_call" | custom-call | bytes 1900544 | tf_op jit(solution)/shard_map/first/pallas_call | solution.py:35
  94.8 3.5 %all-to-all-start.3 = ((bf16[8,64,512]{2,1,0:T(8,128)(2,1)}), bf16[8,64,512]{2,1,0:T(8,128)(2,1)S(1)}, u32[]{:S(2)}, u32[]{:S(2)}) async-start(bf16[8,64,512]{2,1,0:T(8,128)(2,1)} %first.1), calls=%async_computation.3 | async-start | bytes 1048576 | tf_op jit(solution)/shard_map/all_to_all | solution.py:425
  98.3 0.1 collective-permute-start.15
  98.4 1.2 collective-permute-done.15.other
  99.6 0.9 fold.1.high
  100.5 0.0 copy-start.6
  100.5 3.1 %collective-permute-start.16 = (f32[256,128]{1,0:T(8,128)S(1)}, f32[256,128]{1,0:T(8,128)S(1)}, u32[]{:S(2)}, u32[]{:S(2)}) collective-permute-start(f32[256,128]{1,0:T(8,128)S(1)} %fold.1.high), channel_id=1, source_target_pairs={{0,64},{32,96},{64,0},{96,32},{1,65},{33,97},{65,1},{97,33},{2,66}... | collective-permute-start | bytes 393224 | tf_op jit(solution)/shard_map/ppermute | solution.py:69
  103.5 7.6 %collective-permute-done.16.from_high = f32[256,128]{1,0:T(8,128)S(1)} collective-permute-done((f32[256,128]{1,0:T(8,128)S(1)}, f32[256,128]{1,0:T(8,128)S(1)}, u32[]{:S(2)}, u32[]{:S(2)}) %collective-permute-start.16) | collective-permute-done | bytes 131104 | tf_op jit(solution)/shard_map/ppermute | solution.py:69
  111.1 1.0 second.1
  112.2 0.0 all-to-all-done.3.g
  112.2 4.0 %all-to-all-start.2 = ((bf16[8,112,512]{2,1,0:T(8,128)(2,1)}), bf16[8,112,512]{2,1,0:T(8,128)(2,1)S(1)}, u32[]{:S(2)}, u32[]{:S(2)}) async-start(bf16[8,112,512]{2,1,0:T(8,128)(2,1)} %second.1), calls=%async_computation.2 | async-start | bytes 1835008 | tf_op jit(solution)/shard_map/all_to_all | solution.py:433
  116.2 0.0 copy-done.6
  116.2 0.7 fusion
  116.9 2.7 %update_first.1 = (f32[2,512,512]{2,1,0:T(8,128)}, f32[2,512,512]{2,1,0:T(8,128)}) custom-call(bf16[8,64,512]{2,1,0:T(8,128)(2,1)S(1)} %all-to-all-done.3.g, f32[2,512,512]{2,1,0:T(8,128)} %cin.5, f32[2,512,512]{2,1,0:T(8,128)} %tin.5), custom_call_target="tpu_custom_call" | custom-call | bytes 8912896 | tf_op jit(solution)/shard_map/update_first/pallas_call | solution.py:35
  119.6 10.6 %all-to-all-done.2.g = bf16[8,112,512]{2,1,0:T(8,128)(2,1)S(1)} async-done(((bf16[8,112,512]{2,1,0:T(8,128)(2,1)}), bf16[8,112,512]{2,1,0:T(8,128)(2,1)S(1)}, u32[]{:S(2)}, u32[]{:S(2)}) %all-to-all-start.2) | async-done | bytes 917536 | tf_op jit(solution)/shard_map/all_to_all | solution.py:433
  130.3 4.7 %update_second.1 = (f32[2,512,512]{2,1,0:T(8,128)}, f32[2,512,512]{2,1,0:T(8,128)}, f32[2,128,512]{2,1,0:T(8,128)}, f32[2,128,512]{2,1,0:T(8,128)}, f32[2,512]{1,0:T(2,128)}, /*index=5*/f32[2,512]{1,0:T(2,128)}) custom-call(bf16[8,112,512]{2,1,0:T(8,128)(2,1)S(1)} %all-to-all-done.2.g, ...), custom_call_target="tpu_custom_call", output_to_operand_aliasing={{0}: (7, {}), {1}: (8, {})} | custom-call | bytes 15613952 | tf_op jit(solution)/shard_map/update_second/pallas_call | solution.py:35
  (17 shorter events, 0.1 us)
Async XLA Ops:
  1.7 6.9 %collective-permute-start = (bf16[128,1280]{1,0:T(8,128)(2,1)S(1)}, bf16[128,1280]{1,0:T(8,128)(2,1)S(1)}, u32[]{:S(2)}, u32[]{:S(2)}) collective-permute-start(bf16[128,1280]{1,0:T(8,128)(2,1)S(1)} %pack.1.x0), channel_id=1, source_target_pairs={{0,32},{32,0},{64,96},{96,64},{1,33},{33,1},{65,97},{97,65},{2,34}... | collective-permute-start | bytes 983048 | tf_op jit(solution)/shard_map/ppermute | solution.py:69
  1.8 11.8 %collective-permute-start.4 = (bf16[128,1280]{1,0:T(8,128)(2,1)S(1)}, bf16[128,1280]{1,0:T(8,128)(2,1)}, u32[]{:S(2)}, u32[]{:S(2)}) collective-permute-start(bf16[128,1280]{1,0:T(8,128)(2,1)S(1)} %pack.1.x0), channel_id=1, source_target_pairs={{0,64},{32,96},{64,0},{96,32},{1,65},{33,97},{65,1},{97,33},{2,66}... | collective-permute-start | bytes 983048 | tf_op jit(solution)/shard_map/ppermute | solution.py:69
  8.6 7.1 %copy-start.4 = (bf16[128]{0:T(256)(128)(2,1)S(1)}, bf16[128]{0:T(256)(128)(2,1)}, u32[]{:S(2)}) copy-start(bf16[128]{0:T(256)(128)(2,1)} %param.20) | copy-start | bytes 772
  8.6 7.1 %copy-start.5 = (bf16[128]{0:T(256)(128)(2,1)S(1)}, bf16[128]{0:T(256)(128)(2,1)}, u32[]{:S(2)}) copy-start(bf16[128]{0:T(256)(128)(2,1)} %param.19) | copy-start | bytes 772
  13.6 14.0 %copy-start.2 = (f32[2,512]{1,0:T(2,128)S(1)}, f32[2,512]{1,0:T(2,128)}, u32[]{:S(2)}) copy-start(f32[2,512]{1,0:T(2,128)} %thead.1) | copy-start | bytes 12292
  13.6 14.0 %copy-start.3 = (f32[2,512]{1,0:T(2,128)S(1)}, f32[2,512]{1,0:T(2,128)}, u32[]{:S(2)}) copy-start(f32[2,512]{1,0:T(2,128)} %chead.1) | copy-start | bytes 12292
  13.6 5.8 %collective-permute-start.5 = (bf16[128,1280]{1,0:T(8,128)(2,1)}, bf16[128,1280]{1,0:T(8,128)(2,1)S(1)}, u32[]{:S(2)}, u32[]{:S(2)}) collective-permute-start(bf16[128,1280]{1,0:T(8,128)(2,1)} %after.1.x0), channel_id=1, source_target_pairs={{0,32},{32,0},{64,96},{96,64},{1,33},{33,1},{65,97},{97,65},{2,34}... | collective-permute-start | bytes 983048 | tf_op jit(solution)/shard_map/ppermute | solution.py:69
  13.7 13.8 %collective-permute-start.1 = (bf16[64,2048]{1,0:T(8,128)(2,1)}, bf16[64,2048]{1,0:T(8,128)(2,1)S(1)}, u32[]{:S(2)}, u32[]{:S(2)}) collective-permute-start(bf16[64,2048]{1,0:T(8,128)(2,1)} %get-tuple-element.39), channel_id=1, source_target_pairs={{0,8},{8,0},{16,24},{24,16},{1,9},{9,1},{17,25},{25,17},{2,10},{10... | collective-permute-start | bytes 786440 | tf_op jit(solution)/shard_map/ppermute | solution.py:69
  15.7 16.5 %collective-permute-start.2 = (bf16[64,2048]{1,0:T(8,128)(2,1)}, bf16[64,2048]{1,0:T(8,128)(2,1)S(1)}, u32[]{:S(2)}, u32[]{:S(2)}) collective-permute-start(bf16[64,2048]{1,0:T(8,128)(2,1)} %get-tuple-element.40), channel_id=1, source_target_pairs={{0,16},{8,24},{16,0},{24,8},{1,17},{9,25},{17,1},{25,9},{2,18},{10... | collective-permute-start | bytes 786440 | tf_op jit(solution)/shard_map/ppermute | solution.py:69
  19.3 16.2 %collective-permute-start.3 = (bf16[64,2048]{1,0:T(8,128)(2,1)}, bf16[64,2048]{1,0:T(8,128)(2,1)S(1)}, u32[]{:S(2)}, u32[]{:S(2)}) collective-permute-start(bf16[64,2048]{1,0:T(8,128)(2,1)} %get-tuple-element.41), channel_id=1, source_target_pairs={{0,24},{8,16},{16,8},{24,0},{1,25},{9,17},{17,9},{25,1},{2,26},{10... | collective-permute-start | bytes 786440 | tf_op jit(solution)/shard_map/ppermute | solution.py:69
  22.8 12.8 %collective-permute-start.6 = (bf16[64,2048]{1,0:T(8,128)(2,1)S(1)}, bf16[64,2048]{1,0:T(8,128)(2,1)S(1)}, u32[]{:S(2)}, u32[]{:S(2)}) collective-permute-start(bf16[64,2048]{1,0:T(8,128)(2,1)S(1)} %get-tuple-element.43), channel_id=1, source_target_pairs={{0,8},{8,0},{16,24},{24,16},{1,9},{9,1},{17,25},{25,17},{2,10},{10... | collective-permute-start | bytes 786440 | tf_op jit(solution)/shard_map/ppermute | solution.py:69
  22.8 20.3 %collective-permute-start.7 = (bf16[64,2048]{1,0:T(8,128)(2,1)S(1)}, bf16[64,2048]{1,0:T(8,128)(2,1)S(1)}, u32[]{:S(2)}, u32[]{:S(2)}) collective-permute-start(bf16[64,2048]{1,0:T(8,128)(2,1)S(1)} %get-tuple-element.44), channel_id=1, source_target_pairs={{0,16},{8,24},{16,0},{24,8},{1,17},{9,25},{17,1},{25,9},{2,18},{10... | collective-permute-start | bytes 786440 | tf_op jit(solution)/shard_map/ppermute | solution.py:69
  27.5 18.3 %collective-permute-start.8 = (bf16[64,2048]{1,0:T(8,128)(2,1)S(1)}, bf16[64,2048]{1,0:T(8,128)(2,1)S(1)}, u32[]{:S(2)}, u32[]{:S(2)}) collective-permute-start(bf16[64,2048]{1,0:T(8,128)(2,1)S(1)} %get-tuple-element.45), channel_id=1, source_target_pairs={{0,24},{8,16},{16,8},{24,0},{1,25},{9,17},{17,9},{25,1},{2,26},{10... | collective-permute-start | bytes 786440 | tf_op jit(solution)/shard_map/ppermute | solution.py:69
  48.3 16.1 %collective-permute-start.11 = (bf16[128,1024]{1,0:T(8,128)(2,1)S(1)}, bf16[128,1024]{1,0:T(8,128)(2,1)S(1)}, u32[]{:S(2)}, u32[]{:S(2)}) collective-permute-start(bf16[128,1024]{1,0:T(8,128)(2,1)S(1)} %get-tuple-element.46.s0), channel_id=1, source_target_pairs={{0,24},{8,16},{16,8},{24,0},{1,25},{9,17},{17,9},{25,1},{2,26},{10... | collective-permute-start | bytes 786440 | tf_op jit(solution)/shard_map/ppermute | solution.py:69
  48.5 15.9 %collective-permute-start.10 = (bf16[128,1024]{1,0:T(8,128)(2,1)S(1)}, bf16[128,1024]{1,0:T(8,128)(2,1)S(1)}, u32[]{:S(2)}, u32[]{:S(2)}) collective-permute-start(bf16[128,1024]{1,0:T(8,128)(2,1)S(1)} %get-tuple-element.46.s0), channel_id=1, source_target_pairs={{0,16},{8,24},{16,0},{24,8},{1,17},{9,25},{17,1},{25,9},{2,18},{10... | collective-permute-start | bytes 786440 | tf_op jit(solution)/shard_map/ppermute | solution.py:69
  48.9 15.5 %collective-permute-start.9 = (bf16[128,1024]{1,0:T(8,128)(2,1)S(1)}, bf16[128,1024]{1,0:T(8,128)(2,1)S(1)}, u32[]{:S(2)}, u32[]{:S(2)}) collective-permute-start(bf16[128,1024]{1,0:T(8,128)(2,1)S(1)} %get-tuple-element.46.s0), channel_id=1, source_target_pairs={{0,8},{8,0},{16,24},{24,16},{1,9},{9,1},{17,25},{25,17},{2,10},{10... | collective-permute-start | bytes 786440 | tf_op jit(solution)/shard_map/ppermute | solution.py:69
  68.6 6.3 %copy-start.1 = (f32[264,128]{1,0:T(8,128)S(1)}, f32[264,128]{1,0:T(8,128)}, u32[]{:S(2)}) copy-start(f32[264,128]{1,0:T(8,128)} %get-tuple-element.53) | copy-start | bytes 405508
  68.6 23.3 %all-to-all-start.1 = ((bf16[8,160,512]{2,1,0:T(8,128)(2,1)}), bf16[8,160,512]{2,1,0:T(8,128)(2,1)S(1)}, u32[]{:S(2)}, u32[]{:S(2)}) async-start(bf16[8,160,512]{2,1,0:T(8,128)(2,1)} %get-tuple-element.52), calls=%async_computation.1 | async-start | bytes 2621440 | tf_op jit(solution)/shard_map/all_to_all | solution.py:415
  73.3 1.6 %collective-permute-start.12 = (f32[264,128]{1,0:T(8,128)}, f32[264,128]{1,0:T(8,128)S(1)}, u32[]{:S(2)}, u32[]{:S(2)}) collective-permute-start(f32[264,128]{1,0:T(8,128)} %get-tuple-element.54), channel_id=1, source_target_pairs={{0,32},{32,0},{64,96},{96,64},{1,33},{33,1},{65,97},{97,65},{2,34}... | collective-permute-start | bytes 405512 | tf_op jit(solution)/shard_map/ppermute | solution.py:69
  74.9 5.7 %collective-permute-start.13 = (f32[264,128]{1,0:T(8,128)S(1)}, f32[264,128]{1,0:T(8,128)S(1)}, u32[]{:S(2)}, u32[]{:S(2)}) collective-permute-start(f32[264,128]{1,0:T(8,128)S(1)} %add.18), channel_id=1, source_target_pairs={{0,8},{8,0},{16,24},{24,16},{1,9},{9,1},{17,25},{25,17},{2,10},{10... | collective-permute-start | bytes 405512 | tf_op jit(solution)/shard_map/ppermute | solution.py:69
  80.6 6.6 %collective-permute-start.14 = (f32[264,128]{1,0:T(8,128)S(1)}, f32[264,128]{1,0:T(8,128)S(1)}, u32[]{:S(2)}, u32[]{:S(2)}) collective-permute-start(f32[264,128]{1,0:T(8,128)S(1)} %add.19), channel_id=1, source_target_pairs={{0,16},{8,24},{16,0},{24,8},{1,17},{9,25},{17,1},{25,9},{2,18},{10... | collective-permute-start | bytes 405512 | tf_op jit(solution)/shard_map/ppermute | solution.py:69
  93.0 5.3 %copy-start = (f32[128,128]{1,0:T(8,128)S(1)}, f32[128,128]{1,0:T(8,128)}, u32[]{:S(2)}) copy-start(f32[128,128]{1,0:T(8,128)} %action.1.act) | copy-start | bytes 196612
  94.8 17.4 %all-to-all-start.3 = ((bf16[8,64,512]{2,1,0:T(8,128)(2,1)}), bf16[8,64,512]{2,1,0:T(8,128)(2,1)S(1)}, u32[]{:S(2)}, u32[]{:S(2)}) async-start(bf16[8,64,512]{2,1,0:T(8,128)(2,1)} %first.1), calls=%async_computation.3 | async-start | bytes 1048576 | tf_op jit(solution)/shard_map/all_to_all | solution.py:425
  98.3 1.3 collective-permute-start.15
  100.5 15.8 %copy-start.6 = (s32[128]{0:T(128)S(1)}, s32[128]{0:T(128)}, u32[]{:S(2)}) copy-start(s32[128]{0:T(128)} %param.21) | copy-start | bytes 1540
  100.5 10.7 %collective-permute-start.16 = (f32[256,128]{1,0:T(8,128)S(1)}, f32[256,128]{1,0:T(8,128)S(1)}, u32[]{:S(2)}, u32[]{:S(2)}) collective-permute-start(f32[256,128]{1,0:T(8,128)S(1)} %fold.1.high), channel_id=1, source_target_pairs={{0,64},{32,96},{64,0},{96,32},{1,65},{33,97},{65,1},{97,33},{2,66}... | collective-permute-start | bytes 393224 | tf_op jit(solution)/shard_map/ppermute | solution.py:69
  112.2 18.1 %all-to-all-start.2 = ((bf16[8,112,512]{2,1,0:T(8,128)(2,1)}), bf16[8,112,512]{2,1,0:T(8,128)(2,1)S(1)}, u32[]{:S(2)}, u32[]{:S(2)}) async-start(bf16[8,112,512]{2,1,0:T(8,128)(2,1)} %second.1), calls=%async_computation.2 | async-start | bytes 1835008 | tf_op jit(solution)/shard_map/all_to_all | solution.py:433

commit v5 on v3

--- a/solution.py
+++ b/solution.py
@@ -420,8 +420,8 @@
     (chunk,) = call(total_body, [shape(8, 128, 512)], [parts, pair], name="total")
     grad_in = lax.all_to_all(chunk, "dp", 0, 0, tiled=True)
     pairs = [pair] + [swap(pair, "dp", k) for k in (1, 2, 3)]
-    rest = rest + swap(rest, "col", 1)
-    rest = rest + swap(rest, "col", 2)
+    terms = [swap(rest, "col", k) for k in (1, 2, 3)]
+    rest = (rest + terms[0]) + (terms[1] + terms[2])
     action_slope = actor_flags.astype(f32)[:, None] * rest[0:128]
     head = rest[128:136].reshape(2, 512)
     new_head = critic_head - head_rate * head

time: 131 us -> 135 us (1.031)
  starting transfers between devices: 40.4 us -> 43.6 us
    ppermute x20 -> x21, starting transfers between devices: 27.8 us -> 31.1 us  [swap(): return lax.ppermute(x, axis, [(i, i ^ bit) for i in range(n)])]
    ppermute x20 -> x21, waiting for transfers between devices: 42.7 us -> 43.4 us  [swap(): return lax.ppermute(x, axis, [(i, i ^ bit) for i in range(n)])]
  transfers between devices with their start and end apart: 24 -> 25, of which waited for: 11 -> 10; matrix products, arithmetic and copies ran while one was open for 1% -> 1% of each run, Pallas kernels for 11% -> 11%
where the time goes in v5:
time: 135 us
  waiting for transfers between devices  49.5 us (37%)
  starting transfers between devices  43.6 us (32%)
  Pallas kernels  26.3 us (19%)
  blocking collectives  12.6 us (9%)
  other arithmetic  1.57 us (1%)
    ppermute x21, waiting for transfers between devices, swap(): return lax.ppermute(x, axis, [(i, i ^ bit) for i in range(n)])  43.4 us
    ppermute x21, starting transfers between devices, swap(): return lax.ppermute(x, axis, [(i, i ^ bit) for i in range(n)])  31.1 us
    pallas_call x12, Pallas kernels, call(): pl.pallas_call(body, out_shape=tuple((HBM(o.shape, o.dtype) if i in to el...  26.3 us
    all_to_all x1, blocking collectives, on_device(): got = lax.all_to_all(packet, ('row', 'col'), 0, 0, tiled=True)  12.6 us
    all_to_all x1, waiting for transfers between devices, on_device(): moves = lax.all_to_all(moves, 'dp', 0, 0, tiled=True)  6.06 us
    all_to_all x1, starting transfers between devices, on_device(): moves = lax.all_to_all(moves, 'dp', 0, 0, tiled=True)  4.41 us
    all_to_all x1, starting transfers between devices, on_device(): grad_in = lax.all_to_all(chunk, 'dp', 0, 0, tiled=True)  4.01 us
    all_to_all x1, starting transfers between devices, on_device(): parts = lax.all_to_all(grads, 'dp', 0, 0, tiled=True)  3.56 us
  transfers between devices with their start and end apart: 25, of which 10 were waited for; matrix products, arithmetic and copies ran while one was open for 1% of the time, Pallas kernels for 11%

profile of v5, /device:TPU:0, one launch (start us, length us, event | category | flops | bytes accessed | tf_op | source)
XLA Modules:
  0.0 134.6 jit_solution(6446758965463922098)
XLA Ops:
  0.6 1.1 pack.1.x0
  1.7 0.1 collective-permute-start
  1.8 3.4 %collective-permute-start.1 = (bf16[128,1280]{1,0:T(8,128)(2,1)S(1)}, bf16[128,1280]{1,0:T(8,128)(2,1)}, u32[]{:S(2)}, u32[]{:S(2)}) collective-permute-start(bf16[128,1280]{1,0:T(8,128)(2,1)S(1)} %pack.1.x0), channel_id=1, source_target_pairs={{0,64},{32,96},{64,0},{96,32},{1,65},{33,97},{65,1},{97,33},{2,66}... | collective-permute-start | bytes 983048 | tf_op jit(solution)/shard_map/ppermute | solution.py:68
  5.2 0.1 pad.3.clone
  5.2 3.2 %weights.1 = (bf16[4,512,512]{2,1,0:T(8,128)(2,1)S(1)}, bf16[4,128,512]{2,1,0:T(8,128)(2,1)S(1)}, bf16[512,128]{1,0:T(8,128)(2,1)}) custom-call(f32[2,512,512]{2,1,0:T(8,128)} %cin.3, f32[2,512,512]{2,1,0:T(8,128)} %tin.3, f32[2,128,512]{2,1,0:T(8,128)} %cact.3, f32[2,128,512]{2,1,0:T(8,128)} %tact.3), custom_call_target="tpu_custom_call" | custom-call | flops 67108864 | bytes 7995392 | tf_op jit(solution)/shard_map/weights/pallas_call | solution.py:35
  8.5 0.1 pad_add_fusion.at
  8.5 0.0 collective-permute-done.x1
  8.6 3.2 %forward_near.1 = (f32[64,2048]{1,0:T(8,128)}, bf16[64,2048]{1,0:T(8,128)(2,1)}, bf16[64,2048]{1,0:T(8,128)(2,1)}, bf16[64,2048]{1,0:T(8,128)(2,1)}, bf16[2,512,...) custom-call(s32[4]{0:T(128)S(1)} %pad_add_fusion.at, bf16[128,1280]{1,0:T(8,128)(2,1)S(1)} %pack.1.x0, ...), custom_call_target="tpu_custom_call" | custom-call | flops 671088640 | bytes 5177344 | tf_op jit(solution)/shard_map/forward_near/pallas_call | solution.py:35
  11.7 1.8 %collective-permute-done.1.x = bf16[128,1280]{1,0:T(8,128)(2,1)} collective-permute-done((bf16[128,1280]{1,0:T(8,128)(2,1)S(1)}, bf16[128,1280]{1,0:T(8,128)(2,1)}, u32[]{:S(2)}, u32[]{:S(2)}) %collective-permute-start.1) | collective-permute-done | bytes 327712 | tf_op jit(solution)/shard_map/ppermute | solution.py:68
  13.6 0.0 collective-permute-start.2
  13.6 0.1 fusion
  13.7 2.0 %collective-permute-start.3 = (bf16[64,2048]{1,0:T(8,128)(2,1)}, bf16[64,2048]{1,0:T(8,128)(2,1)S(1)}, u32[]{:S(2)}, u32[]{:S(2)}) collective-permute-start(bf16[64,2048]{1,0:T(8,128)(2,1)} %get-tuple-element.47), channel_id=1, source_target_pairs={{0,8},{8,0},{16,24},{24,16},{1,9},{9,1},{17,25},{25,17},{2,10},{10... | collective-permute-start | bytes 786440 | tf_op jit(solution)/shard_map/ppermute | solution.py:68
  15.7 3.7 %collective-permute-start.4 = (bf16[64,2048]{1,0:T(8,128)(2,1)}, bf16[64,2048]{1,0:T(8,128)(2,1)S(1)}, u32[]{:S(2)}, u32[]{:S(2)}) collective-permute-start(bf16[64,2048]{1,0:T(8,128)(2,1)} %get-tuple-element.48), channel_id=1, source_target_pairs={{0,16},{8,24},{16,0},{24,8},{1,17},{9,25},{17,1},{25,9},{2,18},{10... | collective-permute-start | bytes 786440 | tf_op jit(solution)/shard_map/ppermute | solution.py:68
  19.3 0.0 collective-permute-start.5
  19.3 0.0 collective-permute-done.2.x1
  19.3 3.2 %forward_far.1 = (f32[64,2048]{1,0:T(8,128)}, bf16[64,2048]{1,0:T(8,128)(2,1)S(1)}, bf16[64,2048]{1,0:T(8,128)(2,1)S(1)}, bf16[64,2048]{1,0:T(8,128)(2,1)S(1)}, ...) custom-call(s32[4]{0:T(128)S(1)} %pad_add_fusion.at, bf16[128,1280]{1,0:T(8,128)(2,1)} %after.1.x0, ...), custom_call_target="tpu_custom_call" | custom-call | flops 671088640 | bytes 5177344 | tf_op jit(solution)/shard_map/forward_far/pallas_call | solution.py:35
  22.5 0.1 collective-permute-start.6
  22.6 4.6 %collective-permute-start.7 = (bf16[64,2048]{1,0:T(8,128)(2,1)S(1)}, bf16[64,2048]{1,0:T(8,128)(2,1)S(1)}, u32[]{:S(2)}, u32[]{:S(2)}) collective-permute-start(bf16[64,2048]{1,0:T(8,128)(2,1)S(1)} %get-tuple-element.52), channel_id=1, source_target_pairs={{0,16},{8,24},{16,0},{24,8},{1,17},{9,25},{17,1},{25,9},{2,18},{10... | collective-permute-start | bytes 786440 | tf_op jit(solution)/shard_map/ppermute | solution.py:68
  27.2 0.0 collective-permute-done.3.r11
  27.2 0.0 collective-permute-start.8
  27.2 0.1 maximum_maximum_fusion.1.rew
  27.3 0.1 maximum_maximum_fusion.heads
  27.4 4.8 %collective-permute-done.4.r12 = bf16[64,2048]{1,0:T(8,128)(2,1)S(1)} collective-permute-done((bf16[64,2048]{1,0:T(8,128)(2,1)}, bf16[64,2048]{1,0:T(8,128)(2,1)S(1)}, u32[]{:S(2)}, u32[]{:S(2)}) %collective-permute-start.4) | collective-permute-done | bytes 262176 | tf_op jit(solution)/shard_map/ppermute | solution.py:68
  32.2 3.4 %collective-permute-done.5.r13 = bf16[64,2048]{1,0:T(8,128)(2,1)S(1)} collective-permute-done((bf16[64,2048]{1,0:T(8,128)(2,1)}, bf16[64,2048]{1,0:T(8,128)(2,1)S(1)}, u32[]{:S(2)}, u32[]{:S(2)}) %collective-permute-start.5) | collective-permute-done | bytes 262176 | tf_op jit(solution)/shard_map/ppermute | solution.py:68
  35.6 0.0 collective-permute-done.6.r21
  35.6 7.6 %collective-permute-done.7.r22 = bf16[64,2048]{1,0:T(8,128)(2,1)S(1)} collective-permute-done((bf16[64,2048]{1,0:T(8,128)(2,1)S(1)}, bf16[64,2048]{1,0:T(8,128)(2,1)S(1)}, u32[]{:S(2)}, u32[]{:S(2)}) %collective-permute-start.7) | collective-permute-done | bytes 262176 | tf_op jit(solution)/shard_map/ppermute | solution.py:68
  43.1 2.6 %collective-permute-done.8.r23 = bf16[64,2048]{1,0:T(8,128)(2,1)S(1)} collective-permute-done((bf16[64,2048]{1,0:T(8,128)(2,1)S(1)}, bf16[64,2048]{1,0:T(8,128)(2,1)S(1)}, u32[]{:S(2)}, u32[]{:S(2)}) %collective-permute-start.8) | collective-permute-done | bytes 262176 | tf_op jit(solution)/shard_map/ppermute | solution.py:68
  45.7 2.5 %hidden.1 = (bf16[128,1024]{1,0:T(8,128)(2,1)S(1)}, f32[128,1024]{1,0:T(8,128)}, f32[16,8,128]{2,1,0:T(8,128)S(1)}) custom-call(s32[4]{0:T(128)S(1)} %pad_add_fusion.at, f32[64,2048]{1,0:T(8,128)} %get-tuple-element.45.other.m1, bf16[64,2048]{1,0:T(8,128)(2,1)S(1)} %collective-permute-done.3.r11, bf16[64,2048]{1,0:T(8,128)(2,1)S(1)} %collective-permute-done.4.r12, ...), custom_call_target="tpu_custom_call" | custom-call | flops 7864320 | bytes 3493888 | tf_op jit(solution)/shard_map/hidden/pallas_call | solution.py:35
  48.2 0.0 collective-permute-start.10
  48.2 1.3 collective-permute-start.11
  49.5 2.2 %collective-permute-start.9 = (bf16[128,1024]{1,0:T(8,128)(2,1)S(1)}, bf16[128,1024]{1,0:T(8,128)(2,1)S(1)}, u32[]{:S(2)}, u32[]{:S(2)}) collective-permute-start(bf16[128,1024]{1,0:T(8,128)(2,1)S(1)} %get-tuple-element.54.s0), channel_id=1, source_target_pairs={{0,8},{8,0},{16,24},{24,16},{1,9},{9,1},{17,25},{25,17},{2,10},{10... | collective-permute-start | bytes 786440 | tf_op jit(solution)/shard_map/ppermute | solution.py:68
  51.7 12.6 %all_to_all.20.got = f32[16,8,128]{2,1,0:T(8,128)S(1)} all-to-all(f32[16,8,128]{2,1,0:T(8,128)S(1)} %get-tuple-element.55), channel_id=1, replica_groups=mesh['row'=4,'col'=4,'dp'=8] {'row','col'}, dimensions={0} | all-to-all | bytes 131072 | tf_op jit(solution)/shard_map/all_to_all | solution.py:386
  64.4 0.0 collective-permute-done.10.s2
  64.4 2.9 %errors.1 = (bf16[8,48,512]{2,1,0:T(8,128)(2,1)}, bf16[2,512,512]{2,1,0:T(8,128)(2,1)S(1)}, f32[256,128]{1,0:T(8,128)}, f32[256,128]{1,0:T(8,128)}, f32[2,128]{1,0:T(2,128)}) custom-call(s32[4]{0:T(128)S(1)} %pad_add_fusion.at, bf16[128,1024]{1,0:T(8,128)(2,1)S(1)} %get-tuple-element.54.s0, bf16[128,1024]{1,0:T(8,128)(2,1)S(1)} %collective-permute-done.9.s1, ...), custom_call_target="tpu_custom_call" | custom-call | flops 201326592 | bytes 3605504 | tf_op jit(solution)/shard_map/errors/pallas_call | solution.py:35
  67.3 4.4 %all-to-all-start.2 = ((bf16[8,48,512]{2,1,0:T(8,128)(2,1)}), bf16[8,48,512]{2,1,0:T(8,128)(2,1)S(1)}, u32[]{:S(2)}, u32[]{:S(2)}) async-start(bf16[8,48,512]{2,1,0:T(8,128)(2,1)} %get-tuple-element.61), calls=%async_computation.2 | async-start | bytes 786432 | tf_op jit(solution)/shard_map/all_to_all | solution.py:398
  71.7 2.9 %grads.1 = bf16[8,128,512]{2,1,0:T(8,128)(2,1)} custom-call(bf16[2,512,256]{2,1,0:T(8,128)(2,1)} %get-tuple-element.44.left1, bf16[2,512,256]{2,1,0:T(8,128)(2,1)} %get-tuple-element.46.left2, bf16[2,512,512]{2,1,0:T(8,128)(2,1)S(1)} %get-tuple-element.60.delta), custom_call_target="tpu_custom_call" | custom-call | flops 536870912 | bytes 3145728 | tf_op jit(solution)/shard_map/grads/pallas_call | solution.py:35
  74.6 6.1 %all-to-all-done.2.got = bf16[8,48,512]{2,1,0:T(8,128)(2,1)S(1)} async-done(((bf16[8,48,512]{2,1,0:T(8,128)(2,1)}), bf16[8,48,512]{2,1,0:T(8,128)(2,1)S(1)}, u32[]{:S(2)}, u32[]{:S(2)}) %all-to-all-start.2) | async-done | bytes 393248 | tf_op jit(solution)/shard_map/all_to_all | solution.py:398
  80.7 3.6 %all-to-all-start.1 = ((bf16[8,128,512]{2,1,0:T(8,128)(2,1)}), bf16[8,128,512]{2,1,0:T(8,128)(2,1)S(1)}, u32[]{:S(2)}, u32[]{:S(2)}) async-start(bf16[8,128,512]{2,1,0:T(8,128)(2,1)} %grads.1), calls=%async_computation.1 | async-start | bytes 2097152 | tf_op jit(solution)/shard_map/all_to_all | solution.py:403
  84.2 1.4 %action.1 = (f32[392,128]{1,0:T(8,128)S(1)}, f32[392,128]{1,0:T(8,128)S(1)}) custom-call(bf16[8,48,512]{2,1,0:T(8,128)(2,1)S(1)} %all-to-all-done.2.got, bf16[4,512,512]{2,1,0:T(8,128)(2,1)S(1)} %get-tuple-element.43.w, f32[256,128]{1,0:T(8,128)} %get-tuple-element.62.keep, f32[256,128]{1,0:T(8,128)} %get-tuple-element.63.give), custom_call_target="tpu_custom_call" | custom-call | flops 16777216 | bytes 3153920 | tf_op jit(solution)/shard_map/action/pallas_call | solution.py:35
  85.6 1.5 %collective-permute-done.12.other = f32[392,128]{1,0:T(8,128)S(1)} collective-permute-done((f32[392,128]{1,0:T(8,128)S(1)}, f32[392,128]{1,0:T(8,128)S(1)}, u32[]{:S(2)}, u32[]{:S(2)}) %collective-permute-start.12) | collective-permute-done | bytes 200736 | tf_op jit(solution)/shard_map/ppermute | solution.py:68
  87.1 2.8 %collective-permute-start.13 = (f32[256,128]{1,0:T(8,128)S(1)}, f32[256,128]{1,0:T(8,128)S(1)}, u32[]{:S(2)}, u32[]{:S(2)}) collective-permute-start(f32[256,128]{1,0:T(8,128)S(1)} %get-tuple-element.66.high), channel_id=1, source_target_pairs={{0,64},{32,96},{64,0},{96,32},{1,65},{33,97},{65,1},{97,33},{2,66}... | collective-permute-start | bytes 393224 | tf_op jit(solution)/shard_map/ppermute | solution.py:68
  89.9 1.3 collective-permute-start.14
  91.2 0.6 collective-permute-start.15
  91.8 10.8 %collective-permute-done.14.from_low = f32[128,128]{1,0:T(8,128)S(1)} collective-permute-done((f32[128,128]{1,0:T(8,128)S(1)}, f32[128,128]{1,0:T(8,128)S(1)}, u32[]{:S(2)}, u32[]{:S(2)}) %collective-permute-start.14) | collective-permute-done | bytes 65568 | tf_op jit(solution)/shard_map/ppermute | solution.py:68
  102.6 0.0 collective-permute-done.15.from_both
  102.6 0.0 collective-permute-done.13.from_high
  102.6 0.5 collective-permute-start.19
  103.1 2.3 %collective-permute-start.20 = (f32[136,128]{1,0:T(8,128)S(1)}, f32[136,128]{1,0:T(8,128)S(1)}, u32[]{:S(2)}, u32[]{:S(2)}) collective-permute-start(f32[136,128]{1,0:T(8,128)S(1)} %get-tuple-element.72), channel_id=1, source_target_pairs={{0,16},{8,24},{16,0},{24,8},{1,17},{9,25},{17,1},{25,9},{2,18},{10... | collective-permute-start | bytes 208904 | tf_op jit(solution)/shard_map/ppermute | solution.py:68
  105.3 2.0 %collective-permute-start.21 = (f32[136,128]{1,0:T(8,128)S(1)}, f32[136,128]{1,0:T(8,128)S(1)}, u32[]{:S(2)}, u32[]{:S(2)}) collective-permute-start(f32[136,128]{1,0:T(8,128)S(1)} %get-tuple-element.72), channel_id=1, source_target_pairs={{0,24},{8,16},{16,8},{24,0},{1,25},{9,17},{17,9},{25,1},{2,26},{10... | collective-permute-start | bytes 208904 | tf_op jit(solution)/shard_map/ppermute | solution.py:68
  107.4 0.0 all-to-all-done.1.got
  107.4 1.1 total.1
  108.5 4.0 %all-to-all-start.3 = ((bf16[8,128,512]{2,1,0:T(8,128)(2,1)}), bf16[8,128,512]{2,1,0:T(8,128)(2,1)S(1)}, u32[]{:S(2)}, u32[]{:S(2)}) async-start(bf16[8,128,512]{2,1,0:T(8,128)(2,1)} %total.1), calls=%async_computation.3 | async-start | bytes 2097152 | tf_op jit(solution)/shard_map/all_to_all | solution.py:421
  112.5 2.1 %collective-permute-start.16 = (bf16[2,32,512]{2,1,0:T(8,128)(2,1)S(1)}, bf16[2,32,512]{2,1,0:T(8,128)(2,1)S(1)}, u32[]{:S(2)}, u32[]{:S(2)}) collective-permute-start(bf16[2,32,512]{2,1,0:T(8,128)(2,1)S(1)} %get-tuple-element.69.pair.g0), channel_id=1, source_target_pairs={{0,1},{1,0},{2,3},{3,2},{4,5},{5,4},{6,7},{7,6},{8,9},{9,8},{10,11... | collective-permute-start | bytes 196616 | tf_op jit(solution)/shard_map/ppermute | solution.py:68
  114.6 2.7 %collective-permute-start.17 = (bf16[2,32,512]{2,1,0:T(8,128)(2,1)S(1)}, bf16[2,32,512]{2,1,0:T(8,128)(2,1)S(1)}, u32[]{:S(2)}, u32[]{:S(2)}) collective-permute-start(bf16[2,32,512]{2,1,0:T(8,128)(2,1)S(1)} %get-tuple-element.69.pair.g0), channel_id=1, source_target_pairs={{0,2},{1,3},{2,0},{3,1},{4,6},{5,7},{6,4},{7,5},{8,10},{9,11},{10,... | collective-permute-start | bytes 196616 | tf_op jit(solution)/shard_map/ppermute | solution.py:68
  117.3 0.0 collective-permute-done.19
  117.3 0.1 collective-permute-start.18
  117.4 0.0 collective-permute-done.20
  117.4 0.0 collective-permute-done.21
  117.4 0.7 slice_multiply_fusion
  118.1 0.6 multiply_add_fusion
  118.7 8.7 %collective-permute-done.16.g1 = bf16[2,32,512]{2,1,0:T(8,128)(2,1)S(1)} collective-permute-done((bf16[2,32,512]{2,1,0:T(8,128)(2,1)S(1)}, bf16[2,32,512]{2,1,0:T(8,128)(2,1)S(1)}, u32[]{:S(2)}, u32[]{:S(2)}) %collective-permute-start.16) | collective-permute-done | bytes 65568 | tf_op jit(solution)/shard_map/ppermute | solution.py:68
  127.5 2.2 %collective-permute-done.17.g2 = bf16[2,32,512]{2,1,0:T(8,128)(2,1)S(1)} collective-permute-done((bf16[2,32,512]{2,1,0:T(8,128)(2,1)S(1)}, bf16[2,32,512]{2,1,0:T(8,128)(2,1)S(1)}, u32[]{:S(2)}, u32[]{:S(2)}) %collective-permute-start.17) | collective-permute-done | bytes 65568 | tf_op jit(solution)/shard_map/ppermute | solution.py:68
  129.7 0.0 all-to-all-done.3.g
  129.7 4.9 %update.1 = (f32[2,512,512]{2,1,0:T(8,128)}, f32[2,512,512]{2,1,0:T(8,128)}, f32[2,128,512]{2,1,0:T(8,128)}, f32[2,128,512]{2,1,0:T(8,128)}) custom-call(s32[4]{0:T(128)S(1)} %pad_add_fusion.at, bf16[8,128,512]{2,1,0:T(8,128)(2,1)S(1)} %all-to-all-done.3.g, bf16[2,32,512]{2,1,0:T(8,128)(2,1)S(1)} %get-tuple-element.69.pair.g0, ...), custom_call_target="tpu_custom_call" | custom-call | bytes 11796480 | tf_op jit(solution)/shard_map/update/pallas_call | solution.py:35
  (24 shorter events, 0.1 us)
Async XLA Ops:
  1.7 6.8 %collective-permute-start = (bf16[128,1280]{1,0:T(8,128)(2,1)S(1)}, bf16[128,1280]{1,0:T(8,128)(2,1)S(1)}, u32[]{:S(2)}, u32[]{:S(2)}) collective-permute-start(bf16[128,1280]{1,0:T(8,128)(2,1)S(1)} %pack.1.x0), channel_id=1, source_target_pairs={{0,32},{32,0},{64,96},{96,64},{1,33},{33,1},{65,97},{97,65},{2,34}... | collective-permute-start | bytes 983048 | tf_op jit(solution)/shard_map/ppermute | solution.py:68
  1.8 11.8 %collective-permute-start.1 = (bf16[128,1280]{1,0:T(8,128)(2,1)S(1)}, bf16[128,1280]{1,0:T(8,128)(2,1)}, u32[]{:S(2)}, u32[]{:S(2)}) collective-permute-start(bf16[128,1280]{1,0:T(8,128)(2,1)S(1)} %pack.1.x0), channel_id=1, source_target_pairs={{0,64},{32,96},{64,0},{96,32},{1,65},{33,97},{65,1},{97,33},{2,66}... | collective-permute-start | bytes 983048 | tf_op jit(solution)/shard_map/ppermute | solution.py:68
  8.5 7.1 %copy-start.2 = (bf16[128]{0:T(256)(128)(2,1)S(1)}, bf16[128]{0:T(256)(128)(2,1)}, u32[]{:S(2)}) copy-start(bf16[128]{0:T(256)(128)(2,1)} %param.20) | copy-start | bytes 772
  8.5 7.1 %copy-start.3 = (bf16[128]{0:T(256)(128)(2,1)S(1)}, bf16[128]{0:T(256)(128)(2,1)}, u32[]{:S(2)}) copy-start(bf16[128]{0:T(256)(128)(2,1)} %param.19) | copy-start | bytes 772
  13.6 13.8 %copy-start = (f32[2,512]{1,0:T(2,128)S(1)}, f32[2,512]{1,0:T(2,128)}, u32[]{:S(2)}) copy-start(f32[2,512]{1,0:T(2,128)} %param.27) | copy-start | bytes 12292
  13.6 13.8 %copy-start.1 = (f32[2,512]{1,0:T(2,128)S(1)}, f32[2,512]{1,0:T(2,128)}, u32[]{:S(2)}) copy-start(f32[2,512]{1,0:T(2,128)} %param.24) | copy-start | bytes 12292
  13.6 5.8 %collective-permute-start.2 = (bf16[128,1280]{1,0:T(8,128)(2,1)}, bf16[128,1280]{1,0:T(8,128)(2,1)S(1)}, u32[]{:S(2)}, u32[]{:S(2)}) collective-permute-start(bf16[128,1280]{1,0:T(8,128)(2,1)} %after.1.x0), channel_id=1, source_target_pairs={{0,32},{32,0},{64,96},{96,64},{1,33},{33,1},{65,97},{97,65},{2,34}... | collective-permute-start | bytes 983048 | tf_op jit(solution)/shard_map/ppermute | solution.py:68
  13.7 13.6 %collective-permute-start.3 = (bf16[64,2048]{1,0:T(8,128)(2,1)}, bf16[64,2048]{1,0:T(8,128)(2,1)S(1)}, u32[]{:S(2)}, u32[]{:S(2)}) collective-permute-start(bf16[64,2048]{1,0:T(8,128)(2,1)} %get-tuple-element.47), channel_id=1, source_target_pairs={{0,8},{8,0},{16,24},{24,16},{1,9},{9,1},{17,25},{25,17},{2,10},{10... | collective-permute-start | bytes 786440 | tf_op jit(solution)/shard_map/ppermute | solution.py:68
  15.7 16.5 %collective-permute-start.4 = (bf16[64,2048]{1,0:T(8,128)(2,1)}, bf16[64,2048]{1,0:T(8,128)(2,1)S(1)}, u32[]{:S(2)}, u32[]{:S(2)}) collective-permute-start(bf16[64,2048]{1,0:T(8,128)(2,1)} %get-tuple-element.48), channel_id=1, source_target_pairs={{0,16},{8,24},{16,0},{24,8},{1,17},{9,25},{17,1},{25,9},{2,18},{10... | collective-permute-start | bytes 786440 | tf_op jit(solution)/shard_map/ppermute | solution.py:68
  19.3 16.2 %collective-permute-start.5 = (bf16[64,2048]{1,0:T(8,128)(2,1)}, bf16[64,2048]{1,0:T(8,128)(2,1)S(1)}, u32[]{:S(2)}, u32[]{:S(2)}) collective-permute-start(bf16[64,2048]{1,0:T(8,128)(2,1)} %get-tuple-element.49), channel_id=1, source_target_pairs={{0,24},{8,16},{16,8},{24,0},{1,25},{9,17},{17,9},{25,1},{2,26},{10... | collective-permute-start | bytes 786440 | tf_op jit(solution)/shard_map/ppermute | solution.py:68
  22.5 13.0 %collective-permute-start.6 = (bf16[64,2048]{1,0:T(8,128)(2,1)S(1)}, bf16[64,2048]{1,0:T(8,128)(2,1)S(1)}, u32[]{:S(2)}, u32[]{:S(2)}) collective-permute-start(bf16[64,2048]{1,0:T(8,128)(2,1)S(1)} %get-tuple-element.51), channel_id=1, source_target_pairs={{0,8},{8,0},{16,24},{24,16},{1,9},{9,1},{17,25},{25,17},{2,10},{10... | collective-permute-start | bytes 786440 | tf_op jit(solution)/shard_map/ppermute | solution.py:68
  22.6 20.5 %collective-permute-start.7 = (bf16[64,2048]{1,0:T(8,128)(2,1)S(1)}, bf16[64,2048]{1,0:T(8,128)(2,1)S(1)}, u32[]{:S(2)}, u32[]{:S(2)}) collective-permute-start(bf16[64,2048]{1,0:T(8,128)(2,1)S(1)} %get-tuple-element.52), channel_id=1, source_target_pairs={{0,16},{8,24},{16,0},{24,8},{1,17},{9,25},{17,1},{25,9},{2,18},{10... | collective-permute-start | bytes 786440 | tf_op jit(solution)/shard_map/ppermute | solution.py:68
  27.2 18.5 %collective-permute-start.8 = (bf16[64,2048]{1,0:T(8,128)(2,1)S(1)}, bf16[64,2048]{1,0:T(8,128)(2,1)S(1)}, u32[]{:S(2)}, u32[]{:S(2)}) collective-permute-start(bf16[64,2048]{1,0:T(8,128)(2,1)S(1)} %get-tuple-element.53), channel_id=1, source_target_pairs={{0,24},{8,16},{16,8},{24,0},{1,25},{9,17},{17,9},{25,1},{2,26},{10... | collective-permute-start | bytes 786440 | tf_op jit(solution)/shard_map/ppermute | solution.py:68
  48.2 16.1 %collective-permute-start.10 = (bf16[128,1024]{1,0:T(8,128)(2,1)S(1)}, bf16[128,1024]{1,0:T(8,128)(2,1)S(1)}, u32[]{:S(2)}, u32[]{:S(2)}) collective-permute-start(bf16[128,1024]{1,0:T(8,128)(2,1)S(1)} %get-tuple-element.54.s0), channel_id=1, source_target_pairs={{0,16},{8,24},{16,0},{24,8},{1,17},{9,25},{17,1},{25,9},{2,18},{10... | collective-permute-start | bytes 786440 | tf_op jit(solution)/shard_map/ppermute | solution.py:68
  48.2 16.1 %collective-permute-start.11 = (bf16[128,1024]{1,0:T(8,128)(2,1)S(1)}, bf16[128,1024]{1,0:T(8,128)(2,1)S(1)}, u32[]{:S(2)}, u32[]{:S(2)}) collective-permute-start(bf16[128,1024]{1,0:T(8,128)(2,1)S(1)} %get-tuple-element.54.s0), channel_id=1, source_target_pairs={{0,24},{8,16},{16,8},{24,0},{1,25},{9,17},{17,9},{25,1},{2,26},{10... | collective-permute-start | bytes 786440 | tf_op jit(solution)/shard_map/ppermute | solution.py:68
  49.5 14.9 %collective-permute-start.9 = (bf16[128,1024]{1,0:T(8,128)(2,1)S(1)}, bf16[128,1024]{1,0:T(8,128)(2,1)S(1)}, u32[]{:S(2)}, u32[]{:S(2)}) collective-permute-start(bf16[128,1024]{1,0:T(8,128)(2,1)S(1)} %get-tuple-element.54.s0), channel_id=1, source_target_pairs={{0,8},{8,0},{16,24},{24,16},{1,9},{9,1},{17,25},{25,17},{2,10},{10... | collective-permute-start | bytes 786440 | tf_op jit(solution)/shard_map/ppermute | solution.py:68
  67.3 13.4 %all-to-all-start.2 = ((bf16[8,48,512]{2,1,0:T(8,128)(2,1)}), bf16[8,48,512]{2,1,0:T(8,128)(2,1)S(1)}, u32[]{:S(2)}, u32[]{:S(2)}) async-start(bf16[8,48,512]{2,1,0:T(8,128)(2,1)} %get-tuple-element.61), calls=%async_computation.2 | async-start | bytes 786432 | tf_op jit(solution)/shard_map/all_to_all | solution.py:398
  80.7 26.7 %all-to-all-start.1 = ((bf16[8,128,512]{2,1,0:T(8,128)(2,1)}), bf16[8,128,512]{2,1,0:T(8,128)(2,1)S(1)}, u32[]{:S(2)}, u32[]{:S(2)}) async-start(bf16[8,128,512]{2,1,0:T(8,128)(2,1)} %grads.1), calls=%async_computation.1 | async-start | bytes 2097152 | tf_op jit(solution)/shard_map/all_to_all | solution.py:403
  85.6 1.5 %collective-permute-start.12 = (f32[392,128]{1,0:T(8,128)S(1)}, f32[392,128]{1,0:T(8,128)S(1)}, u32[]{:S(2)}, u32[]{:S(2)}) collective-permute-start(f32[392,128]{1,0:T(8,128)S(1)} %get-tuple-element.65), channel_id=1, source_target_pairs={{0,32},{32,0},{64,96},{96,64},{1,33},{33,1},{65,97},{97,65},{2,34}... | collective-permute-start | bytes 602120 | tf_op jit(solution)/shard_map/ppermute | solution.py:68
  87.1 15.5 %collective-permute-start.13 = (f32[256,128]{1,0:T(8,128)S(1)}, f32[256,128]{1,0:T(8,128)S(1)}, u32[]{:S(2)}, u32[]{:S(2)}) collective-permute-start(f32[256,128]{1,0:T(8,128)S(1)} %get-tuple-element.66.high), channel_id=1, source_target_pairs={{0,64},{32,96},{64,0},{96,32},{1,65},{33,97},{65,1},{97,33},{2,66}... | collective-permute-start | bytes 393224 | tf_op jit(solution)/shard_map/ppermute | solution.py:68
  89.9 12.7 %collective-permute-start.14 = (f32[128,128]{1,0:T(8,128)S(1)}, f32[128,128]{1,0:T(8,128)S(1)}, u32[]{:S(2)}, u32[]{:S(2)}) collective-permute-start(f32[128,128]{1,0:T(8,128)S(1)} %get-tuple-element.67.low), channel_id=1, source_target_pairs={{0,4},{1,5},{2,6},{3,7},{4,0},{5,1},{6,2},{7,3},{8,12},{9,13},{10,... | collective-permute-start | bytes 196616 | tf_op jit(solution)/shard_map/ppermute | solution.py:68
  91.2 11.3 %collective-permute-start.15 = (f32[128,128]{1,0:T(8,128)S(1)}, f32[128,128]{1,0:T(8,128)S(1)}, u32[]{:S(2)}, u32[]{:S(2)}) collective-permute-start(f32[128,128]{1,0:T(8,128)S(1)} %get-tuple-element.67.low), channel_id=1, source_target_pairs={{0,68},{1,69},{2,70},{3,71},{4,64},{5,65},{6,66},{7,67},{32,100},{... | collective-permute-start | bytes 196616 | tf_op jit(solution)/shard_map/ppermute | solution.py:415
  102.6 14.7 %collective-permute-start.19 = (f32[136,128]{1,0:T(8,128)S(1)}, f32[136,128]{1,0:T(8,128)S(1)}, u32[]{:S(2)}, u32[]{:S(2)}) collective-permute-start(f32[136,128]{1,0:T(8,128)S(1)} %get-tuple-element.72), channel_id=1, source_target_pairs={{0,8},{8,0},{16,24},{24,16},{1,9},{9,1},{17,25},{25,17},{2,10},{10... | collective-permute-start | bytes 208904 | tf_op jit(solution)/shard_map/ppermute | solution.py:68
  103.1 14.3 %collective-permute-start.20 = (f32[136,128]{1,0:T(8,128)S(1)}, f32[136,128]{1,0:T(8,128)S(1)}, u32[]{:S(2)}, u32[]{:S(2)}) collective-permute-start(f32[136,128]{1,0:T(8,128)S(1)} %get-tuple-element.72), channel_id=1, source_target_pairs={{0,16},{8,24},{16,0},{24,8},{1,17},{9,25},{17,1},{25,9},{2,18},{10... | collective-permute-start | bytes 208904 | tf_op jit(solution)/shard_map/ppermute | solution.py:68
  105.3 12.0 %collective-permute-start.21 = (f32[136,128]{1,0:T(8,128)S(1)}, f32[136,128]{1,0:T(8,128)S(1)}, u32[]{:S(2)}, u32[]{:S(2)}) collective-permute-start(f32[136,128]{1,0:T(8,128)S(1)} %get-tuple-element.72), channel_id=1, source_target_pairs={{0,24},{8,16},{16,8},{24,0},{1,25},{9,17},{17,9},{25,1},{2,26},{10... | collective-permute-start | bytes 208904 | tf_op jit(solution)/shard_map/ppermute | solution.py:68
  107.4 5.1 %copy-start.4 = (s32[128]{0:T(128)S(1)}, s32[128]{0:T(128)}, u32[]{:S(2)}) copy-start(s32[128]{0:T(128)} %param.21) | copy-start | bytes 1540
  108.5 21.2 %all-to-all-start.3 = ((bf16[8,128,512]{2,1,0:T(8,128)(2,1)}), bf16[8,128,512]{2,1,0:T(8,128)(2,1)S(1)}, u32[]{:S(2)}, u32[]{:S(2)}) async-start(bf16[8,128,512]{2,1,0:T(8,128)(2,1)} %total.1), calls=%async_computation.3 | async-start | bytes 2097152 | tf_op jit(solution)/shard_map/all_to_all | solution.py:421
  112.5 15.0 %collective-permute-start.16 = (bf16[2,32,512]{2,1,0:T(8,128)(2,1)S(1)}, bf16[2,32,512]{2,1,0:T(8,128)(2,1)S(1)}, u32[]{:S(2)}, u32[]{:S(2)}) collective-permute-start(bf16[2,32,512]{2,1,0:T(8,128)(2,1)S(1)} %get-tuple-element.69.pair.g0), channel_id=1, source_target_pairs={{0,1},{1,0},{2,3},{3,2},{4,5},{5,4},{6,7},{7,6},{8,9},{9,8},{10,11... | collective-permute-start | bytes 196616 | tf_op jit(solution)/shard_map/ppermute | solution.py:68
  114.6 15.1 %collective-permute-start.17 = (bf16[2,32,512]{2,1,0:T(8,128)(2,1)S(1)}, bf16[2,32,512]{2,1,0:T(8,128)(2,1)S(1)}, u32[]{:S(2)}, u32[]{:S(2)}) collective-permute-start(bf16[2,32,512]{2,1,0:T(8,128)(2,1)S(1)} %get-tuple-element.69.pair.g0), channel_id=1, source_target_pairs={{0,2},{1,3},{2,0},{3,1},{4,6},{5,7},{6,4},{7,5},{8,10},{9,11},{10,... | collective-permute-start | bytes 196616 | tf_op jit(solution)/shard_map/ppermute | solution.py:68
  117.3 12.4 %collective-permute-start.18 = (bf16[2,32,512]{2,1,0:T(8,128)(2,1)S(1)}, bf16[2,32,512]{2,1,0:T(8,128)(2,1)S(1)}, u32[]{:S(2)}, u32[]{:S(2)}) collective-permute-start(bf16[2,32,512]{2,1,0:T(8,128)(2,1)S(1)} %get-tuple-element.69.pair.g0), channel_id=1, source_target_pairs={{0,3},{1,2},{2,1},{3,0},{4,7},{5,6},{6,5},{7,4},{8,11},{9,10},{10,... | collective-permute-start | bytes 196616 | tf_op jit(solution)/shard_map/ppermute | solution.py:68
